TPU v7x, 32 devices: a whole 2x2x4 slice. The times are simulated.
32 devices in a mesh: fsdp: 16 (over z, x, core), tp: 2 (over y).
Axes of the slice: x: 2, y: 2, z: 4, core: 2. Of those that a mesh axis runs over, the one named last changes fastest.
Arguments:
- clean_patches: float32 [256, 256, 16], P(('fsdp', 'tp')), may hold values from -6 to 6
- noise_patches: float32 [256, 256, 16], P(('fsdp', 'tp'))
- timesteps: int32 [256], P('fsdp'), may hold values from 0 to 999
- labels: int32 [256], P('fsdp'), may hold values from 0 to 31
- qkv_weight: float32 [2, 1024, 3072], P(None, 'fsdp', 'tp'), may hold values from -0.125 to 0.125
- out_weight: float32 [2, 1024, 1024], P(None, 'tp', 'fsdp')
- expand_weight: float32 [2, 1024, 4096], P(None, 'fsdp', 'tp'), may hold values from -0.1875 to 0.1875
- reduce_weight: float32 [2, 4096, 1024], P(None, 'tp', 'fsdp')
- modulate_weight: float32 [1024, 14336], P('fsdp', 'tp'), may hold values from -0.09375 to 0.09375
- embed_weight: float32 [1344, 1024], P(None, ('fsdp', 'tp'))
- bias_vector: float32 [29696], P(('fsdp', 'tp'))
- qkv_first: float32 [2, 1024, 3072], P(None, 'fsdp', 'tp'), may hold values from -9.536743e-06 to 9.536743e-06
- out_first: float32 [2, 1024, 1024], P(None, 'tp', 'fsdp'), may hold values from -9.536743e-06 to 9.536743e-06
- expand_first: float32 [2, 1024, 4096], P(None, 'fsdp', 'tp'), may hold values from -9.536743e-06 to 9.536743e-06
- reduce_first: float32 [2, 4096, 1024], P(None, 'tp', 'fsdp'), may hold values from -9.536743e-06 to 9.536743e-06
- modulate_first: float32 [1024, 14336], P('fsdp', 'tp'), may hold values from -9.536743e-06 to 9.536743e-06
- embed_first: float32 [1344, 1024], P(None, ('fsdp', 'tp')), may hold values from -9.536743e-06 to 9.536743e-06
- bias_first: float32 [29696], P(('fsdp', 'tp')), may hold values from -3.8146973e-05 to 3.8146973e-05
- qkv_second: float32 [2, 1024, 3072], P(None, 'fsdp', 'tp'), may hold values from 2.4241342e-12 to 9.696537e-12
- out_second: float32 [2, 1024, 1024], P(None, 'tp', 'fsdp'), may hold values from 2.4241342e-12 to 9.696537e-12
- expand_second: float32 [2, 1024, 4096], P(None, 'fsdp', 'tp'), may hold values from 2.4241342e-12 to 9.696537e-12
- reduce_second: float32 [2, 4096, 1024], P(None, 'tp', 'fsdp'), may hold values from 2.4241342e-12 to 9.696537e-12
- modulate_second: float32 [1024, 14336], P('fsdp', 'tp'), may hold values from 2.4241342e-12 to 9.696537e-12
- embed_second: float32 [1344, 1024], P(None, ('fsdp', 'tp')), may hold values from 2.4241342e-12 to 9.696537e-12
- bias_second: float32 [29696], P(('fsdp', 'tp')), may hold values from 3.8786148e-11 to 1.5514459e-10
Outputs:
- loss_total: float32 [], replicated
- grad_norm: float32 [], replicated
- qkv_moment: float32 [2, 1024, 3072], P(None, 'fsdp', 'tp')
- qkv_square: float32 [2, 1024, 3072], P(None, 'fsdp', 'tp')
- qkv_master: float32 [2, 1024, 3072], P(None, 'fsdp', 'tp')
- out_moment: float32 [2, 1024, 1024], P(None, 'tp', 'fsdp')
- out_square: float32 [2, 1024, 1024], P(None, 'tp', 'fsdp')
- out_master: float32 [2, 1024, 1024], P(None, 'tp', 'fsdp')
- expand_moment: float32 [2, 1024, 4096], P(None, 'fsdp', 'tp')
- expand_square: float32 [2, 1024, 4096], P(None, 'fsdp', 'tp')
- expand_master: float32 [2, 1024, 4096], P(None, 'fsdp', 'tp')
- reduce_moment: float32 [2, 4096, 1024], P(None, 'tp', 'fsdp')
- reduce_square: float32 [2, 4096, 1024], P(None, 'tp', 'fsdp')
- reduce_master: float32 [2, 4096, 1024], P(None, 'tp', 'fsdp')
- modulate_moment: float32 [1024, 14336], P('fsdp', 'tp')
- modulate_square: float32 [1024, 14336], P('fsdp', 'tp')
- modulate_master: float32 [1024, 14336], P('fsdp', 'tp')
- embed_moment: float32 [1344, 1024], P(None, ('fsdp', 'tp'))
- embed_square: float32 [1344, 1024], P(None, ('fsdp', 'tp'))
- embed_master: float32 [1344, 1024], P(None, ('fsdp', 'tp'))
- bias_moment: float32 [29696], P(('fsdp', 'tp'))
- bias_square: float32 [29696], P(('fsdp', 'tp'))
- bias_master: float32 [29696], P(('fsdp', 'tp'))
- qkv_copy: bfloat16 [2, 1024, 3072], P(None, 'fsdp', 'tp')
- out_copy: bfloat16 [2, 1024, 1024], P(None, 'tp', 'fsdp')
- expand_copy: bfloat16 [2, 1024, 4096], P(None, 'fsdp', 'tp')
- reduce_copy: bfloat16 [2, 4096, 1024], P(None, 'tp', 'fsdp')
- modulate_copy: bfloat16 [1024, 14336], P('fsdp', 'tp')
- embed_copy: bfloat16 [1344, 1024], P(None, ('fsdp', 'tp'))
All inputs are finite; a program needn't handle non-finite values.
Results may differ from a plain program's by a relative error of at most 0.0079.
The roundings to bfloat16 on the way count: a program that leaves them out, or rounds other values in their place, can miss the bound.
Values may be sent and summed in bfloat16 or wider, within the bound.
A program may use at most 640 MiB of HBM per device.

v0:
```python
import math

import jax
import jax.numpy as jnp
from jax import lax
from jax.sharding import PartitionSpec as P

D = 1024
HEAD = 64
FF = 4096
CH = 16
FREQ = 256
CLASSES = 32
SIDE = 16
LAYERS = 2
MB = 2
STEP = 10
TOK_LAT = 256
MODS = 14336


CLIP_AT = 0.01
RATE = 0.05
BETA_ONE = 0.5
BETA_TWO = 0.5
DECAY = 0.01
ADAM_EPS = 1e-08
NORM_EPS = 1e-06
EXACT = lax.Precision.HIGHEST


def contract(left, right, form):
    return jnp.einsum(form, left, right, preferred_element_type=jnp.float32)


def exact_dot(left, right):
    return jnp.dot(left, right, precision=EXACT)


def layer_norm(value):
    center = value - jnp.mean(value, -1, keepdims=True)
    return center * lax.rsqrt(jnp.mean(center * center, -1, keepdims=True) + NORM_EPS)


def gelu_tanh(value):
    return jax.nn.gelu(value, approximate=True)


def local_back(func, value, grad):
    _, pullback = jax.vjp(func, value)
    return pullback(grad)[0]


def accumulate(old, new):
    return new if old is None else jax.tree.map(jnp.add, old, new)


def noise_levels(steps):
    angle = (steps.astype(jnp.float32) / 1000.0 + 0.008) / 1.008 * (math.pi / 2)
    return (jnp.cos(angle), jnp.sin(angle))


def step_features(steps):
    half = FREQ // 2
    rates = jnp.exp(-math.log(10000.0) * jnp.arange(half, dtype=jnp.float32) / half)
    phase = steps.astype(jnp.float32)[:, None] * rates[None, :]
    return jnp.concatenate([jnp.cos(phase), jnp.sin(phase)], axis=1)


def place_table():
    quarter = D // 4
    rates = 1.0 / 10000.0 ** (jnp.arange(quarter, dtype=jnp.float32) / quarter)
    index = jnp.arange(TOK_LAT, dtype=jnp.int32)
    rows = (index // SIDE).astype(jnp.float32)[:, None] * rates[None, :]
    columns = (index % SIDE).astype(jnp.float32)[:, None] * rates[None, :]
    return jnp.concatenate(
        [jnp.sin(rows), jnp.cos(rows), jnp.sin(columns), jnp.cos(columns)], axis=1
    )


def split_embed(embed):
    start = FREQ + D
    return (
        embed[:FREQ],
        embed[FREQ:start],
        embed[start : start + CH],
        embed[start + CH : start + CH + CLASSES],
        embed[start + CH + CLASSES :],
    )


def split_bias(bias):
    layers = []
    for layer in range(LAYERS):
        base = MODS + layer * (2 * D + FF)
        layers.append(
            (
                bias[base : base + D],
                bias[base + D : base + D + FF],
                bias[base + D + FF : base + 2 * D + FF],
            )
        )
    tail = MODS + LAYERS * (2 * D + FF)
    return (
        bias[:MODS],
        layers,
        bias[tail : tail + D],
        bias[tail + D : tail + 2 * D],
        bias[tail + 2 * D : tail + 3 * D],
    )


def spread(value):
    return lax.all_gather(value.astype(jnp.bfloat16), "tp", axis=0, tiled=True)


def collect(partial_sum):
    return lax.psum_scatter(partial_sum, "tp", scatter_dimension=0, tiled=True)


def spread_grad(value):
    return lax.all_gather(value.astype(jnp.bfloat16), "tp", axis=0, tiled=True)


def collect_grad(partial_sum):
    return lax.psum_scatter(partial_sum, "tp", scatter_dimension=0, tiled=True)


def layer_forward(stream, modulation, weights, biases):
    w_qkv, w_out, w_expand, w_reduce = weights
    out_bias, expand_bias, reduce_bias = biases
    shift_a, scale_a, gate_a, shift_m, scale_m, gate_m = [
        modulation[:, i, None, :] for i in range(6)
    ]
    normed_a = layer_norm(stream)
    seq_a = spread(normed_a * (1.0 + scale_a) + shift_a)
    qkv = contract(seq_a, w_qkv, "gtd,de->gte").astype(jnp.bfloat16)
    count, length = (qkv.shape[0], qkv.shape[1])
    split = qkv.reshape(count, length, -1, 3, HEAD)
    query, key, value = (split[:, :, :, 0], split[:, :, :, 1], split[:, :, :, 2])
    scores = contract(query, key, "gqhe,gkhe->ghqk") / math.sqrt(HEAD)
    log_total = jax.nn.logsumexp(scores, axis=-1, keepdims=True)
    probs = jnp.exp(scores - log_total).astype(jnp.bfloat16)
    att = contract(probs, value, "ghqk,gkhe->gqhe").astype(jnp.bfloat16).reshape(count, length, -1)
    branch_a = collect(contract(att, w_out, "gtc,cd->gtd"))
    mid = stream + gate_a * (branch_a + out_bias)
    normed_m = layer_norm(mid)
    seq_m = spread(normed_m * (1.0 + scale_m) + shift_m)
    pre = contract(seq_m, w_expand, "gtd,df->gtf") + expand_bias
    acted = gelu_tanh(pre).astype(jnp.bfloat16)
    branch_m = collect(contract(acted, w_reduce, "gtf,fd->gtd"))
    result = mid + gate_m * (branch_m + reduce_bias)
    kept = (
        stream,
        normed_a,
        seq_a,
        query,
        key,
        value,
        log_total,
        att,
        branch_a,
        mid,
        normed_m,
        seq_m,
        pre,
        acted,
        branch_m,
    )
    return (result, kept)


def layer_backward(grad_out, modulation, weights, biases, kept):
    w_qkv, w_out, w_expand, w_reduce = weights
    out_bias, expand_bias, reduce_bias = biases
    (
        stream,
        normed_a,
        seq_a,
        query,
        key,
        value,
        log_total,
        att,
        branch_a,
        mid,
        normed_m,
        seq_m,
        pre,
        acted,
        branch_m,
    ) = kept
    shift_a, scale_a, gate_a, shift_m, scale_m, gate_m = [
        modulation[:, i, None, :] for i in range(6)
    ]
    grad_gate_m = jnp.sum(grad_out * (branch_m + reduce_bias), axis=1)
    carried_m = gate_m * grad_out
    grad_reduce_bias = jnp.sum(carried_m, axis=(0, 1))
    seq_grad_m = spread_grad(carried_m)
    grad_reduce = contract(acted, seq_grad_m, "gtf,gtd->fd")
    grad_acted = contract(seq_grad_m, w_reduce, "gtd,fd->gtf")
    grad_pre = local_back(gelu_tanh, pre, grad_acted).astype(jnp.bfloat16)
    grad_expand_bias = jnp.sum(grad_pre.astype(jnp.float32), axis=(0, 1))
    grad_expand = contract(seq_m, grad_pre, "gtd,gtf->df")
    grad_seq_m = collect_grad(contract(grad_pre, w_expand, "gtf,df->gtd"))
    grad_shift_m = jnp.sum(grad_seq_m, axis=1)
    grad_scale_m = jnp.sum(grad_seq_m * normed_m, axis=1)
    grad_mid = grad_out + local_back(layer_norm, mid, grad_seq_m * (1.0 + scale_m))
    grad_gate_a = jnp.sum(grad_mid * (branch_a + out_bias), axis=1)
    carried_a = gate_a * grad_mid
    grad_out_bias = jnp.sum(carried_a, axis=(0, 1))
    seq_grad_a = spread_grad(carried_a)
    grad_w_out = contract(att, seq_grad_a, "gtc,gtd->cd")
    grad_att = contract(seq_grad_a, w_out, "gtd,cd->gtc").astype(jnp.bfloat16).reshape(query.shape)
    scores = contract(query, key, "gqhe,gkhe->ghqk") / math.sqrt(HEAD)
    probs = jnp.exp(scores - log_total)
    grad_value = contract(probs.astype(jnp.bfloat16), grad_att, "ghqk,gqhe->gkhe")
    grad_probs = contract(grad_att, value, "gqhe,gkhe->ghqk")
    grad_scores = probs * (grad_probs - jnp.sum(grad_probs * probs, axis=-1, keepdims=True))
    grad_scores = grad_scores.astype(jnp.bfloat16)
    grad_query = contract(grad_scores, key, "ghqk,gkhe->gqhe") / math.sqrt(HEAD)
    grad_key = contract(grad_scores, query, "ghqk,gqhe->gkhe") / math.sqrt(HEAD)
    grad_qkv = jnp.stack([grad_query, grad_key, grad_value], axis=3).astype(jnp.bfloat16)
    grad_qkv = grad_qkv.reshape(seq_a.shape[0], seq_a.shape[1], -1)
    grad_w_qkv = contract(seq_a, grad_qkv, "gtd,gte->de")
    grad_seq_a = collect_grad(contract(grad_qkv, w_qkv, "gte,de->gtd"))
    grad_shift_a = jnp.sum(grad_seq_a, axis=1)
    grad_scale_a = jnp.sum(grad_seq_a * normed_a, axis=1)
    grad_in = grad_mid + local_back(layer_norm, stream, grad_seq_a * (1.0 + scale_a))
    grad_mod = jnp.stack(
        [grad_shift_a, grad_scale_a, grad_gate_a, grad_shift_m, grad_scale_m, grad_gate_m], axis=1
    )
    return (
        grad_in,
        grad_mod,
        (grad_w_qkv, grad_w_out, grad_expand, grad_reduce),
        (grad_out_bias, grad_expand_bias, grad_reduce_bias),
    )


def adam(weight, first, second, grad, factor):
    grad = grad * factor
    new_first = BETA_ONE * first + (1.0 - BETA_ONE) * grad
    new_second = BETA_TWO * second + (1.0 - BETA_TWO) * grad * grad
    first_hat = new_first / (1.0 - BETA_ONE**STEP)
    second_hat = new_second / (1.0 - BETA_TWO**STEP)
    new_weight = weight - RATE * (first_hat / (jnp.sqrt(second_hat) + ADAM_EPS) + DECAY * weight)
    return (new_first, new_second, new_weight)


def per_device(
    clean_patches,
    noise_patches,
    timesteps,
    labels,
    qkv_weight,
    out_weight,
    expand_weight,
    reduce_weight,
    modulate_weight,
    embed_weight,
    bias_vector,
    qkv_first,
    out_first,
    expand_first,
    reduce_first,
    modulate_first,
    embed_first,
    bias_first,
    qkv_second,
    out_second,
    expand_second,
    reduce_second,
    modulate_second,
    embed_second,
    bias_second,
):
    tp_count = lax.axis_size("tp")
    tp_rank = lax.axis_index("tp")
    embed, bias = (
        lax.all_gather(embed_weight, ("fsdp", "tp"), axis=1, tiled=True),
        lax.all_gather(bias_vector, ("fsdp", "tp"), axis=0, tiled=True),
    )
    step_in, step_out, patch_in, table, patch_out = split_embed(embed)
    step_in_low = step_in.astype(jnp.bfloat16)
    step_out_low = step_out.astype(jnp.bfloat16)
    patch_in_low = patch_in.astype(jnp.bfloat16)
    table_low = table.astype(jnp.bfloat16)
    patch_out_low = patch_out.astype(jnp.bfloat16)
    ada_bias, layer_bias_all, step_in_bias, step_out_bias, patch_bias = split_bias(bias)
    columns = modulate_weight.shape[1]
    hidden_cols = expand_weight.shape[2]
    ada_weight = lax.all_gather(modulate_weight.astype(jnp.bfloat16), "fsdp", axis=0, tiled=True)
    ada_bias_own = lax.dynamic_slice_in_dim(ada_bias, tp_rank * columns, columns)
    layer_bias = [
        (out_b, lax.dynamic_slice_in_dim(expand_b, tp_rank * hidden_cols, hidden_cols), reduce_b)
        for out_b, expand_b, reduce_b in layer_bias_all
    ]
    low_qkv = qkv_weight.astype(jnp.bfloat16)
    low_out = out_weight.astype(jnp.bfloat16)
    low_expand = expand_weight.astype(jnp.bfloat16)
    low_reduce = reduce_weight.astype(jnp.bfloat16)

    def fetch(layer):
        return (
            lax.all_gather(low_qkv[layer], "fsdp", axis=0, tiled=True),
            lax.all_gather(low_out[layer], "fsdp", axis=1, tiled=True),
            lax.all_gather(low_expand[layer], "fsdp", axis=0, tiled=True),
            lax.all_gather(low_reduce[layer], "fsdp", axis=1, tiled=True),
        )

    own = clean_patches.shape[0] // MB
    step_grid = timesteps.reshape(tp_count, MB, own)
    label_grid = labels.reshape(tp_count, MB, own)
    places = place_table()
    total = float(
        clean_patches.shape[0]
        * clean_patches.shape[1]
        * clean_patches.shape[2]
        * lax.axis_size("fsdp")
        * tp_count
    )
    loss_local = jnp.zeros((), jnp.float32)
    layer_grads = [None] * LAYERS
    layer_bias_grads = [None] * LAYERS
    small = None
    for batch_index in range(MB):
        steps_all = step_grid[:, batch_index].reshape(-1)
        labels_all = label_grid[:, batch_index].reshape(-1)
        steps_own = lax.dynamic_index_in_dim(step_grid[:, batch_index], tp_rank, 0, keepdims=False)
        clean = clean_patches[batch_index * own : (batch_index + 1) * own]
        noise = noise_patches[batch_index * own : (batch_index + 1) * own]
        signal, spread_level = noise_levels(steps_own)
        noisy = (signal[:, None, None] * clean + spread_level[:, None, None] * noise).astype(
            jnp.bfloat16
        )
        features = step_features(steps_all).astype(jnp.bfloat16)
        step_pre = contract(features, step_in_low, "gf,fd->gd") + step_in_bias
        step_hidden = jax.nn.silu(step_pre).astype(jnp.bfloat16)
        onehot = (labels_all[:, None] == jnp.arange(CLASSES, dtype=jnp.int32)[None, :]).astype(
            jnp.float32
        )
        cond = (
            contract(step_hidden, step_out_low, "gd,de->ge")
            + step_out_bias
            + contract(onehot.astype(jnp.bfloat16), table_low, "gc,cd->gd")
        )
        cond_act = jax.nn.silu(cond).astype(jnp.bfloat16)
        mod_part = contract(cond_act, ada_weight, "gd,de->ge") + ada_bias_own
        mods = lax.all_to_all(mod_part, "tp", split_axis=0, concat_axis=1, tiled=True).reshape(
            own, 6 * LAYERS + 2, -1
        )
        stream = contract(noisy, patch_in_low, "gtc,cd->gtd") + patch_bias + places[None]
        kept_all = []
        for layer in range(LAYERS):
            stream, kept = layer_forward(
                stream, mods[:, 6 * layer : 6 * layer + 6], fetch(layer), layer_bias[layer]
            )
            kept_all.append(kept)
        shift_f = mods[:, 6 * LAYERS, None, :]
        scale_f = mods[:, 6 * LAYERS + 1, None, :]
        normed_f = layer_norm(stream)
        final = (normed_f * (1.0 + scale_f) + shift_f).astype(jnp.bfloat16)
        pred = contract(final, patch_out_low, "gtd,cd->gtc")
        error = pred - noise
        loss_local = loss_local + jnp.sum(error * error)
        grad_pred = (error * (2.0 / total)).astype(jnp.bfloat16)
        grad_patch_out = contract(grad_pred, final, "gtc,gtd->cd")
        grad_final = contract(grad_pred, patch_out_low, "gtc,cd->gtd")
        grad_final_mod = jnp.stack(
            [jnp.sum(grad_final, axis=1), jnp.sum(grad_final * normed_f, axis=1)], axis=1
        )
        grad_stream = local_back(layer_norm, stream, grad_final * (1.0 + scale_f))
        mod_grads = [None] * LAYERS
        for layer in reversed(range(LAYERS)):
            grad_stream, mod_grads[layer], weight_grads, bias_grads = layer_backward(
                grad_stream,
                mods[:, 6 * layer : 6 * layer + 6],
                fetch(layer),
                layer_bias[layer],
                kept_all[layer],
            )
            layer_grads[layer] = accumulate(layer_grads[layer], weight_grads)
            layer_bias_grads[layer] = accumulate(layer_bias_grads[layer], bias_grads)
        grad_embedded = grad_stream.astype(jnp.bfloat16)
        grad_patch_in = contract(noisy, grad_embedded, "gtc,gtd->cd")
        grad_patch_bias = jnp.sum(grad_embedded.astype(jnp.float32), axis=(0, 1))
        grad_mods = (
            jnp.concatenate(mod_grads + [grad_final_mod], axis=1)
            .reshape(own, -1)
            .astype(jnp.bfloat16)
        )
        grad_columns = lax.all_to_all(grad_mods, "tp", split_axis=1, concat_axis=0, tiled=True)
        grad_ada_bias = jnp.sum(grad_columns.astype(jnp.float32), axis=0)
        grad_ada = contract(cond_act, grad_columns, "gd,ge->de")
        grad_cond_act = contract(grad_columns, ada_weight, "ge,de->gd")
        grad_cond = local_back(jax.nn.silu, cond, grad_cond_act)
        grad_table = exact_dot(onehot.T, grad_cond)
        grad_step_out = exact_dot(step_hidden.astype(jnp.float32).T, grad_cond)
        grad_step_out_bias = jnp.sum(grad_cond, axis=0)
        grad_hidden = exact_dot(grad_cond, step_out_low.astype(jnp.float32).T)
        grad_step_pre = local_back(jax.nn.silu, step_pre, grad_hidden)
        grad_step_in = exact_dot(features.astype(jnp.float32).T, grad_step_pre)
        grad_step_in_bias = jnp.sum(grad_step_pre, axis=0)
        small = accumulate(
            small,
            (
                grad_step_in,
                grad_step_out,
                grad_patch_in,
                grad_table,
                grad_patch_out,
                grad_step_in_bias,
                grad_step_out_bias,
                grad_patch_bias,
                grad_ada_bias,
                grad_ada,
            ),
        )
    (
        grad_step_in,
        grad_step_out,
        grad_patch_in,
        grad_table,
        grad_patch_out,
        grad_step_in_bias,
        grad_step_out_bias,
        grad_patch_bias,
        grad_ada_bias,
        grad_ada,
    ) = small
    stack_qkv = jnp.stack([layer_grads[layer][0] for layer in range(LAYERS)])
    stack_out = jnp.stack([layer_grads[layer][1] for layer in range(LAYERS)])
    stack_expand = jnp.stack([layer_grads[layer][2] for layer in range(LAYERS)])
    stack_reduce = jnp.stack([layer_grads[layer][3] for layer in range(LAYERS)])
    reduced = (
        lax.psum_scatter(stack_qkv, "fsdp", scatter_dimension=1, tiled=True),
        lax.psum_scatter(stack_out, "fsdp", scatter_dimension=2, tiled=True),
        lax.psum_scatter(stack_expand, "fsdp", scatter_dimension=1, tiled=True),
        lax.psum_scatter(stack_reduce, "fsdp", scatter_dimension=2, tiled=True),
        lax.psum_scatter(grad_ada, "fsdp", scatter_dimension=0, tiled=True),
    )
    pieces = [
        lax.dynamic_update_slice_in_dim(
            jnp.zeros((ada_bias.shape[0],), jnp.float32), grad_ada_bias, tp_rank * columns, 0
        )
    ]
    for layer in range(LAYERS):
        grad_out_b, grad_expand_b, grad_reduce_b = layer_bias_grads[layer]
        pieces += [
            grad_out_b,
            lax.dynamic_update_slice_in_dim(
                jnp.zeros((FF,), jnp.float32), grad_expand_b, tp_rank * hidden_cols, 0
            ),
            grad_reduce_b,
        ]
    pieces += [grad_step_in_bias, grad_step_out_bias, grad_patch_bias]
    embed_full = jnp.concatenate(
        [grad_step_in, grad_step_out, grad_patch_in, grad_table, grad_patch_out], axis=0
    )
    bias_full = jnp.concatenate(pieces)
    embed_grad, bias_grad = (
        lax.psum_scatter(embed_full, ("fsdp", "tp"), scatter_dimension=1, tiled=True),
        lax.psum_scatter(bias_full, ("fsdp", "tp"), scatter_dimension=0, tiled=True),
    )
    grads = tuple(reduced) + (embed_grad, bias_grad)
    square = jnp.zeros((), jnp.float32)
    for grad in grads:
        square = square + jnp.sum(grad * grad)
    square, loss_total = lax.psum((square, loss_local), ("fsdp", "tp"))
    grad_norm = jnp.sqrt(square)
    factor = CLIP_AT / jnp.maximum(grad_norm, CLIP_AT)
    params = (
        qkv_weight,
        out_weight,
        expand_weight,
        reduce_weight,
        modulate_weight,
        embed_weight,
        bias_vector,
    )
    firsts = (
        qkv_first,
        out_first,
        expand_first,
        reduce_first,
        modulate_first,
        embed_first,
        bias_first,
    )
    seconds = (
        qkv_second,
        out_second,
        expand_second,
        reduce_second,
        modulate_second,
        embed_second,
        bias_second,
    )
    news = [adam(w, f, s, g, factor) for w, f, s, g in zip(params, firsts, seconds, grads)]
    qkv_moment, qkv_square, qkv_master = news[0]
    out_moment, out_square, out_master = news[1]
    expand_moment, expand_square, expand_master = news[2]
    reduce_moment, reduce_square, reduce_master = news[3]
    modulate_moment, modulate_square, modulate_master = news[4]
    embed_moment, embed_square, embed_master = news[5]
    bias_moment, bias_square, bias_master = news[6]
    return (
        loss_total,
        grad_norm,
        qkv_moment,
        qkv_square,
        qkv_master,
        out_moment,
        out_square,
        out_master,
        expand_moment,
        expand_square,
        expand_master,
        reduce_moment,
        reduce_square,
        reduce_master,
        modulate_moment,
        modulate_square,
        modulate_master,
        embed_moment,
        embed_square,
        embed_master,
        bias_moment,
        bias_square,
        bias_master,
        qkv_master.astype(jnp.bfloat16),
        out_master.astype(jnp.bfloat16),
        expand_master.astype(jnp.bfloat16),
        reduce_master.astype(jnp.bfloat16),
        modulate_master.astype(jnp.bfloat16),
        embed_master.astype(jnp.bfloat16),
    )


def solution(mesh):
    return jax.shard_map(
        per_device,
        mesh=mesh,
        in_specs=(
            P(("fsdp", "tp"), None, None),
            P(("fsdp", "tp"), None, None),
            P("fsdp"),
            P("fsdp"),
            P(None, "fsdp", "tp"),
            P(None, "tp", "fsdp"),
            P(None, "fsdp", "tp"),
            P(None, "tp", "fsdp"),
            P("fsdp", "tp"),
            P(None, ("fsdp", "tp")),
            P(("fsdp", "tp")),
            P(None, "fsdp", "tp"),
            P(None, "tp", "fsdp"),
            P(None, "fsdp", "tp"),
            P(None, "tp", "fsdp"),
            P("fsdp", "tp"),
            P(None, ("fsdp", "tp")),
            P(("fsdp", "tp")),
            P(None, "fsdp", "tp"),
            P(None, "tp", "fsdp"),
            P(None, "fsdp", "tp"),
            P(None, "tp", "fsdp"),
            P("fsdp", "tp"),
            P(None, ("fsdp", "tp")),
            P(("fsdp", "tp")),
        ),
        out_specs=(
            P(),
            P(),
            P(None, "fsdp", "tp"),
            P(None, "fsdp", "tp"),
            P(None, "fsdp", "tp"),
            P(None, "tp", "fsdp"),
            P(None, "tp", "fsdp"),
            P(None, "tp", "fsdp"),
            P(None, "fsdp", "tp"),
            P(None, "fsdp", "tp"),
            P(None, "fsdp", "tp"),
            P(None, "tp", "fsdp"),
            P(None, "tp", "fsdp"),
            P(None, "tp", "fsdp"),
            P("fsdp", "tp"),
            P("fsdp", "tp"),
            P("fsdp", "tp"),
            P(None, ("fsdp", "tp")),
            P(None, ("fsdp", "tp")),
            P(None, ("fsdp", "tp")),
            P(("fsdp", "tp")),
            P(("fsdp", "tp")),
            P(("fsdp", "tp")),
            P(None, "fsdp", "tp"),
            P(None, "tp", "fsdp"),
            P(None, "fsdp", "tp"),
            P(None, "tp", "fsdp"),
            P("fsdp", "tp"),
            P(None, ("fsdp", "tp")),
        ),
        check_vma=False,
    )
```

profile of v0, /device:TPU:0, one launch (start us, length us, event | category | flops | bytes accessed | tf_op | source)
XLA Modules:
  0.0 5367.4 jit_solution(48089058838735699)
XLA Ops:
  18.3 119.9 %all-reduce.10.cloned.1.call-done = f32[29696]{0:T(1024)} async-done(((f32[29696]{0:T(1024)}), f32[29696]{0:T(1024)}) %all-reduce.10.cloned.1.call-update) | async-done | bytes 118800
  140.4 60.1 %all-gather.35.cloned.1.call-done = bf16[1344,1024]{0,1:T(8,128)(2,1)} async-done(((bf16[1344,32]{0,1:T(8,128)(2,1)}), bf16[1344,1024]{0,1:T(8,128)(2,1)}) %all-gather.35.cloned.1.call-update) | async-done | bytes 2752528 | tf_op jit(solution)/shard_map/all_gather | solution.py:281
  213.0 102.9 %all-gather.37.cloned.1.call-done = bf16[1024,7168]{1,0:T(8,128)(2,1)} async-done(((bf16[64,7168]{1,0:T(8,128)(2,1)}), bf16[1024,7168]{1,0:T(8,128)(2,1)}) %all-gather.37.cloned.1.call-update) | async-done | bytes 14680080 | tf_op jit(solution)/shard_map/all_gather | solution.py:293
  362.2 57.0 %all-gather.47.cloned.1.call-done = bf16[8,256,1024]{2,1,0:T(8,128)(2,1)} async-done(((bf16[4,256,1024]{2,1,0:T(8,128)(2,1)}), bf16[8,256,1024]{2,1,0:T(8,128)(2,1)}) %all-gather.47.cloned.1.call-update) | async-done | bytes 4194320 | tf_op jit(solution)/shard_map/all_gather | solution.py:114
  479.8 96.8 %reduce-scatter.31.cloned.1.call-done = f32[4,256,1024]{2,1,0:T(8,128)} async-done(((f32[8,256,1024]{2,1,0:T(8,128)}), f32[4,256,1024]{2,1,0:T(8,128)}) %reduce-scatter.31.cloned.1.call-update) | async-done | bytes 4194320 | tf_op jit(solution)/shard_map/reduce_scatter | solution.py:118
  630.3 56.9 %all-gather.49.cloned.1.call-done = bf16[8,256,1024]{2,1,0:T(8,128)(2,1)} async-done(((bf16[4,256,1024]{2,1,0:T(8,128)(2,1)}), bf16[8,256,1024]{2,1,0:T(8,128)(2,1)}) %all-gather.49.cloned.1.call-update) | async-done | bytes 4194320 | tf_op jit(solution)/shard_map/all_gather | solution.py:114
  758.9 97.1 %reduce-scatter.33.cloned.1.call-done = f32[4,256,1024]{2,1,0:T(8,128)} async-done(((f32[8,256,1024]{2,1,0:T(8,128)}), f32[4,256,1024]{2,1,0:T(8,128)}) %reduce-scatter.33.cloned.1.call-update) | async-done | bytes 4194320 | tf_op jit(solution)/shard_map/reduce_scatter | solution.py:118
  903.9 57.1 %all-gather.51.cloned.1.call-done = bf16[8,256,1024]{2,1,0:T(8,128)(2,1)} async-done(((bf16[4,256,1024]{2,1,0:T(8,128)(2,1)}), bf16[8,256,1024]{2,1,0:T(8,128)(2,1)}) %all-gather.51.cloned.1.call-update) | async-done | bytes 4194320 | tf_op jit(solution)/shard_map/all_gather | solution.py:114
  1020.0 98.3 %reduce-scatter.35.cloned.1.call-done = f32[4,256,1024]{2,1,0:T(8,128)} async-done(((f32[8,256,1024]{2,1,0:T(8,128)}), f32[4,256,1024]{2,1,0:T(8,128)}) %reduce-scatter.35.cloned.1.call-update) | async-done | bytes 4194320 | tf_op jit(solution)/shard_map/reduce_scatter | solution.py:118
  1299.8 97.7 %reduce-scatter.37.cloned.1.call-done = f32[4,256,1024]{2,1,0:T(8,128)} async-done(((f32[8,256,1024]{2,1,0:T(8,128)}), f32[4,256,1024]{2,1,0:T(8,128)}) %reduce-scatter.37.cloned.1.call-update) | async-done | bytes 4194320 | tf_op jit(solution)/shard_map/reduce_scatter | solution.py:118
  1511.9 99.3 %reduce-scatter.45.cloned.1.call-done = f32[4,256,1024]{2,1,0:T(8,128)} async-done(((f32[8,256,1024]{2,1,0:T(8,128)}), f32[4,256,1024]{2,1,0:T(8,128)}) %reduce-scatter.45.cloned.1.call-update) | async-done | bytes 4194320 | tf_op jit(solution)/shard_map/reduce_scatter | solution.py:126
  1628.0 56.9 %all-gather.65.cloned.1.call-done = bf16[8,256,1024]{2,1,0:T(8,128)(2,1)} async-done(((bf16[4,256,1024]{2,1,0:T(8,128)(2,1)}), bf16[8,256,1024]{2,1,0:T(8,128)(2,1)}) %all-gather.65.cloned.1.call-update) | async-done | bytes 4194320 | tf_op jit(solution)/shard_map/all_gather | solution.py:122
  1749.9 99.3 %reduce-scatter.47.cloned.1.call-done = f32[4,256,1024]{2,1,0:T(8,128)} async-done(((f32[8,256,1024]{2,1,0:T(8,128)}), f32[4,256,1024]{2,1,0:T(8,128)}) %reduce-scatter.47.cloned.1.call-update) | async-done | bytes 4194320 | tf_op jit(solution)/shard_map/reduce_scatter | solution.py:126
  1865.7 56.9 %all-gather.67.cloned.1.call-done = bf16[8,256,1024]{2,1,0:T(8,128)(2,1)} async-done(((bf16[4,256,1024]{2,1,0:T(8,128)(2,1)}), bf16[8,256,1024]{2,1,0:T(8,128)(2,1)}) %all-gather.67.cloned.1.call-update) | async-done | bytes 4194320 | tf_op jit(solution)/shard_map/all_gather | solution.py:122
  1964.4 99.3 %reduce-scatter.49.cloned.1.call-done = f32[4,256,1024]{2,1,0:T(8,128)} async-done(((f32[8,256,1024]{2,1,0:T(8,128)}), f32[4,256,1024]{2,1,0:T(8,128)}) %reduce-scatter.49.cloned.1.call-update) | async-done | bytes 4194320 | tf_op jit(solution)/shard_map/reduce_scatter | solution.py:126
  2226.6 77.0 %reduce-scatter.57.cloned.1.call-done = f32[4,256,1024]{2,1,0:T(8,128)} async-done(((f32[8,256,1024]{2,1,0:T(8,128)}), f32[4,256,1024]{2,1,0:T(8,128)}) %reduce-scatter.57.cloned.1.call-update) | async-done | bytes 4194320 | tf_op jit(solution)/shard_map/reduce_scatter | solution.py:126
  2426.7 99.2 %reduce-scatter.23.cloned.1.call-done = f32[4,256,1024]{2,1,0:T(8,128)} async-done(((f32[8,256,1024]{2,1,0:T(8,128)}), f32[4,256,1024]{2,1,0:T(8,128)}) %reduce-scatter.23.cloned.1.call-update) | async-done | bytes 4194320 | tf_op jit(solution)/shard_map/reduce_scatter | solution.py:118
  2626.8 98.9 %reduce-scatter.25.cloned.1.call-done = f32[4,256,1024]{2,1,0:T(8,128)} async-done(((f32[8,256,1024]{2,1,0:T(8,128)}), f32[4,256,1024]{2,1,0:T(8,128)}) %reduce-scatter.25.cloned.1.call-update) | async-done | bytes 4194320 | tf_op jit(solution)/shard_map/reduce_scatter | solution.py:118
  2848.9 99.2 %reduce-scatter.27.cloned.1.call-done = f32[4,256,1024]{2,1,0:T(8,128)} async-done(((f32[8,256,1024]{2,1,0:T(8,128)}), f32[4,256,1024]{2,1,0:T(8,128)}) %reduce-scatter.27.cloned.1.call-update) | async-done | bytes 4194320 | tf_op jit(solution)/shard_map/reduce_scatter | solution.py:118
  2957.4 56.9 %all-gather.45.cloned.1.call-done = bf16[8,256,1024]{2,1,0:T(8,128)(2,1)} async-done(((bf16[4,256,1024]{2,1,0:T(8,128)(2,1)}), bf16[8,256,1024]{2,1,0:T(8,128)(2,1)}) %all-gather.45.cloned.1.call-update) | async-done | bytes 4194320 | tf_op jit(solution)/shard_map/all_gather | solution.py:114
  3048.7 98.9 %reduce-scatter.29.cloned.1.call-done = f32[4,256,1024]{2,1,0:T(8,128)} async-done(((f32[8,256,1024]{2,1,0:T(8,128)}), f32[4,256,1024]{2,1,0:T(8,128)}) %reduce-scatter.29.cloned.1.call-update) | async-done | bytes 4194320 | tf_op jit(solution)/shard_map/reduce_scatter | solution.py:118
  3262.0 99.3 %reduce-scatter.39.cloned.1.call-done = f32[4,256,1024]{2,1,0:T(8,128)} async-done(((f32[8,256,1024]{2,1,0:T(8,128)}), f32[4,256,1024]{2,1,0:T(8,128)}) %reduce-scatter.39.cloned.1.call-update) | async-done | bytes 4194320 | tf_op jit(solution)/shard_map/reduce_scatter | solution.py:126
  3378.0 56.9 %all-gather.57.cloned.1.call-done = bf16[8,256,1024]{2,1,0:T(8,128)(2,1)} async-done(((bf16[4,256,1024]{2,1,0:T(8,128)(2,1)}), bf16[8,256,1024]{2,1,0:T(8,128)(2,1)}) %all-gather.57.cloned.1.call-update) | async-done | bytes 4194320 | tf_op jit(solution)/shard_map/all_gather | solution.py:122
  3499.7 99.3 %reduce-scatter.41.cloned.1.call-done = f32[4,256,1024]{2,1,0:T(8,128)} async-done(((f32[8,256,1024]{2,1,0:T(8,128)}), f32[4,256,1024]{2,1,0:T(8,128)}) %reduce-scatter.41.cloned.1.call-update) | async-done | bytes 4194320 | tf_op jit(solution)/shard_map/reduce_scatter | solution.py:126
  3615.6 56.9 %all-gather.59.cloned.1.call-done = bf16[8,256,1024]{2,1,0:T(8,128)(2,1)} async-done(((bf16[4,256,1024]{2,1,0:T(8,128)(2,1)}), bf16[8,256,1024]{2,1,0:T(8,128)(2,1)}) %all-gather.59.cloned.1.call-update) | async-done | bytes 4194320 | tf_op jit(solution)/shard_map/all_gather | solution.py:122
  3714.5 99.3 %reduce-scatter.43.cloned.1.call-done = f32[4,256,1024]{2,1,0:T(8,128)} async-done(((f32[8,256,1024]{2,1,0:T(8,128)}), f32[4,256,1024]{2,1,0:T(8,128)}) %reduce-scatter.43.cloned.1.call-update) | async-done | bytes 4194320 | tf_op jit(solution)/shard_map/reduce_scatter | solution.py:126
  3830.4 56.9 %all-gather.61.cloned.1.call-done = bf16[8,256,1024]{2,1,0:T(8,128)(2,1)} async-done(((bf16[4,256,1024]{2,1,0:T(8,128)(2,1)}), bf16[8,256,1024]{2,1,0:T(8,128)(2,1)}) %all-gather.61.cloned.1.call-update) | async-done | bytes 4194320 | tf_op jit(solution)/shard_map/all_gather | solution.py:122
  4334.1 266.4 %all-reduce.14.cloned.1.call-done = (f32[2,512,1024]{1,0,2:T(2,128)}, f32[2,2048,1024]{1,0,2:T(2,128)}) async-done(((f32[2,512,1024]{1,0,2:T(2,128)}, f32[2,2048,1024]{1,0,2:T(2,128)}), (f32[2,512,1024]{1,0,2:T(2,128)}, f32[2,2048,1024]{1,0,2:T(2,128)})) %all-reduce.14.cloned.1.call-update) | async-done | bytes 20971536
  4605.9 122.6 %all-reduce.12.cloned.1.call-done = f32[29696]{0:T(1024)} async-done(((f32[29696]{0:T(1024)}), f32[29696]{0:T(1024)}) %all-reduce.12.cloned.1.call-update) | async-done | bytes 118800
  4729.9 137.9 %reduce-scatter.51.cloned.1.call-done = f32[2,64,1536]{2,1,0:T(8,128)} async-done(((f32[2,1024,1536]{2,1,0:T(8,128)}), f32[2,64,1536]{2,1,0:T(8,128)}) %reduce-scatter.51.cloned.1.call-update) | async-done | bytes 786448 | tf_op jit(solution)/shard_map/reduce_scatter | solution.py:437
  4872.3 142.2 %reduce-scatter.61.cloned.1.call-done = f32[32,1344]{1,0:T(8,128)} async-done(((f32[1024,1344]{1,0:T(8,128)}), f32[32,1344]{1,0:T(8,128)}) %reduce-scatter.61.cloned.1.call-update) | async-done | bytes 172048
  5016.4 278.3 %reduce-scatter.59.cloned.1.call-done = f32[64,7168]{1,0:T(8,128)} async-done(((f32[1024,7168]{1,0:T(8,128)}), f32[64,7168]{1,0:T(8,128)}) %reduce-scatter.59.cloned.1.call-update) | async-done | bytes 1835024 | tf_op jit(solution)/shard_map/reduce_scatter | solution.py:441
  (1123 shorter events, 2139.2 us)
Async XLA Ops:
  8.9 191.5 %all-gather.35.cloned.1.call-start = ((), (), s32[]{:S(2)}) async-start(), calls=%async_computation.24 | async-start | bytes 2973696 | tf_op jit(solution)/shard_map/all_gather | solution.py:281
  10.6 305.3 %all-gather.37.cloned.1.call-start = ((), (), s32[]{:S(2)}) async-start(), calls=%async_computation.25 | async-start | bytes 15597568 | tf_op jit(solution)/shard_map/all_gather | solution.py:293
  13.2 349.0 %all-gather.71.cloned.1.call-start = ((), (), s32[]{:S(2)}) async-start(), calls=%async_computation.61 | async-start | bytes 3342336 | tf_op jit(solution)/shard_map/all_gather | solution.py:306
  338.5 238.1 %reduce-scatter.31.cloned.1.call-start = ((), (), s32[]{:S(2)}) async-start(), calls=%async_computation.35 | async-start | bytes 12582912 | tf_op jit(solution)/shard_map/reduce_scatter | solution.py:118
  479.3 207.9 %all-gather.49.cloned.1.call-start = ((), (), s32[]{:S(2)}) async-start(), calls=%async_computation.36 | async-start | bytes 6291456 | tf_op jit(solution)/shard_map/all_gather | solution.py:114
  587.2 268.8 %reduce-scatter.33.cloned.1.call-start = ((), (), s32[]{:S(2)}) async-start(), calls=%async_computation.37 | async-start | bytes 12582912 | tf_op jit(solution)/shard_map/reduce_scatter | solution.py:118
  758.7 202.4 %all-gather.51.cloned.1.call-start = ((), (), s32[]{:S(2)}) async-start(), calls=%async_computation.38 | async-start | bytes 6291456 | tf_op jit(solution)/shard_map/all_gather | solution.py:114
  865.9 252.5 %reduce-scatter.35.cloned.1.call-start = ((), (), s32[]{:S(2)}) async-start(), calls=%async_computation.39 | async-start | bytes 12582912 | tf_op jit(solution)/shard_map/reduce_scatter | solution.py:118
  1019.5 209.1 %all-gather.53.cloned.1.call-start = ((), (), s32[]{:S(2)}) async-start(), calls=%async_computation.40 | async-start | bytes 6291456 | tf_op jit(solution)/shard_map/all_gather | solution.py:114
  1128.2 269.3 %reduce-scatter.37.cloned.1.call-start = ((), (), s32[]{:S(2)}) async-start(), calls=%async_computation.41 | async-start | bytes 12582912 | tf_op jit(solution)/shard_map/reduce_scatter | solution.py:118
  1413.6 197.6 %reduce-scatter.45.cloned.1.call-start = ((), (), s32[]{:S(2)}) async-start(), calls=%async_computation.50 | async-start | bytes 12582912 | tf_op jit(solution)/shard_map/reduce_scatter | solution.py:126
  1511.9 173.0 %all-gather.65.cloned.1.call-start = ((), (), s32[]{:S(2)}) async-start(), calls=%async_computation.51 | async-start | bytes 6291456 | tf_op jit(solution)/shard_map/all_gather | solution.py:122
  1627.9 221.3 %reduce-scatter.47.cloned.1.call-start = ((), (), s32[]{:S(2)}) async-start(), calls=%async_computation.52 | async-start | bytes 12582912 | tf_op jit(solution)/shard_map/reduce_scatter | solution.py:126
  1865.7 198.0 %reduce-scatter.49.cloned.1.call-start = ((), (), s32[]{:S(2)}) async-start(), calls=%async_computation.54 | async-start | bytes 12582912 | tf_op jit(solution)/shard_map/reduce_scatter | solution.py:126
  2080.2 223.4 %reduce-scatter.57.cloned.1.call-start = ((), (), s32[]{:S(2)}) async-start(), calls=%async_computation.59 | async-start | bytes 12582912 | tf_op jit(solution)/shard_map/reduce_scatter | solution.py:126
  2312.6 213.3 %reduce-scatter.23.cloned.1.call-start = ((), (), s32[]{:S(2)}) async-start(), calls=%async_computation.27 | async-start | bytes 12582912 | tf_op jit(solution)/shard_map/reduce_scatter | solution.py:118
  2535.5 190.3 %reduce-scatter.25.cloned.1.call-start = ((), (), s32[]{:S(2)}) async-start(), calls=%async_computation.29 | async-start | bytes 12582912 | tf_op jit(solution)/shard_map/reduce_scatter | solution.py:118
  2735.1 212.9 %reduce-scatter.27.cloned.1.call-start = ((), (), s32[]{:S(2)}) async-start(), calls=%async_computation.31 | async-start | bytes 12582912 | tf_op jit(solution)/shard_map/reduce_scatter | solution.py:118
  2957.4 190.3 %reduce-scatter.29.cloned.1.call-start = ((), (), s32[]{:S(2)}) async-start(), calls=%async_computation.33 | async-start | bytes 12582912 | tf_op jit(solution)/shard_map/reduce_scatter | solution.py:118
  3163.8 197.6 %reduce-scatter.39.cloned.1.call-start = ((), (), s32[]{:S(2)}) async-start(), calls=%async_computation.43 | async-start | bytes 12582912 | tf_op jit(solution)/shard_map/reduce_scatter | solution.py:126
  3262.0 172.9 %all-gather.57.cloned.1.call-start = ((), (), s32[]{:S(2)}) async-start(), calls=%async_computation.44 | async-start | bytes 6291456 | tf_op jit(solution)/shard_map/all_gather | solution.py:122
  3377.9 221.0 %reduce-scatter.41.cloned.1.call-start = ((), (), s32[]{:S(2)}) async-start(), calls=%async_computation.45 | async-start | bytes 12582912 | tf_op jit(solution)/shard_map/reduce_scatter | solution.py:126
  3499.6 172.9 %all-gather.59.cloned.1.call-start = ((), (), s32[]{:S(2)}) async-start(), calls=%async_computation.46 | async-start | bytes 6291456 | tf_op jit(solution)/shard_map/all_gather | solution.py:122
  3615.6 198.2 %reduce-scatter.43.cloned.1.call-start = ((), (), s32[]{:S(2)}) async-start(), calls=%async_computation.47 | async-start | bytes 12582912 | tf_op jit(solution)/shard_map/reduce_scatter | solution.py:126
  3714.4 172.8 %all-gather.61.cloned.1.call-start = ((), (), s32[]{:S(2)}) async-start(), calls=%async_computation.48 | async-start | bytes 6291456 | tf_op jit(solution)/shard_map/all_gather | solution.py:122
  3830.4 354.1 %reduce-scatter.55.cloned.1.call-start = ((), (), s32[]{:S(2)}) async-start(), calls=%async_computation.58 | async-start | bytes 12582912 | tf_op jit(solution)/shard_map/reduce_scatter | solution.py:126
  3952.1 379.9 %reduce-scatter.53.cloned.1.call-start = ((), (), s32[]{:S(2)}) async-start(), calls=%async_computation.57 | async-start | bytes 17825792 | tf_op jit(solution)/shard_map/reduce_scatter | solution.py:439
  4009.1 591.4 %all-reduce.14.cloned.1.call-start = ((), (), s32[]{:S(2)}) async-start(), calls=%async_computation.72 | async-start | bytes 41943040
  4226.1 502.5 %all-reduce.12.cloned.1.call-start = ((), (), s32[]{:S(2)}) async-start(), calls=%async_computation.71 | async-start | bytes 237568
  4260.9 606.9 %reduce-scatter.51.cloned.1.call-start = ((), (), s32[]{:S(2)}) async-start(), calls=%async_computation.56 | async-start | bytes 13369344 | tf_op jit(solution)/shard_map/reduce_scatter | solution.py:437
  4271.6 742.9 %reduce-scatter.61.cloned.1.call-start = ((), (), s32[]{:S(2)}) async-start(), calls=%async_computation.70 | async-start | bytes 5947392
  4294.2 1000.5 %reduce-scatter.59.cloned.1.call-start = ((), (), s32[]{:S(2)}) async-start(), calls=%async_computation.60 | async-start | bytes 31195136 | tf_op jit(solution)/shard_map/reduce_scatter | solution.py:441
  (346 other events, 17329.0 us)
Sparse Core Ops, SparseCore 0:
  14.2 123.9 all-reduce.9
  141.6 58.7 all-gather.34
  203.4 112.4 all-gather.36
  477.3 99.2 reduce-scatter.30
  758.2 97.7 reduce-scatter.32
  1019.1 99.2 reduce-scatter.34
  1299.7 97.7 reduce-scatter.36
  1512.0 99.2 reduce-scatter.44
  1628.0 56.7 all-gather.64
  1749.9 99.2 reduce-scatter.46
  1865.8 56.7 all-gather.66
  1964.4 99.2 reduce-scatter.48
  2201.8 101.6 reduce-scatter.56
  2426.6 99.2 reduce-scatter.22
  2535.6 56.7 all-gather.40
  2626.5 99.2 reduce-scatter.24
  2735.2 56.7 all-gather.42
  2848.8 99.2 reduce-scatter.26
  2957.5 56.7 all-gather.44
  3048.4 99.2 reduce-scatter.28
  3262.1 99.2 reduce-scatter.38
  3378.1 56.7 all-gather.56
  3499.7 99.2 reduce-scatter.40
  3714.5 99.2 reduce-scatter.42
  3830.5 56.7 all-gather.60
  3952.3 99.2 reduce-scatter.54
  4055.6 178.4 reduce-scatter.52
  4238.2 362.2 all-reduce.13
  4607.4 121.1 all-reduce.11
  4733.0 134.7 reduce-scatter.50
  4870.0 144.3 reduce-scatter.60
  5019.0 275.7 reduce-scatter.58
  (17 shorter events, 871.7 us)
where the time goes:
time: 5380 us; the launch traced here: 5370 us
  waiting for transfers between devices  3840 us (71%)
  matrix products  901 us (17%)
  other arithmetic  344 us (6%)
  local copies, waits for them, and re-layouts  198 us (4%)
    dot_general x94, matrix products, contract(): return jnp.einsum(form, left, right, preferred_element_type=jnp.float32)  888 us
    reduce_scatter x8, waiting for transfers between devices, collect(): return lax.psum_scatter(partial_sum, 'tp', scatter_dimension=0, tiled=True)  786 us
    reduce_scatter x8, waiting for transfers between devices, collect_grad(): return lax.psum_scatter(partial_sum, 'tp', scatter_dimension=0, tiled=True)  673 us
    unnamed x53, waiting for transfers between devices  654 us
    all_gather x8, waiting for transfers between devices, spread(): return lax.all_gather(value.astype(jnp.bfloat16), 'tp', axis=0, tiled=True)  455 us
    all_gather x8, waiting for transfers between devices, spread_grad(): return lax.all_gather(value.astype(jnp.bfloat16), 'tp', axis=0, tiled=True)  455 us
    reduce_scatter x1, waiting for transfers between devices, per_device(): lax.psum_scatter(grad_ada, 'fsdp', scatter_dimension=0, tiled=True)  278 us
    reduce_scatter x1, waiting for transfers between devices, per_device(): lax.psum_scatter(stack_qkv, 'fsdp', scatter_dimension=1, tiled=True)  138 us
  transfers between devices with their start and end apart: 53, of which 47 were waited for; matrix products, arithmetic and copies ran while one was open for 11% of the time, Pallas kernels for 0%

commit v1 on v0

v1 whole, which is shorter than its diff:
```python
import functools
import math

import jax
import jax.numpy as jnp
from jax import lax
from jax.experimental import pallas as pl
from jax.experimental.pallas import tpu as pltpu
from jax.sharding import PartitionSpec as P

D = 1024
HEAD = 64
FF = 4096
CH = 16
FREQ = 256
CLASSES = 32
SIDE = 16
LAYERS = 2
STEP = 10
TOK_LAT = 256
MODS = 14336


CLIP_AT = 0.01
RATE = 0.05
BETA_ONE = 0.5
BETA_TWO = 0.5
DECAY = 0.01
ADAM_EPS = 1e-08
NORM_EPS = 1e-06
EXACT = lax.Precision.HIGHEST


def contract(left, right, form):
    return jnp.einsum(form, left, right, preferred_element_type=jnp.float32)


def exact_dot(left, right):
    return jnp.dot(left, right, precision=EXACT)


def layer_norm(value):
    center = value - jnp.mean(value, -1, keepdims=True)
    return center * lax.rsqrt(jnp.mean(center * center, -1, keepdims=True) + NORM_EPS)


def gelu_tanh(value):
    return jax.nn.gelu(value, approximate=True)


def local_back(func, value, grad):
    _, pullback = jax.vjp(func, value)
    return pullback(grad)[0]


def noise_levels(steps):
    angle = (steps.astype(jnp.float32) / 1000.0 + 0.008) / 1.008 * (math.pi / 2)
    return (jnp.cos(angle), jnp.sin(angle))


def step_features(steps):
    half = FREQ // 2
    rates = jnp.exp(-math.log(10000.0) * jnp.arange(half, dtype=jnp.float32) / half)
    phase = steps.astype(jnp.float32)[:, None] * rates[None, :]
    return jnp.concatenate([jnp.cos(phase), jnp.sin(phase)], axis=1)


def place_table():
    quarter = D // 4
    rates = 1.0 / 10000.0 ** (jnp.arange(quarter, dtype=jnp.float32) / quarter)
    index = jnp.arange(TOK_LAT, dtype=jnp.int32)
    rows = (index // SIDE).astype(jnp.float32)[:, None] * rates[None, :]
    columns = (index % SIDE).astype(jnp.float32)[:, None] * rates[None, :]
    return jnp.concatenate(
        [jnp.sin(rows), jnp.cos(rows), jnp.sin(columns), jnp.cos(columns)], axis=1
    )


def split_embed(embed):
    start = FREQ + D
    return (
        embed[:FREQ],
        embed[FREQ:start],
        embed[start : start + CH],
        embed[start + CH : start + CH + CLASSES],
        embed[start + CH + CLASSES :],
    )


def split_bias(bias):
    layers = []
    for layer in range(LAYERS):
        base = MODS + layer * (2 * D + FF)
        layers.append(
            (
                bias[base : base + D],
                bias[base + D : base + D + FF],
                bias[base + D + FF : base + 2 * D + FF],
            )
        )
    tail = MODS + LAYERS * (2 * D + FF)
    return (
        bias[:MODS],
        layers,
        bias[tail : tail + D],
        bias[tail + D : tail + 2 * D],
        bias[tail + 2 * D : tail + 3 * D],
    )


LANES = 128
FSDP, TP = ("fsdp", "tp")
GELU_A = math.sqrt(2.0 / math.pi)
GELU_B = 0.044715
VMEM_BYTES = 60 * 1024 * 1024


def swap(value, flip):
    name, bits = (FSDP, flip[0]) if flip[0] else (TP, flip[1])
    return lax.ppermute(value, name, [(i, i ^ bits) for i in range(lax.axis_size(name))])


def bit_flips(name):
    bits = [1 << i for i in range(lax.axis_size(name).bit_length() - 1)]
    return [(bit, 0) if name == FSDP else (0, bit) for bit in bits]


def far_flips():
    return [(k << 2, 0) for k in range(max(lax.axis_size(FSDP) >> 2, 1))]


def middle_flips(first):
    fsdp, tp = (bit_flips(FSDP)[1:2], bit_flips(TP))
    return fsdp + tp if first == FSDP else tp + fsdp


CORE = (1, 0)


def both(one, other):
    return (one[0] ^ other[0], one[1] ^ other[1])


def gather_far(value):
    flips = far_flips()
    held = [value[None]] + [swap(value, flip)[None] for flip in flips[1:]]
    return jnp.concatenate(held, axis=0), flips


def double(held, flips, flip):
    return jnp.concatenate([held, swap(held, flip)], axis=0), flips + [both(f, flip) for f in flips]


def gather_relative(value, hops):
    held, flips = (value[None], [(0, 0)])
    for flip in hops:
        held, flips = double(held, flips, flip)
    return held, flips


def gather_small(value, axes):
    held, _ = gather_relative(value, [flip for name in reversed(axes) for flip in bit_flips(name)])
    return jnp.take(held, jnp.arange(held.shape[0]) ^ lax.axis_index(axes), axis=0)


def split_bit(value, axis, index):
    return lax.index_in_dim(value, index, axis, keepdims=False)


def scatter_sum(value, axes, axis):
    flips = [flip for name in reversed(axes) for flip in bit_flips(name)][::-1]
    count = 1 << len(flips)
    shape = value.shape
    value = value.reshape(shape[:axis] + (count, shape[axis] // count) + shape[axis + 1 :])
    value = jnp.take(value, jnp.arange(count) ^ lax.axis_index(axes), axis=axis)
    keep = jnp.moveaxis(value, axis, 0).reshape(
        (2,) * len(flips) + shape[:axis] + (shape[axis] // count,) + shape[axis + 1 :]
    )
    dims = list(flips)
    for flip in sorted(flips, key=lambda flip: flip != CORE):
        at = dims.index(flip)
        keep = split_bit(keep, at, 0) + swap(split_bit(keep, at, 1), flip)
        dims = dims[:at] + dims[at + 1 :]
    return keep


def exchange_tp(value):
    count, rank = (lax.axis_size(TP), lax.axis_index(TP))
    value = jnp.take(value, jnp.arange(count) ^ rank, axis=0)
    got = jnp.stack([value[0]] + [swap(value[k], (0, k)) for k in range(1, count)])
    return jnp.take(got, jnp.arange(count) ^ rank, axis=0)


def push_kernel(plans, arrays, *refs):
    ins, outs = (refs[:arrays], refs[arrays : 2 * arrays])
    send, recv = refs[2 * arrays :]
    fsdp, tp = (lax.axis_index(FSDP), lax.axis_index(TP))
    count = lax.axis_size(FSDP) * lax.axis_size(TP)
    me = fsdp * lax.axis_size(TP) + tp

    def partner(k):
        other = lax.rem(me + k, count)
        return (other // lax.axis_size(TP), lax.rem(other, lax.axis_size(TP)))

    barrier = pltpu.get_barrier_semaphore()

    def greet(k, carry):
        pl.semaphore_signal(barrier, inc=1, device_id=partner(k), device_id_type=pl.DeviceIdType.MESH)
        return carry

    lax.fori_loop(1, count, greet, 0)
    pl.semaphore_wait(barrier, count - 1)

    def copies(k):
        other = lax.rem(me + k, count)
        found = []
        for i, (plan, source, target) in enumerate(zip(plans, ins, outs)):
            view = source.at[other] if plan == 1 else source
            found.append(
                pltpu.make_async_remote_copy(
                    src_ref=view,
                    dst_ref=target.at[me],
                    send_sem=send.at[i, k],
                    recv_sem=recv.at[i, k],
                    device_id=partner(k),
                    device_id_type=pl.DeviceIdType.MESH,
                )
            )
        return found

    def start(k, carry):
        for plan, copy in zip(plans, copies(k)):
            if plan > 1:
                pl.when(partner(k)[1] < plan - 1)(copy.start)
            else:
                copy.start()
        return carry

    def finish(k, carry):
        for plan, copy in zip(plans, copies(k)):
            if plan > 1:
                pl.when(partner(k)[1] < plan - 1)(copy.wait_send)
                pl.when(tp < plan - 1)(copy.wait_recv)
            else:
                copy.wait()
        return carry

    lax.fori_loop(1, count, start, 0)
    for plan, source, target in zip(plans, ins, outs):
        target[pl.ds(me, 1)] = source[pl.ds(me, 1)] if plan == 1 else source[...][None]
    lax.fori_loop(1, count, finish, 0)


def push(arrays, plans, identity):
    count = lax.axis_size(FSDP) * lax.axis_size(TP)
    shapes = [array.shape[1:] if plan == 1 else array.shape for array, plan in zip(arrays, plans)]
    block = pl.BlockSpec(memory_space=pltpu.VMEM)
    return pl.pallas_call(
        functools.partial(push_kernel, plans, len(arrays)),
        in_specs=[block] * len(arrays),
        out_specs=[block] * len(arrays),
        out_shape=[
            jax.ShapeDtypeStruct((count,) + shape, array.dtype) for shape, array in zip(shapes, arrays)
        ],
        scratch_shapes=[pltpu.SemaphoreType.DMA((len(arrays), count))] * 2,
        compiler_params=pltpu.CompilerParams(
            collective_id=identity, has_side_effects=True, vmem_limit_bytes=VMEM_BYTES
        ),
        cost_estimate=pl.CostEstimate(flops=int(5e9), bytes_accessed=int(5e7), transcendentals=0),
    )(*arrays)


def flipped(index, bits):
    result, bit = (index, 1)
    while bit <= bits:
        if bits & bit:
            result = result + bit * (1 - 2 * lax.rem(index // bit, 2))
        bit *= 2
    return result


def head_kernel(packed, step_in, cond, modulate, shard, *refs):
    packed_all, step_in_all, cond_all, modulate_all, matrix = refs[:5]
    send, recv, small_send, small_recv, local = refs[5:]
    fsdp, tp = (lax.axis_index(FSDP), lax.axis_index(TP))
    tp_count = lax.axis_size(TP)
    count = lax.axis_size(FSDP) * tp_count
    me = fsdp * tp_count + tp
    slot = lax.rem(fsdp, 4)

    def device(k):
        other = lax.rem(me + k, count)
        return (other // tp_count, lax.rem(other, tp_count))

    barrier = pltpu.get_barrier_semaphore()

    def greet(k, carry):
        pl.semaphore_signal(barrier, inc=1, device_id=device(k), device_id_type=pl.DeviceIdType.MESH)
        return carry

    lax.fori_loop(1, count, greet, 0)
    pl.semaphore_wait(barrier, count - 1)

    made = []

    def remote(source, target, flip):
        copy = pltpu.make_async_remote_copy(
            src_ref=source,
            dst_ref=target,
            send_sem=send.at[len(made)],
            recv_sem=recv.at[len(made)],
            device_id=(flipped(fsdp, flip[0]), flipped(tp, flip[1])),
            device_id_type=pl.DeviceIdType.MESH,
        )
        made.append(copy)
        copy.start()
        return copy

    rows, columns = shard.shape

    def region(flip, cols):
        row = pl.multiple_of(flipped(fsdp, flip[0]) * rows, rows)
        return matrix.at[flipped(tp, flip[1]), pl.ds(row, rows), cols]

    every = slice(0, columns)
    far = far_flips()
    own_copies = [
        pltpu.make_async_copy(modulate, modulate_all.at[slot], local.at[0]),
        pltpu.make_async_copy(shard, region((0, 0), every), local.at[1]),
    ]
    for copy in own_copies:
        copy.start()
    near = [remote(modulate, modulate_all.at[slot], (2, 0))]
    under_way = [remote(shard, region((0, 0), every), flip) for flip in far[1:]]
    plane = [(f, t) for f in range(4) for t in range(tp_count)][1:]
    last = [remote(cond, cond_all.at[slot * tp_count + tp], flip) for flip in plane]

    def small(k):
        pairs = ((packed, packed_all), (step_in, step_in_all))
        return [
            pltpu.make_async_remote_copy(
                src_ref=source,
                dst_ref=target.at[me],
                send_sem=small_send.at[i, k],
                recv_sem=small_recv.at[i, k],
                device_id=device(k),
                device_id_type=pl.DeviceIdType.MESH,
            )
            for i, (source, target) in enumerate(pairs)
        ]

    def start_small(k, carry):
        for copy in small(k):
            copy.start()
        return carry

    def finish_small(k, carry):
        for copy in small(k):
            copy.wait()
        return carry

    lax.fori_loop(1, count, start_small, 0)
    packed_all[pl.ds(me, 1)] = packed[...][None]
    step_in_all[pl.ds(me, 1)] = step_in[...][None]
    cond_all[pl.ds(slot * tp_count + tp, 1)] = cond[...][None]
    for copy in own_copies:
        copy.wait()
    for copy in near:
        copy.wait()
    last.append(remote(modulate, modulate_all.at[slot], CORE))
    partner = flipped(slot, 2)
    last.append(remote(modulate_all.at[partner], modulate_all.at[partner], CORE))
    for copy in under_way:
        copy.wait()
    orders = (middle_flips(FSDP), middle_flips(TP))
    held = [list(far), list(far)]
    halves = (slice(0, columns // 2), slice(columns // 2, columns))
    for step in range(len(orders[0])):
        under_way = []
        for color, cols in enumerate(halves):
            flip = orders[color][step]
            under_way += [remote(region(f, cols), region(f, cols), flip) for f in held[color]]
            held[color] = held[color] + [both(f, flip) for f in held[color]]
        for copy in under_way:
            copy.wait()
    last += [remote(region(f, every), region(f, every), CORE) for f in held[0]]
    lax.fori_loop(1, count, finish_small, 0)
    for copy in last:
        copy.wait()


def run_head(packed, step_in, cond, modulate, shard, identity):
    tp, fsdp = (lax.axis_size(TP), lax.axis_size(FSDP))
    count = fsdp * tp
    rows, columns = shard.shape
    vmem = pl.BlockSpec(memory_space=pltpu.VMEM)
    total = fsdp // 4 + 4 * tp + 2 + 2 * (fsdp // 4) * (2 * tp - 1) + fsdp * tp
    shapes = [
        ((count,) + packed.shape, F32),
        ((count,) + step_in.shape, BF16),
        ((4 * tp,) + cond.shape, BF16),
        ((4,) + modulate.shape, BF16),
        ((tp, rows * fsdp, columns), BF16),
    ]
    return pl.pallas_call(
        head_kernel,
        in_specs=[vmem] * 3 + [ANY] * 2,
        out_specs=[vmem] * 3 + [ANY] * 2,
        out_shape=[jax.ShapeDtypeStruct(shape, dtype) for shape, dtype in shapes],
        scratch_shapes=[pltpu.SemaphoreType.DMA((total,))] * 2
        + [pltpu.SemaphoreType.DMA((2, count))] * 2
        + [pltpu.SemaphoreType.DMA((2,))],
        compiler_params=pltpu.CompilerParams(
            collective_id=identity, has_side_effects=True, vmem_limit_bytes=VMEM_BYTES
        ),
        cost_estimate=pl.CostEstimate(flops=int(4e10), bytes_accessed=int(1e8), transcendentals=0),
    )(packed, step_in, cond, modulate, shard)


def padded(vector):
    return jnp.pad(vector, (0, -vector.shape[0] % (8 * LANES))).reshape(-1, LANES)


class GradientSum:
    def __init__(self, keep, send, first):
        fsdp = bit_flips(FSDP)
        self.dims = bit_flips(TP)[::-1] + fsdp[2:][::-1] + fsdp[1:2]
        self.rows, self.columns = (keep.shape[1] * 2 // lax.axis_size(FSDP), keep.shape[2])
        self.flips = middle_flips(first)[::-1]
        self.keep = keep.reshape((2,) * len(self.dims) + (self.rows, self.columns))
        self.sent = send
        self.next = CORE
        self.far = None

    def step(self):
        got = swap(self.sent, self.next).reshape(self.keep.shape)

        def part(axis, index):
            return split_bit(self.keep, axis, index).astype(F32) + split_bit(got, axis, index).astype(F32)

        if self.flips:
            self.next = self.flips.pop(0)
            axis = self.dims.index(self.next)
            self.sent, self.keep = (part(axis, 1).astype(BF16), part(axis, 0).astype(BF16))
            self.dims = self.dims[:axis] + self.dims[axis + 1 :]
            return [self.sent]
        blocks = (-1, self.rows, self.columns)
        self.keep, got = (self.keep.reshape(blocks), got.reshape(blocks))
        self.far = [part(0, k).astype(BF16) for k in range(1, self.keep.shape[0])]
        self.keep = part(0, 0)
        return self.far

    def finish(self):
        result = self.keep
        for flip, sent in zip(far_flips()[1:], self.far):
            result = result + swap(sent, flip).astype(F32)
        return result


def nt_dot(left, right):
    return lax.dot_general(left, right, (((1,), (1,)), ((), ())), preferred_element_type=jnp.float32)


def nn_dot(left, right):
    return lax.dot_general(left, right, (((1,), (0,)), ((), ())), preferred_element_type=jnp.float32)


def tn_dot(left, right):
    return lax.dot_general(left, right, (((0,), (0,)), ((), ())), preferred_element_type=jnp.float32)


def norm_parts(value):
    center = value - jnp.mean(value, -1, keepdims=True)
    inverse = lax.rsqrt(jnp.mean(center * center, -1, keepdims=True) + NORM_EPS)
    return center * inverse, inverse


def norm_back(normed, inverse, grad):
    mean_grad = jnp.mean(grad, -1, keepdims=True)
    mean_both = jnp.mean(grad * normed, -1, keepdims=True)
    return inverse * (grad - mean_grad - normed * mean_both)


def row_sum(value):
    return jnp.sum(value, axis=0, keepdims=True)


def column_copy(start, ref, target, sem):
    return [pltpu.make_async_copy(ref.at[:, :, pl.ds(start, target.shape[2])], target, sem)]


def run_copies(*groups):
    for group in groups:
        for copy in group:
            copy.start()
    for group in groups:
        for copy in group:
            copy.wait()


def lane_masks(dtype):
    lane = lax.broadcasted_iota(jnp.int32, (1, LANES), 1)
    return [((lane // HEAD) == i).astype(jnp.float32).astype(dtype) for i in range(LANES // HEAD)]


def attn_forward_kernel(info, columns, stream, mods, bias, *rest):
    parts, (seq_a, qkv, lse, att, branch, mid, seq_m, weight, sems) = (rest[0], rest[1:])
    tp = weight.shape[0]
    third = columns // 3

    @pl.when(pl.program_id(0) == 0)
    def _():
        run_copies(column_copy(info, parts, weight, sems))

    value = stream[...]
    normed, _ = norm_parts(value)
    seq_a[...] = (normed * (1.0 + mods[0, 1:2, :]) + mods[0, 0:1, :]).astype(jnp.bfloat16)
    for p in range(tp):
        qkv[:, p * columns : (p + 1) * columns] = nn_dot(
            seq_a[...], weight[p, :, :columns]
        ).astype(jnp.bfloat16)
    masks = lane_masks(jnp.bfloat16)
    for p in range(tp):
        for pair in range(third // LANES):
            base = p * columns + pair * LANES
            query = qkv[:, base : base + LANES]
            key = qkv[:, base + third : base + third + LANES]
            val = qkv[:, base + 2 * third : base + 2 * third + LANES]
            out = None
            for i, mask in enumerate(masks):
                scores = nt_dot(key, query * mask) * (1.0 / math.sqrt(HEAD))
                top = jnp.max(scores, axis=0, keepdims=True)
                raised = jnp.exp(scores - top)
                total = row_sum(raised)
                probs = (raised * (1.0 / total)).astype(jnp.bfloat16)
                head = (p * third + pair * LANES) // HEAD + i
                lse[0, head : head + 1, :] = top + jnp.log(total)
                term = tn_dot(probs, val * mask)
                out = term if out is None else out + term
            att[:, p * third + pair * LANES : p * third + (pair + 1) * LANES] = out.astype(jnp.bfloat16)
    total = None
    for p in range(tp):
        term = nt_dot(att[:, p * third : (p + 1) * third], weight[p, :, columns:])
        total = term if total is None else total + term
    branch[...] = total.astype(jnp.bfloat16)
    after = value + mods[0, 2:3, :] * (total + bias[...])
    mid[...] = after
    normed, _ = norm_parts(after)
    seq_m[...] = (normed * (1.0 + mods[0, 4:5, :]) + mods[0, 3:4, :]).astype(jnp.bfloat16)


def gelu_parts(value):
    square = value * value
    inner = GELU_A * (value + GELU_B * (square * value))
    return jnp.tanh(inner), square


def mlp_forward_kernel(info, chunk, seq_m, mid, mods, expand_bias, reduce_bias, *rest):
    parts_e, parts_r, pre, acted, branch, stream, w_expand, w_reduce, sems = rest
    tp, _, columns = w_expand.shape

    @pl.when(pl.program_id(0) == 0)
    def _():
        run_copies(
            column_copy(info[0], parts_e, w_expand, sems.at[0]),
            column_copy(info[1], parts_r, w_reduce, sems.at[1]),
        )

    total = None
    for p in range(tp):
        for start in range(0, columns, chunk):
            cols = slice(p * columns + start, p * columns + start + chunk)
            value = nn_dot(seq_m[...], w_expand[p, :, start : start + chunk]) + expand_bias[:, cols]
            pre[:, cols] = value
            bent, _ = gelu_parts(value)
            hidden = (0.5 * value * (1.0 + bent)).astype(jnp.bfloat16)
            acted[:, cols] = hidden
            term = nt_dot(hidden, w_reduce[p, :, start : start + chunk])
            total = term if total is None else total + term
    branch[...] = total.astype(jnp.bfloat16)
    stream[...] = mid[...] + mods[0, 5:6, :] * (total + reduce_bias[...])


def mlp_backward_kernel(info, chunk, grad_out, branch_m, pre, mid, branch_a, mods, reduce_bias, out_bias, *rest):
    parts_e, parts_r, seq_grad_m, grad_pre, grad_mid, seq_grad_a = rest[:6]
    mod_grads, d_out, d_expand, d_reduce, w_expand, w_reduce, sems = rest[6:]
    tp, _, columns = w_expand.shape

    @pl.when(pl.program_id(0) == 0)
    def _():
        run_copies(
            column_copy(info[0], parts_e, w_expand, sems.at[0]),
            column_copy(info[1], parts_r, w_reduce, sems.at[1]),
        )
        d_out[...] = jnp.zeros_like(d_out)
        d_expand[...] = jnp.zeros_like(d_expand)
        d_reduce[...] = jnp.zeros_like(d_reduce)

    grad = grad_out[...]
    carried = mods[0, 5:6, :] * grad
    d_reduce[...] += row_sum(carried)
    mod_grads[0, 5:6, :] = row_sum(grad * (branch_m[...].astype(jnp.float32) + reduce_bias[...]))
    seq_grad_m[...] = carried.astype(jnp.bfloat16)
    total = None
    for p in range(tp):
        for start in range(0, columns, chunk):
            cols = slice(p * columns + start, p * columns + start + chunk)
            back = nn_dot(seq_grad_m[...], w_reduce[p, :, start : start + chunk])
            value = pre[:, cols]
            bent, square = gelu_parts(value)
            slope = 0.5 * (1.0 + bent) + (0.5 * GELU_A) * value * (1.0 - bent * bent) * (
                1.0 + (3.0 * GELU_B) * square
            )
            low = (back * slope).astype(jnp.bfloat16)
            grad_pre[:, cols] = low
            d_expand[:, cols] += row_sum(low.astype(jnp.float32))
            term = nt_dot(low, w_expand[p, :, start : start + chunk])
            total = term if total is None else total + term
    normed, inverse = norm_parts(mid[...])
    mod_grads[0, 3:4, :] = row_sum(total)
    mod_grads[0, 4:5, :] = row_sum(total * normed)
    after = grad_out[...] + norm_back(normed, inverse, total * (1.0 + mods[0, 4:5, :]))
    grad_mid[...] = after
    mod_grads[0, 2:3, :] = row_sum(after * (branch_a[...].astype(jnp.float32) + out_bias[...]))
    carried = mods[0, 2:3, :] * after
    d_out[...] += row_sum(carried)
    seq_grad_a[...] = carried.astype(jnp.bfloat16)
    mod_grads[0, 0:2, :] = jnp.zeros((2, mod_grads.shape[2]), jnp.float32)


def attn_backward_kernel(info, columns, seq_grad, qkv, lse, stream, grad_mid, mods, *rest):
    parts, (grad_qkv, grad_in, mod_grads, back, weight, sems) = (rest[0], rest[1:])
    tp = weight.shape[0]
    third = columns // 3

    @pl.when(pl.program_id(0) == 0)
    def _():
        run_copies(column_copy(info, parts, weight, sems))

    masks = lane_masks(jnp.bfloat16)
    for p in range(tp):
        back[:, p * third : (p + 1) * third] = nn_dot(
            seq_grad[...], weight[p, :, columns:]
        ).astype(jnp.bfloat16)
    scale = 1.0 / math.sqrt(HEAD)
    for p in range(tp):
        for pair in range(third // LANES):
            base = p * columns + pair * LANES
            query = qkv[:, base : base + LANES]
            key = qkv[:, base + third : base + third + LANES]
            val = qkv[:, base + 2 * third : base + 2 * third + LANES]
            grad = back[:, p * third + pair * LANES : p * third + (pair + 1) * LANES]
            d_query, d_key, d_val = (None, None, None)
            for i, mask in enumerate(masks):
                head = (p * third + pair * LANES) // HEAD + i
                query_i, key_i, grad_i = (query * mask, key * mask, grad * mask)
                scores = nt_dot(key, query_i) * scale
                probs = jnp.exp(scores - lse[0, head : head + 1, :])
                d_probs = nt_dot(val, grad_i)
                d_scores = probs * (d_probs - row_sum(d_probs * probs))
                d_scores = d_scores.astype(jnp.bfloat16)
                terms = (
                    tn_dot(d_scores, key_i),
                    nn_dot(d_scores, query_i),
                    nn_dot(probs.astype(jnp.bfloat16), grad_i),
                )
                if i == 0:
                    d_query, d_key, d_val = terms
                else:
                    d_query, d_key, d_val = (d_query + terms[0], d_key + terms[1], d_val + terms[2])
            grad_qkv[:, base : base + LANES] = (d_query * scale).astype(jnp.bfloat16)
            grad_qkv[:, base + third : base + third + LANES] = (d_key * scale).astype(jnp.bfloat16)
            grad_qkv[:, base + 2 * third : base + 2 * third + LANES] = d_val.astype(jnp.bfloat16)
    total = None
    for p in range(tp):
        term = nt_dot(grad_qkv[:, p * columns : (p + 1) * columns], weight[p, :, :columns])
        total = term if total is None else total + term
    normed, inverse = norm_parts(stream[...])
    mod_grads[0, 0:1, :] = row_sum(total)
    mod_grads[0, 1:2, :] = row_sum(total * normed)
    grad_in[...] = grad_mid[...] + norm_back(normed, inverse, total * (1.0 + mods[0, 1:2, :]))


def final_kernel(scale_pred, stream, mods, noise, patch_out, grad_stream, mod_grads, d_patch, loss):
    @pl.when(pl.program_id(0) == 0)
    def _():
        d_patch[...] = jnp.zeros_like(d_patch)
        loss[...] = jnp.zeros_like(loss)

    normed, inverse = norm_parts(stream[...])
    final = (normed * (1.0 + mods[0, 1:2, :]) + mods[0, 0:1, :]).astype(jnp.bfloat16)
    error = nt_dot(final, patch_out[...]) - noise[0]
    loss[...] += row_sum(error * error)
    grad_pred = (error * scale_pred).astype(jnp.bfloat16)
    d_patch[...] += tn_dot(grad_pred, final)
    grad_final = nn_dot(grad_pred, patch_out[...])
    mod_grads[0, 0:1, :] = row_sum(grad_final)
    mod_grads[0, 1:2, :] = row_sum(grad_final * normed)
    grad_stream[...] = norm_back(normed, inverse, grad_final * (1.0 + mods[0, 1:2, :]))


def weight_grad_kernel(count, groups, place, left, right, *refs):
    turned = refs[-1]
    depth = turned.shape[0]
    rows = depth // count

    @pl.when((pl.program_id(0) == 0) & (pl.program_id(1) == 0))
    def _():
        for start in range(0, depth, LANES):
            block = jnp.transpose(left[:, start : start + LANES])
            for i in range(LANES // rows):
                k = place[0] ^ (start // rows + i)
                slot = (k % 2) * (count // 2) + k // 2
                turned[pl.ds(pl.multiple_of(slot * rows, rows), rows), :] = block[i * rows : (i + 1) * rows]

    half = depth // 2
    steps = pl.num_programs(1) // groups
    for group in range(groups):
        keep, send = refs[2 * group : 2 * group + 2]

        @pl.when(pl.program_id(1) // steps == group)
        def _():
            send[0] = nn_dot(turned[half:, :], right[...]).astype(jnp.bfloat16)
            keep[0] = nn_dot(turned[:half, :], right[...]).astype(jnp.bfloat16)


def params(semantics=1):
    return pltpu.CompilerParams(
        dimension_semantics=("arbitrary",) * semantics, vmem_limit_bytes=VMEM_BYTES
    )


ANY = pl.BlockSpec(memory_space=pl.ANY)
F32, BF16 = (jnp.float32, jnp.bfloat16)


def cost(flops, nbytes):
    return pl.CostEstimate(flops=int(flops), bytes_accessed=int(nbytes), transcendentals=0)


def hold(value, *after):
    def body(*refs):
        pass

    return pl.pallas_call(
        body,
        in_specs=[ANY] * (1 + len(after)),
        out_specs=ANY,
        out_shape=jax.ShapeDtypeStruct(value.shape, value.dtype),
        input_output_aliases={0: 0},
        cost_estimate=cost(0, 0),
    )(value, *after)


def token_rows(width, dtype):
    return ("token", (width,), dtype)


def latent_rows(dims, dtype):
    return ("latent", dims, dtype)


def one_sum(width):
    return ("sum", (1, width), F32)


def call_part(kernel, part, parts, latents, ins, anys, outs, scratch, estimate, after, before):
    count = latents // parts
    first = part * count

    def spec(kind, dims):
        if kind == "token":
            return pl.BlockSpec((TOK_LAT, dims[-1]), lambda i: (i + first, 0))
        if kind == "latent":
            return pl.BlockSpec((1,) + dims, lambda i: (i + first,) + (0,) * len(dims))
        return pl.BlockSpec(dims, lambda i: (0,) * len(dims))

    def dims_of(kind, array):
        return array.shape[1:] if kind == "latent" else array.shape

    out_shape = []
    for kind, dims, dtype in outs:
        lead = {"token": (latents * TOK_LAT,), "latent": (latents,), "sum": ()}[kind]
        out_shape.append(jax.ShapeDtypeStruct(lead + dims, dtype))
    filled = [i for i, (kind, _, _) in enumerate(outs) if kind != "sum"] if before else []
    head = len(ins) + len(anys)
    unused = len(filled) + len(after)

    def body(*refs):
        kernel(*refs[:head], *refs[head + unused :])

    return pl.pallas_call(
        body,
        grid=(count,),
        in_specs=[spec(kind, dims_of(kind, array)) for kind, array in ins] + [ANY] * (len(anys) + unused),
        out_specs=[spec(kind, dims) for kind, dims, _ in outs],
        out_shape=out_shape,
        scratch_shapes=scratch,
        input_output_aliases={head + j: i for j, i in enumerate(filled)},
        compiler_params=params(),
        cost_estimate=cost(estimate[0] / parts, estimate[1] / parts),
    )(*[array for _, array in ins], *anys, *[before[i] for i in filled], *after)


def call_parts(kernel, latents, ins, anys, outs, scratch, estimate, afters):
    parts = 2 if afters and latents % 2 == 0 else 1
    afters = afters or [list, list]
    result, sums = (None, None)
    for part in range(parts):
        after = afters[part]() if parts > 1 else afters[0]() + afters[1]()
        result = call_part(
            kernel, part, parts, latents, ins, anys, outs, scratch, estimate, after, result
        )
        own = [value for value, (kind, _, _) in zip(result, outs) if kind == "sum"]
        sums = own if sums is None else [a + b for a, b in zip(sums, own)]
    sums = iter(sums)
    return [next(sums) if kind == "sum" else value for value, (kind, _, _) in zip(result, outs)]


def run_attn_forward(stream, mods, out_bias, pieces, columns, afters):
    total, depth = stream.shape
    latents = total // TOK_LAT
    tp = lax.axis_size(TP)
    third = columns // 3
    width = columns + third
    return call_parts(
        functools.partial(attn_forward_kernel, pieces[1], columns),
        latents,
        [("token", stream), ("latent", mods), ("whole", out_bias)],
        [pieces[0]],
        [
            token_rows(depth, BF16),
            token_rows(tp * columns, BF16),
            latent_rows((tp * third // HEAD, TOK_LAT), F32),
            token_rows(tp * third, BF16),
            token_rows(depth, BF16),
            token_rows(depth, F32),
            token_rows(depth, BF16),
        ],
        [pltpu.VMEM((tp, depth, width), BF16), pltpu.SemaphoreType.DMA],
        (2 * total * depth * width * tp * 2.5, total * depth * 24),
        afters,
    )


def mlp_scratch(pieces_e, pieces_r, depth):
    tp = lax.axis_size(TP)
    columns = pieces_e[2]
    return [
        pltpu.VMEM((tp, depth, columns), BF16),
        pltpu.VMEM((tp, depth, columns), BF16),
        pltpu.SemaphoreType.DMA((2,)),
    ]


def run_mlp_forward(seq_m, mid, mods, expand_bias, reduce_bias, pieces_e, pieces_r, afters):
    total, depth = mid.shape
    hidden = expand_bias.shape[1]
    chunk = min(hidden // lax.axis_size(TP), 512)
    return call_parts(
        functools.partial(mlp_forward_kernel, (pieces_e[1], pieces_r[1]), chunk),
        total // TOK_LAT,
        [("token", seq_m), ("token", mid), ("latent", mods), ("whole", expand_bias), ("whole", reduce_bias)],
        [pieces_e[0], pieces_r[0]],
        [
            token_rows(hidden, F32),
            token_rows(hidden, BF16),
            token_rows(depth, BF16),
            token_rows(depth, F32),
        ],
        mlp_scratch(pieces_e, pieces_r, depth),
        (6 * total * depth * hidden, total * hidden * 6),
        afters,
    )


def run_mlp_backward(
    grad_out, branch_m, pre, mid, branch_a, mods, reduce_bias, out_bias, pieces_e, pieces_r, afters
):
    total, depth = mid.shape
    hidden = pre.shape[1]
    chunk = min(hidden // lax.axis_size(TP), 512)
    return call_parts(
        functools.partial(mlp_backward_kernel, (pieces_e[1], pieces_r[1]), chunk),
        total // TOK_LAT,
        [
            ("token", grad_out),
            ("token", branch_m),
            ("token", pre),
            ("token", mid),
            ("token", branch_a),
            ("latent", mods),
            ("whole", reduce_bias),
            ("whole", out_bias),
        ],
        [pieces_e[0], pieces_r[0]],
        [
            token_rows(depth, BF16),
            token_rows(hidden, BF16),
            token_rows(depth, F32),
            token_rows(depth, BF16),
            latent_rows((6, depth), F32),
            one_sum(depth),
            one_sum(hidden),
            one_sum(depth),
        ],
        mlp_scratch(pieces_e, pieces_r, depth),
        (6 * total * depth * hidden, total * hidden * 6),
        afters,
    )


def run_attn_backward(seq_grad, qkv, lse, stream, grad_mid, mods, pieces, columns, afters):
    total, depth = stream.shape
    tp = lax.axis_size(TP)
    third = columns // 3
    width = columns + third
    return call_parts(
        functools.partial(attn_backward_kernel, pieces[1], columns),
        total // TOK_LAT,
        [
            ("token", seq_grad),
            ("token", qkv),
            ("latent", lse),
            ("token", stream),
            ("token", grad_mid),
            ("latent", mods),
        ],
        [pieces[0]],
        [token_rows(tp * columns, BF16), token_rows(depth, F32), latent_rows((2, depth), F32)],
        [
            pltpu.VMEM((TOK_LAT, tp * third), BF16),
            pltpu.VMEM((tp, depth, width), BF16),
            pltpu.SemaphoreType.DMA,
        ],
        (2 * total * depth * width * tp * 3, total * depth * 24),
        afters,
    )


def run_final(stream, mods, noise, patch_out, scale_pred):
    total, depth = stream.shape
    return call_part(
        functools.partial(final_kernel, scale_pred),
        0,
        1,
        total // TOK_LAT,
        [("token", stream), ("latent", mods), ("latent", noise), ("whole", patch_out)],
        [],
        [
            token_rows(depth, F32),
            latent_rows((2, depth), F32),
            ("sum", (CH, depth), F32),
            one_sum(CH),
        ],
        [],
        (6 * total * depth * LANES, total * depth * 8),
        [],
        None,
    )


def start_sums(left, right, columns, firsts, after):
    total, depth = left.shape
    tp, count = (lax.axis_size(TP), lax.axis_size(FSDP))
    groups = len(firsts)
    width = columns // groups
    chunk = next(size for size in (768, 512, 384, 256, 128) if width % size == 0)
    steps = columns // chunk
    each = width // chunk
    place = jnp.stack([lax.axis_index(FSDP), lax.axis_index(TP)]).astype(jnp.int32)

    def out(group):
        return pl.BlockSpec(
            (1, depth // 2, chunk),
            lambda p, j, place: (p, 0, jnp.clip(j - group * each, 0, each - 1)),
        )

    def body(place, left, right, *rest):
        weight_grad_kernel(count, groups, place, left, right, *rest[len(after) :])

    results = pl.pallas_call(
        body,
        grid_spec=pltpu.PrefetchScalarGridSpec(
            num_scalar_prefetch=1,
            grid=(tp, steps),
            in_specs=[
                pl.BlockSpec((total, depth), lambda p, j, place: (0, 0)),
                pl.BlockSpec((total, chunk), lambda p, j, place: (0, (p ^ place[1]) * steps + j)),
            ]
            + [ANY] * len(after),
            out_specs=[out(i // 2) for i in range(2 * groups)],
            scratch_shapes=[pltpu.VMEM((depth, total), BF16)],
        ),
        out_shape=[jax.ShapeDtypeStruct((tp, depth // 2, width), BF16)] * (2 * groups),
        compiler_params=params(2),
        cost_estimate=cost(2.5 * total * depth * columns * tp, total * (depth + columns * tp) * 2),
    )(place, left, right, *after)
    return [GradientSum(*results[2 * i : 2 * i + 2], first) for i, first in enumerate(firsts)]


def heads_apart(matrix):
    rows, columns = matrix.shape
    return matrix.reshape(rows, columns // (3 * HEAD), 3, HEAD).swapaxes(1, 2).reshape(rows, columns)


def heads_together(matrix):
    rows, columns = matrix.shape
    return matrix.reshape(rows, 3, columns // (3 * HEAD), HEAD).swapaxes(1, 2).reshape(rows, columns)


def adam(weight, first, second, grad, factor):
    grad = grad * factor
    new_first = BETA_ONE * first + (1.0 - BETA_ONE) * grad
    new_second = BETA_TWO * second + (1.0 - BETA_TWO) * grad * grad
    first_hat = new_first / (1.0 - BETA_ONE**STEP)
    second_hat = new_second / (1.0 - BETA_TWO**STEP)
    new_weight = weight - RATE * (first_hat / (jnp.sqrt(second_hat) + ADAM_EPS) + DECAY * weight)
    return (new_first, new_second, new_weight)


def per_device(
    clean_patches,
    noise_patches,
    timesteps,
    labels,
    qkv_weight,
    out_weight,
    expand_weight,
    reduce_weight,
    modulate_weight,
    embed_weight,
    bias_vector,
    qkv_first,
    out_first,
    expand_first,
    reduce_first,
    modulate_first,
    embed_first,
    bias_first,
    qkv_second,
    out_second,
    expand_second,
    reduce_second,
    modulate_second,
    embed_second,
    bias_second,
):
    tp_count, fsdp_count = (lax.axis_size(TP), lax.axis_size(FSDP))
    tp_rank, fsdp_rank = (lax.axis_index(TP), lax.axis_index(FSDP))
    everywhere = (FSDP, TP)
    rank = lax.axis_index(everywhere)
    own, length, _ = clean_patches.shape
    latents = own * fsdp_count * tp_count
    depth, columns = (embed_weight.shape[0] - FREQ - 2 * CH - CLASSES, embed_weight.shape[1])
    cols_qkv = qkv_weight.shape[2]

    step_in_own, step_out_own, patch_in_own, table_own, patch_out_own = split_embed(
        embed_weight.astype(BF16)
    )
    group = timesteps.shape[0]
    vector = jnp.concatenate(
        [
            timesteps.astype(F32),
            labels.astype(F32),
            bias_vector,
            patch_in_own.astype(F32).reshape(-1),
            patch_out_own.astype(F32).reshape(-1),
        ]
    )
    def shard(name, layer):
        if name == "attn":
            parts = [heads_apart(qkv_weight[layer].astype(BF16)), out_weight[layer].T.astype(BF16)]
            return jnp.concatenate(parts, axis=1)
        if name == "expand":
            return expand_weight[layer].astype(BF16)
        return reduce_weight[layer].T.astype(BF16)

    low_modulate = modulate_weight.astype(BF16)
    cond_columns = jnp.concatenate([step_out_own, table_own], axis=0).reshape(-1, LANES)
    cond_rows = cond_columns.shape[0]
    cond_columns = jnp.pad(cond_columns, ((0, -cond_rows % 16), (0, 0)))
    packed, step_in, near_columns, near_modulate, matrix = run_head(
        padded(vector), step_in_own.reshape(-1, LANES), cond_columns, low_modulate, shard("attn", 0), 0
    )
    near_modulate = near_modulate.reshape(-1, modulate_weight.shape[1])
    near_columns = near_columns[:, :cond_rows].reshape(-1, depth + CLASSES, columns)
    near_columns = near_columns.swapaxes(0, 1).reshape(depth + CLASSES, -1)
    packed = packed.reshape(packed.shape[0], -1)[:, : vector.shape[0]]
    step_in = step_in.reshape(-1, FREQ, columns)
    first_of_tp = packed.reshape(fsdp_count, tp_count, -1)[:, 0]
    steps_all = first_of_tp[:, :group].reshape(-1).astype(jnp.int32)
    labels_all = first_of_tp[:, group : 2 * group].reshape(-1).astype(jnp.int32)
    at = 2 * group + bias_vector.shape[0]
    bias = packed[:, 2 * group : at].reshape(-1)

    def rows_of(block):
        return block.reshape(-1, CH, columns).swapaxes(0, 1).reshape(CH, -1).astype(BF16)

    patch_in_low = rows_of(packed[:, at : at + CH * columns])
    patch_out_low = rows_of(packed[:, at + CH * columns :])
    step_in_low = step_in.swapaxes(0, 1).reshape(FREQ, -1)
    ada_bias, layer_bias, step_in_bias, step_out_bias, patch_bias = split_bias(bias)

    def gather(shards):
        packed = jnp.concatenate(shards, axis=1)
        whole = lax.all_gather(packed, (TP, FSDP), axis=0, tiled=True)
        return whole.reshape(tp_count, -1, packed.shape[1])

    hidden = expand_weight.shape[2]
    width = hidden + cols_qkv + out_weight.shape[1]
    first_half = gather([shard("expand", 0), shard("reduce", 0)])
    rest = jnp.concatenate([shard(name, 1) for name in ("attn", "expand", "reduce")], axis=1)
    second_half = gather([hold(rest, matrix)])
    attn_width = width - hidden
    pieces = {
        ("attn", 0): (matrix, 0, attn_width),
        ("expand", 0): (first_half, 0, hidden),
        ("reduce", 0): (first_half, hidden, hidden),
        ("attn", 1): (second_half, 0, attn_width),
        ("expand", 1): (second_half, attn_width, hidden),
        ("reduce", 1): (second_half, width, hidden),
    }

    features = step_features(steps_all).astype(BF16)
    step_pre = contract(features, step_in_low, "gf,fd->gd") + step_in_bias
    step_hidden = jax.nn.silu(step_pre).astype(BF16)
    onehot = (labels_all[:, None] == jnp.arange(CLASSES, dtype=jnp.int32)[None, :]).astype(F32)
    wide = tp_count * columns
    near_bias = jnp.take(
        step_out_bias.reshape(-1, 4 * wide), fsdp_rank // 4, axis=0
    )
    cond_near = (
        contract(step_hidden, near_columns[:depth], "gd,de->ge")
        + near_bias
        + contract(onehot.astype(BF16), near_columns[depth:], "gc,cd->gd")
    )
    place = (fsdp_rank % 4) * wide
    act_near = jax.nn.silu(cond_near).astype(BF16)
    act_own = lax.dynamic_slice_in_dim(act_near, place, wide, axis=1)
    far = far_flips()
    far_order = jnp.array([flip[0] for flip in far]) ^ fsdp_rank
    act_far = jnp.take(act_near.reshape(fsdp_count, group, -1), far_order, axis=0)
    mod_part = contract(
        act_far.reshape(len(far) * group, -1), near_modulate, "gd,de->ge"
    ).reshape(len(far), group, -1)
    mod_sum = mod_part[0]
    for k, flip in list(enumerate(far))[1:]:
        mod_sum = mod_sum + swap(mod_part[k].astype(BF16), flip).astype(F32)
    mods = exchange_tp(mod_sum.reshape(tp_count, own, -1)).swapaxes(0, 1).reshape(own, -1) + ada_bias
    mods = mods.reshape(own, 6 * LAYERS + 2, -1)
    steps_own = lax.dynamic_slice_in_dim(timesteps, tp_rank * own, own)
    signal, spread_level = noise_levels(steps_own)
    noisy = (
        signal[:, None, None] * clean_patches + spread_level[:, None, None] * noise_patches
    ).astype(BF16)
    stream = contract(noisy, patch_in_low, "gtc,cd->gtd") + patch_bias + place_table()[None]
    stream = stream.reshape(-1, depth)
    kept = [None] * LAYERS

    for layer in range(LAYERS):
        modulation = mods[:, 6 * layer : 6 * layer + 6]
        out_bias, expand_bias, reduce_bias = [value[None] for value in layer_bias[layer]]
        seq_a, qkv, lse, att, branch_a, mid, seq_m = run_attn_forward(
            stream, modulation, out_bias, pieces["attn", layer], cols_qkv, None
        )
        pre, acted, branch_m, after = run_mlp_forward(
            seq_m,
            mid,
            modulation,
            expand_bias,
            reduce_bias,
            pieces["expand", layer],
            pieces["reduce", layer],
            None,
        )
        kept[layer] = (stream, seq_a, qkv, lse, att, branch_a, mid, seq_m, pre, acted, branch_m)
        stream = after
    cond_matrix = jnp.concatenate([step_out_own, table_own], axis=0).T
    cond_matrix = lax.all_gather(hold(cond_matrix, seq_m), everywhere, axis=0, tiled=True)
    total = float(latents * length * CH)
    grad_stream, grad_final_mod, grad_patch_out, loss_rows = run_final(
        stream, mods[:, 6 * LAYERS :], noise_patches, patch_out_low, 2.0 / total
    )
    loss_local = jnp.sum(loss_rows)

    sums, reduced = ({}, {})

    def step(*wanted):
        return lambda: [sent for key in wanted for sent in sums[key].step()]

    def mlp_backward(layer, grad, afters):
        stream, seq_a, qkv, lse, att, branch_a, mid, seq_m, pre, acted, branch_m = kept[layer]
        out_bias, expand_bias, reduce_bias = [value[None] for value in layer_bias[layer]]
        return run_mlp_backward(
            grad,
            branch_m,
            pre,
            mid,
            branch_a,
            mods[:, 6 * layer : 6 * layer + 6],
            reduce_bias,
            out_bias,
            pieces["expand", layer],
            pieces["reduce", layer],
            afters,
        )

    mod_grads = [None] * LAYERS
    layer_bias_grads = [None] * LAYERS
    cols_out = out_weight.shape[1]
    halves = 2 if cols_qkv // 2 % LANES == 0 else 1
    qkv_keys = [[("qkv", layer, i) for i in range(halves)] for layer in range(LAYERS)]
    rest_keys = [[("reduce", layer, 0), ("expand", layer, 0), ("out", layer, 0)] for layer in range(LAYERS)]
    mlp_afters = [(step(*rest_keys[1]), step(*qkv_keys[1])), (step(), step())]
    grad_afters = [[step(), step(*qkv_keys[1]), step(*qkv_keys[1])], [step()] * 3]

    attn_afters = [
        (step(*rest_keys[0][:2]), step(*rest_keys[0])),
        (step(*rest_keys[1][:2]), step(*rest_keys[1][2:])),
    ]

    def start(name, layer, left, right, width, firsts, after):
        started = start_sums(left, right, width, firsts, list(after))
        for i, total_sum in enumerate(started):
            sums[name, layer, i] = total_sum

    for layer in reversed(range(LAYERS)):
        stream, seq_a, qkv, lse, att, branch_a, mid, seq_m, pre, acted, branch_m = kept[layer]
        seq_grad_m, grad_pre, grad_mid, seq_grad_a, mod_late, d_out, d_expand, d_reduce = mlp_backward(
            layer, grad_stream, mlp_afters[layer]
        )
        after = grad_afters[layer]
        if layer == 0:
            mod_known = [jnp.zeros_like(mod_late[:, :2]), mod_late[:, 2:]] + mod_grads[1:]
            mod_known = jnp.concatenate(mod_known + [grad_final_mod], axis=1).reshape(own, -1)
            mod_known = mod_known.astype(BF16)
            known_columns = mod_known.reshape(own, tp_count, -1).swapaxes(0, 1)
            known_columns = exchange_tp(known_columns).reshape(group, -1)
            known_columns = lax.all_gather(known_columns, FSDP, axis=0, tiled=True)
        start("reduce", layer, seq_grad_m, acted, hidden, [FSDP], after[0]())
        start("expand", layer, seq_m, grad_pre, hidden, [TP], after[1]())
        start("out", layer, seq_grad_a, att, cols_out, [FSDP], after[2]())
        grad_qkv, grad_stream, mod_early = run_attn_backward(
            seq_grad_a,
            qkv,
            lse,
            stream,
            grad_mid,
            mods[:, 6 * layer : 6 * layer + 6],
            pieces["attn", layer],
            cols_qkv,
            attn_afters[layer],
        )
        after = step(*rest_keys[layer])()
        start("qkv", layer, seq_a, grad_qkv, cols_qkv, [TP, FSDP][:halves], after)
        mod_grads[layer] = jnp.concatenate([mod_early, mod_late[:, 2:]], axis=1)
        layer_bias_grads[layer] = (d_out[0], d_expand[0], d_reduce[0])
    last_sent = sums["qkv", 0, 0].sent
    mod_columns = modulate_weight.shape[1]
    mod_early = hold(mod_early, last_sent)
    mod_last = mod_early.reshape(own, -1).astype(BF16)
    last_columns = push([mod_last.reshape(-1, LANES)], [-(-mod_last.shape[1] // mod_columns) + 1], 3)[0]
    last_columns = last_columns.reshape(latents, -1)
    for total_sum in sums.values():
        while total_sum.far is None:
            last_sent = total_sum.step()[0]
    for (name, layer, i), total_sum in sums.items():
        reduced.setdefault((name, layer), []).append(total_sum.finish())
    reduced = {key: jnp.concatenate(parts, axis=1) for key, parts in reduced.items()}
    for layer in range(LAYERS):
        reduced["qkv", layer] = heads_together(reduced["qkv", layer])
    grad_stream = hold(grad_stream, sums["qkv", 0, 0].far[0])
    grad_embedded = grad_stream.astype(BF16)
    grad_patch_in = contract(noisy.reshape(-1, CH), grad_embedded, "tc,td->cd")
    grad_patch_bias = jnp.sum(grad_embedded.astype(F32), axis=0)

    last_columns = jnp.pad(last_columns, ((0, 0), (0, modulate_weight.shape[1] * tp_count - last_columns.shape[1])))
    grad_columns = known_columns + lax.dynamic_slice_in_dim(
        last_columns, tp_rank * modulate_weight.shape[1], modulate_weight.shape[1], axis=1
    )
    grad_ada = contract(act_own, grad_columns, "gd,ge->de")
    act_part = contract(grad_columns, low_modulate, "ge,de->gd").reshape(-1, own, low_modulate.shape[0])
    act_part = jnp.pad(act_part, ((0, 0), (0, -own % 8), (0, -act_part.shape[2] % LANES)))
    act_part = push([act_part], [1], 4)[0][:, :own, : low_modulate.shape[0]]
    act_part = jnp.sum(act_part.reshape(fsdp_count, tp_count, own, -1), axis=1).swapaxes(0, 1).reshape(own, -1)

    def of_own(value):
        return lax.dynamic_slice_in_dim(value, rank * own, own)

    cond_mine = (
        contract(of_own(step_hidden), cond_matrix[:, :depth], "gd,ed->ge")
        + step_out_bias
        + contract(of_own(onehot).astype(BF16), cond_matrix[:, depth:], "gc,dc->gd")
    )
    grad_cond = local_back(jax.nn.silu, cond_mine, act_part)
    grad_hidden = exact_dot(grad_cond, cond_matrix[:, :depth].astype(F32))
    grad_step_pre = local_back(jax.nn.silu, of_own(step_pre), grad_hidden)
    both_grads = jnp.concatenate([grad_cond, grad_step_pre], axis=0).reshape(2 * own, -1, columns)
    both_grads = jnp.pad(
        both_grads.swapaxes(0, 1), ((0, 0), (0, -2 * own % 8), (0, -columns % LANES))
    )

    pieces_bias = [
        jnp.sum(mod_known.astype(F32), axis=0)
        + jnp.pad(jnp.sum(mod_last.astype(F32), axis=0), (0, mod_known.shape[1] - mod_last.shape[1]))
    ]
    for layer in range(LAYERS):
        pieces_bias += layer_bias_grads[layer]
    pieces_bias += [jnp.zeros((2 * depth,), F32), grad_patch_bias]
    chunk = bias_vector.shape[0]
    small = jnp.concatenate(
        [
            jnp.concatenate(pieces_bias).reshape(-1, chunk),
            jnp.concatenate([grad_patch_in, grad_patch_out])
            .reshape(2 * CH, -1, columns)
            .swapaxes(0, 1)
            .reshape(-1, 2 * CH * columns),
        ],
        axis=1,
    )
    width = small.shape[1]
    small = jnp.pad(small, ((0, 0), (0, -width % (8 * LANES)))).reshape(small.shape[0], -1, LANES)
    small, both_grads = push([hold(small, sums["qkv", 0, 0].far[0]), both_grads], [1, 1], 1)
    small = jnp.sum(small, axis=0).reshape(-1)[:width]
    grad_cond = both_grads[:, :own, :columns].reshape(latents, columns)
    grad_step_pre = both_grads[:, own : 2 * own, :columns].reshape(latents, columns)
    grad_table = exact_dot(onehot.T, grad_cond)
    grad_step_out = exact_dot(step_hidden.astype(F32).T, grad_cond)
    grad_step_in = exact_dot(features.astype(F32).T, grad_step_pre)
    step_bias_grads = jnp.concatenate([jnp.sum(grad_step_pre, axis=0), jnp.sum(grad_cond, axis=0)])
    bias_grad = small[:chunk]
    patch_grads = small[chunk:].reshape(2 * CH, columns)
    embed_grad = jnp.concatenate(
        [grad_step_in, grad_step_out, patch_grads[:CH], grad_table, patch_grads[CH:]], axis=0
    )
    grads = (
        jnp.stack([reduced["qkv", i] for i in range(LAYERS)]),
        jnp.stack([reduced["out", i].T for i in range(LAYERS)]),
        jnp.stack([reduced["expand", i] for i in range(LAYERS)]),
        jnp.stack([reduced["reduce", i].T for i in range(LAYERS)]),
        grad_ada,
        embed_grad,
        bias_grad,
    )
    square = jnp.zeros((), jnp.float32)
    for grad in grads:
        square = square + jnp.sum(grad * grad)
    square = square + jnp.sum(step_bias_grads * step_bias_grads)
    last = push([padded(jnp.concatenate([square[None], loss_local[None], step_bias_grads]))], [0], 2)[0]
    last = last.reshape(last.shape[0], -1)
    square, loss_total = jnp.sum(last[:, 0]), jnp.sum(last[:, 1])
    step_biases = [last[:, 2 : 2 + columns].reshape(-1), last[:, 2 + columns : 2 + 2 * columns].reshape(-1)]
    before = jnp.zeros((bias.shape[0] - 3 * depth,), F32)
    step_biases = jnp.concatenate([before] + step_biases + [jnp.zeros((depth,), F32)])
    bias_grad = bias_grad + lax.dynamic_slice_in_dim(step_biases, rank * chunk, chunk)
    grads = grads[:-1] + (bias_grad,)
    grad_norm = jnp.sqrt(square)
    factor = CLIP_AT / jnp.maximum(grad_norm, CLIP_AT)
    params = (
        qkv_weight,
        out_weight,
        expand_weight,
        reduce_weight,
        modulate_weight,
        embed_weight,
        bias_vector,
    )
    firsts = (
        qkv_first,
        out_first,
        expand_first,
        reduce_first,
        modulate_first,
        embed_first,
        bias_first,
    )
    seconds = (
        qkv_second,
        out_second,
        expand_second,
        reduce_second,
        modulate_second,
        embed_second,
        bias_second,
    )
    news = [adam(w, f, s, g, factor) for w, f, s, g in zip(params, firsts, seconds, grads)]
    qkv_moment, qkv_square, qkv_master = news[0]
    out_moment, out_square, out_master = news[1]
    expand_moment, expand_square, expand_master = news[2]
    reduce_moment, reduce_square, reduce_master = news[3]
    modulate_moment, modulate_square, modulate_master = news[4]
    embed_moment, embed_square, embed_master = news[5]
    bias_moment, bias_square, bias_master = news[6]
    return (
        loss_total,
        grad_norm,
        qkv_moment,
        qkv_square,
        qkv_master,
        out_moment,
        out_square,
        out_master,
        expand_moment,
        expand_square,
        expand_master,
        reduce_moment,
        reduce_square,
        reduce_master,
        modulate_moment,
        modulate_square,
        modulate_master,
        embed_moment,
        embed_square,
        embed_master,
        bias_moment,
        bias_square,
        bias_master,
        qkv_master.astype(jnp.bfloat16),
        out_master.astype(jnp.bfloat16),
        expand_master.astype(jnp.bfloat16),
        reduce_master.astype(jnp.bfloat16),
        modulate_master.astype(jnp.bfloat16),
        embed_master.astype(jnp.bfloat16),
    )


def solution(mesh):
    return jax.shard_map(
        per_device,
        mesh=mesh,
        in_specs=(
            P((FSDP, TP), None, None),
            P((FSDP, TP), None, None),
            P(FSDP),
            P(FSDP),
            P(None, FSDP, TP),
            P(None, TP, FSDP),
            P(None, FSDP, TP),
            P(None, TP, FSDP),
            P(FSDP, TP),
            P(None, (FSDP, TP)),
            P((FSDP, TP)),
            P(None, FSDP, TP),
            P(None, TP, FSDP),
            P(None, FSDP, TP),
            P(None, TP, FSDP),
            P(FSDP, TP),
            P(None, (FSDP, TP)),
            P((FSDP, TP)),
            P(None, FSDP, TP),
            P(None, TP, FSDP),
            P(None, FSDP, TP),
            P(None, TP, FSDP),
            P(FSDP, TP),
            P(None, (FSDP, TP)),
            P((FSDP, TP)),
        ),
        out_specs=(
            P(),
            P(),
            P(None, FSDP, TP),
            P(None, FSDP, TP),
            P(None, FSDP, TP),
            P(None, TP, FSDP),
            P(None, TP, FSDP),
            P(None, TP, FSDP),
            P(None, FSDP, TP),
            P(None, FSDP, TP),
            P(None, FSDP, TP),
            P(None, TP, FSDP),
            P(None, TP, FSDP),
            P(None, TP, FSDP),
            P(FSDP, TP),
            P(FSDP, TP),
            P(FSDP, TP),
            P(None, (FSDP, TP)),
            P(None, (FSDP, TP)),
            P(None, (FSDP, TP)),
            P((FSDP, TP)),
            P((FSDP, TP)),
            P((FSDP, TP)),
            P(None, FSDP, TP),
            P(None, TP, FSDP),
            P(None, FSDP, TP),
            P(None, TP, FSDP),
            P(FSDP, TP),
            P(None, (FSDP, TP)),
        ),
        check_vma=False,
    )
```

time: 5380 us -> 1380 us (0.26)
  waiting for transfers between devices: 3840 us -> 186 us
  Pallas kernels: 0 us -> 883 us
  matrix products: 901 us -> 32.6 us
  other arithmetic: 344 us -> 115 us
  local copies, waits for them, and re-layouts: 198 us -> 56.8 us
  starting transfers between devices: 18.5 us -> 81.7 us
    reduce_scatter x19 -> x0, waiting for transfers between devices: 1880 us -> none  [the longest x8 786 us: collect(): return lax.psum_scatter(partial_sum, 'tp', scatter_dimension=0, tiled=True)]
    all_gather x26 -> x4, waiting for transfers between devices: 1300 us -> 35.7 us  [the longest x2 35.7 us: gather(): whole = lax.all_gather(packed, (TP, FSDP), axis=0, tiled=True)]
    pallas_call x0 -> x31, Pallas kernels: none -> 883 us  [the longest x13 551 us: call_part(): pl.pallas_call(body, grid=(count,), in_specs=[spec(kind, dims_of(kind, ar...]
    dot_general x94 -> x10, matrix products: 888 us -> 26.3 us  [contract(): return jnp.einsum(form, left, right, preferred_element_type=jnp.float32)]
    unnamed x53 -> x4, waiting for transfers between devices: 654 us -> 0.07 us
    reduce_sum x48 -> x9, other arithmetic: 175 us -> 8.79 us  [the longest x1 3.95 us: per_device(): grad_patch_bias = jnp.sum(grad_embedded.astype(F32), axis=0)]
    ppermute x0 -> x65, waiting for transfers between devices: none -> 150 us  [swap(): lax.ppermute(value, name, [(i, i ^ bits) for i in range(lax.axis_size(nam...]
    unnamed x684 -> x279, local copies, waits for them, and re-layouts: 97.9 us -> 13.6 us
  transfers between devices with their start and end apart: 53 -> 69, of which waited for: 47 -> 26; matrix products, arithmetic and copies ran while one was open for 11% -> 12% of each run, Pallas kernels for 0% -> 47%
where the time goes in v1:
time: 1380 us
  Pallas kernels  883 us (64%)
  waiting for transfers between devices  186 us (13%)
  other arithmetic  115 us (8%)
  starting transfers between devices  81.7 us (6%)
  local copies, waits for them, and re-layouts  56.8 us (4%)
  matrix products  32.6 us (2%)
  between operations  23.5 us (2%)
    pallas_call x13, Pallas kernels, call_part(): pl.pallas_call(body, grid=(count,), in_specs=[spec(kind, dims_of(kind, ar...  551 us
    pallas_call x8, Pallas kernels, start_sums(): pl.pallas_call(body, grid_spec=pltpu.PrefetchScalarGridSpec(num_scalar_pr...  162 us
    ppermute x65, waiting for transfers between devices, swap(): lax.ppermute(value, name, [(i, i ^ bits) for i in range(lax.axis_size(nam...  150 us
    pallas_call x1, Pallas kernels, run_head(): pl.pallas_call(head_kernel, in_specs=[vmem] * 3 + [ANY] * 2, out_specs=[v...  113 us
    ppermute x65, starting transfers between devices, swap(): lax.ppermute(value, name, [(i, i ^ bits) for i in range(lax.axis_size(nam...  81 us
    pallas_call x4, Pallas kernels, push(): pl.pallas_call(functools.partial(push_kernel, plans, len(arrays)), in_spe...  56.8 us
    convert_element_type x20, other arithmetic, step(): part(axis, 0).astype(BF16)  36.7 us
    all_gather x2, waiting for transfers between devices, gather(): whole = lax.all_gather(packed, (TP, FSDP), axis=0, tiled=True)  35.7 us
  transfers between devices with their start and end apart: 69, of which 26 were waited for; matrix products, arithmetic and copies ran while one was open for 12% of the time, Pallas kernels for 47%

profile of v1, /device:TPU:0, one launch (start us, length us, event | category | flops | bytes accessed | tf_op | source)
XLA Modules:
  0.0 1378.0 jit_solution(2554594300423338529)
XLA Ops:
  19.2 112.6 %shard_map.473 = (f32[32,16,128]{2,1,0:T(8,128)}, bf16[32,64,128]{2,1,0:T(8,128)(2,1)}, bf16[8,272,128]{2,1,0:T(8,128)(2,1)}, bf16[4,64,7168]{2,1,0:T(8,128)(2,1)}, bf16[2,1024,2048]{2,1,0:T(8,128)(2,1)}) custom-call(f32[16,128]{1,0:T(8,128)} %pad_bitcast_fusion.packed, bf16[64,128]{1,0:T(8,128)(2,1)} %reshape.840.step_in, bf16[272,128]{1,0:T(8,128)(2,1)} %pad.33.cond, ...), custom_call_target="tpu_custom_call" | custom-call | flops 40000000000 | bytes 100000000 | tf_op jit(solution)/shard_map/pallas_call | solution.py:405
  164.2 11.8 collective-permute-done
  195.7 57.2 %shard_map.474 = (bf16[2048,1024]{1,0:T(8,128)(2,1)}, bf16[2048,3072]{1,0:T(8,128)(2,1)}, f32[8,16,256]{2,1,0:T(8,128)}, bf16[2048,1024]{1,0:T(8,128)(2,1)}, bf1...) custom-call(f32[2048,1024]{1,0:T(8,128)} %bitcast.528, ...), custom_call_target="tpu_custom_call" | custom-call | flops 42949672960 | bytes 50331648 | tf_op jit(solution)/shard_map/pallas_call | solution.py:792
  252.9 55.7 %shard_map.475 = (f32[2048,4096]{1,0:T(8,128)}, bf16[2048,4096]{1,0:T(8,128)(2,1)}, bf16[2048,1024]{1,0:T(8,128)(2,1)}, f32[2048,1024]{1,0:T(8,128)}) custom-call(bf16[2048,1024]{1,0:T(8,128)(2,1)} %get-tuple-element.134.refs_0_.left, f32[2048,1024]{1,0:T(8,128)} %get-tuple-element.135.refs_1_.refs_3_, ...), custom_call_target="tpu_custom_call" | custom-call | flops 51539607552 | bytes 50331648 | tf_op jit(solution)/shard_map/pallas_call | solution.py:792
  308.6 35.7 %all-gather.7.cloned.1.call-done = bf16[2048,6144]{1,0:T(8,128)(2,1)} async-done(((bf16[64,6144]{1,0:T(8,128)(2,1)}), bf16[2048,6144]{1,0:T(8,128)(2,1)}) %all-gather.7.cloned.1.call-update) | async-done | bytes 25165840 | tf_op jit(solution)/shard_map/all_gather | solution.py:1107
  344.3 56.5 %shard_map.477 = (bf16[2048,1024]{1,0:T(8,128)(2,1)}, bf16[2048,3072]{1,0:T(8,128)(2,1)}, f32[8,16,256]{2,1,0:T(8,128)}, bf16[2048,1024]{1,0:T(8,128)(2,1)}, bf1...) custom-call(f32[2048,1024]{1,0:T(8,128)} %get-tuple-element.136.refs_0_.refs_3_, ...), custom_call_target="tpu_custom_call" | custom-call | flops 42949672960 | bytes 50331648 | tf_op jit(solution)/shard_map/pallas_call | solution.py:792
  400.8 55.7 %shard_map.478 = (f32[2048,4096]{1,0:T(8,128)}, bf16[2048,4096]{1,0:T(8,128)(2,1)}, bf16[2048,1024]{1,0:T(8,128)(2,1)}, f32[2048,1024]{1,0:T(8,128)}) custom-call(bf16[2048,1024]{1,0:T(8,128)(2,1)} %get-tuple-element.137.refs_0_.left.refs_1_, f32[2048,1024]{1,0:T(8,128)} %get-tuple-element.138.refs_1_.refs_3_, ...), custom_call_target="tpu_custom_call" | custom-call | flops 51539607552 | bytes 50331648 | tf_op jit(solution)/shard_map/pallas_call | solution.py:792
  456.5 14.0 %shard_map.479 = (f32[2048,1024]{1,0:T(8,128)}, f32[8,2,1024]{2,1,0:T(2,128)}, f32[16,1024]{1,0:T(8,128)}, f32[1,16]{1,0:T(1,128)}) custom-call(f32[2048,1024]{1,0:T(8,128)} %get-tuple-element.139.refs_0_, f32[8,2,1024]{2,1,0:T(2,128)} %slice.1019.refs_1_, f32[8,256,16]{2,1,0:T(8,128)} %copy.222.refs_2_, bf16[16,1024]{1,0:T(8,128)(2,1)} %convert_element_type.1419.refs_3_), custom_call_target="tpu_custom_call" | custom-call | flops 1610612736 | bytes 16777216 | tf_op jit(solution)/shard_map/pallas_call | solution.py:792
  470.5 41.7 %shard_map.480 = (bf16[2048,1024]{1,0:T(8,128)(2,1)}, bf16[2048,4096]{1,0:T(8,128)(2,1)}, f32[2048,1024]{1,0:T(8,128)}, bf16[2048,1024]{1,0:T(8,128)(2,1)}, f32[...) custom-call(f32[2048,1024]{1,0:T(8,128)} %get-tuple-element.140.refs_0_, ...), custom_call_target="tpu_custom_call" | custom-call | flops 25769803776 | bytes 25165824 | tf_op jit(solution)/shard_map/pallas_call | solution.py:792
  512.1 41.9 %shard_map.481 = (bf16[2048,1024]{1,0:T(8,128)(2,1)}, bf16[2048,4096]{1,0:T(8,128)(2,1)}, f32[2048,1024]{1,0:T(8,128)}, bf16[2048,1024]{1,0:T(8,128)(2,1)}, f32[...) custom-call(f32[2048,1024]{1,0:T(8,128)} %get-tuple-element.140.refs, ...), custom_call_target="tpu_custom_call", output_to_operand_aliasing={{0}: (10, {}), {1}: (11, {}), {2}: (12, {}), {3}: (13, {}),... | custom-call | flops 25769803776 | bytes 25165824 | tf_op jit(solution)/shard_map/pallas_call | solution.py:792
  564.6 24.7 %shard_map.483 = (bf16[2,512,2048]{2,1,0:T(8,128)(2,1)}, bf16[2,512,2048]{2,1,0:T(8,128)(2,1)}) custom-call(s32[2]{0:T(128)} %pad_add_fusion.place, bf16[2048,1024]{1,0:T(8,128)(2,1)} %get-tuple-element.137.refs_0_.left.refs_1_, bf16[2048,4096]{1,0:T(8,128)(2,1)} %get-tuple-element.157.right), custom_call_target="tpu_custom_call" | custom-call | flops 21474836480 | bytes 20971520 | tf_op jit(solution)/shard_map/pallas_call | solution.py:982
  589.6 25.1 %shard_map.482 = (bf16[2,512,2048]{2,1,0:T(8,128)(2,1)}, bf16[2,512,2048]{2,1,0:T(8,128)(2,1)}) custom-call(s32[2]{0:T(128)} %pad_add_fusion.place, bf16[2048,1024]{1,0:T(8,128)(2,1)} %get-tuple-element.153.left, bf16[2048,4096]{1,0:T(8,128)(2,1)} %get-tuple-element.154.right), custom_call_target="tpu_custom_call" | custom-call | flops 21474836480 | bytes 20971520 | tf_op jit(solution)/shard_map/pallas_call | solution.py:982
  616.9 12.7 collective-permute-done.11
  631.1 10.5 collective-permute-done.12
  668.6 35.9 %shard_map.484 = (bf16[2048,3072]{1,0:T(8,128)(2,1)}, f32[2048,1024]{1,0:T(8,128)}, f32[8,2,1024]{2,1,0:T(2,128)}) custom-call(bf16[2048,1024]{1,0:T(8,128)(2,1)} %get-tuple-element.149.refs_0_.left, bf16[2048,3072]{1,0:T(8,128)(2,1)} %get-tuple-element.150.refs_1_, f32[8,16,256]{2,1,0:T(8,128)} %get-tuple-element.151.refs_2_, ...), custom_call_target="tpu_custom_call" | custom-call | flops 25769803776 | bytes 25165824 | tf_op jit(solution)/shard_map/pallas_call | solution.py:792
  704.6 36.3 %shard_map.486 = (bf16[2048,3072]{1,0:T(8,128)(2,1)}, f32[2048,1024]{1,0:T(8,128)}, f32[8,2,1024]{2,1,0:T(2,128)}) custom-call(bf16[2048,1024]{1,0:T(8,128)(2,1)} %get-tuple-element.149.refs_0_.left, bf16[2048,3072]{1,0:T(8,128)(2,1)} %get-tuple-element.150.refs_1_, ...), custom_call_target="tpu_custom_call", output_to_operand_aliasing={{0}: (7, {}), {1}: (8, {}), {2}: (9, {})} | custom-call | flops 25769803776 | bytes 25165824 | tf_op jit(solution)/shard_map/pallas_call | solution.py:792
  749.5 20.8 %shard_map.488 = (bf16[2,512,768]{2,1,0:T(8,128)(2,1)}, bf16[2,512,768]{2,1,0:T(8,128)(2,1)}, bf16[2,512,768]{2,1,0:T(8,128)(2,1)}, bf16[2,512,768]{2,1,0:T(8,128)(2,1)}) custom-call(s32[2]{0:T(128)} %pad_add_fusion.place, bf16[2048,1024]{1,0:T(8,128)(2,1)} %get-tuple-element.175.left, bf16[2048,3072]{1,0:T(8,128)(2,1)} %get-tuple-element.176.right, ...), custom_call_target="tpu_custom_call" | custom-call | flops 16106127360 | bytes 16777216 | tf_op jit(solution)/shard_map/pallas_call | solution.py:982
  779.9 41.8 %shard_map.487 = (bf16[2048,1024]{1,0:T(8,128)(2,1)}, bf16[2048,4096]{1,0:T(8,128)(2,1)}, f32[2048,1024]{1,0:T(8,128)}, bf16[2048,1024]{1,0:T(8,128)(2,1)}, f32[...) custom-call(f32[2048,1024]{1,0:T(8,128)} %get-tuple-element.166.refs_0_, ...), custom_call_target="tpu_custom_call" | custom-call | flops 25769803776 | bytes 25165824 | tf_op jit(solution)/shard_map/pallas_call | solution.py:792
  848.7 42.2 %shard_map.489 = (bf16[2048,1024]{1,0:T(8,128)(2,1)}, bf16[2048,4096]{1,0:T(8,128)(2,1)}, f32[2048,1024]{1,0:T(8,128)}, bf16[2048,1024]{1,0:T(8,128)(2,1)}, f32[...) custom-call(f32[2048,1024]{1,0:T(8,128)} %get-tuple-element.166.refs, ...), custom_call_target="tpu_custom_call", output_to_operand_aliasing={{0}: (10, {}), {1}: (11, {}), {2}: (12, {}), {3}: (13, {}),... | custom-call | flops 25769803776 | bytes 25165824 | tf_op jit(solution)/shard_map/pallas_call | solution.py:792
  897.5 13.2 collective-permute-done.17
  914.7 24.9 %shard_map.490 = (bf16[2,512,2048]{2,1,0:T(8,128)(2,1)}, bf16[2,512,2048]{2,1,0:T(8,128)(2,1)}) custom-call(s32[2]{0:T(128)} %pad_add_fusion.place, bf16[2048,1024]{1,0:T(8,128)(2,1)} %get-tuple-element.185.left, bf16[2048,4096]{1,0:T(8,128)(2,1)} %get-tuple-element.186.right), custom_call_target="tpu_custom_call" | custom-call | flops 21474836480 | bytes 20971520 | tf_op jit(solution)/shard_map/pallas_call | solution.py:982
  942.2 10.4 shard_map.493
  953.1 24.9 %shard_map.491 = (bf16[2,512,2048]{2,1,0:T(8,128)(2,1)}, bf16[2,512,2048]{2,1,0:T(8,128)(2,1)}) custom-call(s32[2]{0:T(128)} %pad_add_fusion.place, bf16[2048,1024]{1,0:T(8,128)(2,1)} %get-tuple-element.134.refs_0_.left, bf16[2048,4096]{1,0:T(8,128)(2,1)} %get-tuple-element.189.right, bf16[2,2,64,768]{3,2,1,0:T(8,128)(2,1)} %copy-done.60, ...), custom_call_target="tpu_custom_call" | custom-call | flops 21474836480 | bytes 20971520 | tf_op jit(solution)/shard_map/pallas_call | solution.py:982
  1042.5 36.1 %shard_map.492 = (bf16[2048,3072]{1,0:T(8,128)(2,1)}, f32[2048,1024]{1,0:T(8,128)}, f32[8,2,1024]{2,1,0:T(2,128)}) custom-call(bf16[2048,1024]{1,0:T(8,128)(2,1)} %get-tuple-element.181.refs_0_.left, bf16[2048,3072]{1,0:T(8,128)(2,1)} %get-tuple-element.182.refs_1_, f32[8,16,256]{2,1,0:T(8,128)} %get-tuple-element.183.refs_2_, f32[2048,1024]{1,0:T(8,128)} %bitcast.529, ...), custom_call_target="tpu_custom_call" | custom-call | flops 25769803776 | bytes 25165824 | tf_op jit(solution)/shard_map/pallas_call | solution.py:792
  1094.7 15.2 %collective-permute-done.24 = bf16[2,2,64,2048]{3,2,1,0:T(8,128)(2,1)S(1)} collective-permute-done((bf16[2,2,64,2048]{3,2,1,0:T(8,128)(2,1)S(1)}, bf16[2,2,64,2048]{3,2,1,0:T(8,128)(2,1)S(1)}, u32[]{:S(2)}, u32[]{:S(2)}) %collective-permute-start.24) | collective-permute-done | bytes 1048608 | tf_op jit(solution)/shard_map/ppermute | solution.py:120
  1119.7 36.2 %shard_map.494 = (bf16[2048,3072]{1,0:T(8,128)(2,1)}, f32[2048,1024]{1,0:T(8,128)}, f32[8,2,1024]{2,1,0:T(2,128)}) custom-call(bf16[2048,1024]{1,0:T(8,128)(2,1)} %get-tuple-element.181.refs_0_.left, bf16[2048,3072]{1,0:T(8,128)(2,1)} %get-tuple-element.182.refs_1_, ...), custom_call_target="tpu_custom_call", output_to_operand_aliasing={{0}: (7, {}), {1}: (8, {}), {2}: (9, {})} | custom-call | flops 25769803776 | bytes 25165824 | tf_op jit(solution)/shard_map/pallas_call | solution.py:792
  1164.5 21.0 %shard_map.495 = (bf16[2,512,768]{2,1,0:T(8,128)(2,1)}, bf16[2,512,768]{2,1,0:T(8,128)(2,1)}, bf16[2,512,768]{2,1,0:T(8,128)(2,1)}, bf16[2,512,768]{2,1,0:T(8,128)(2,1)}) custom-call(s32[2]{0:T(128)} %pad_add_fusion.place, bf16[2048,1024]{1,0:T(8,128)(2,1)} %get-tuple-element.133.left, bf16[2048,3072]{1,0:T(8,128)(2,1)} %get-tuple-element.198.right, ...), custom_call_target="tpu_custom_call" | custom-call | flops 16106127360 | bytes 16777216 | tf_op jit(solution)/shard_map/pallas_call | solution.py:982
  1187.1 18.5 %shard_map.497 = bf16[32,128,128]{2,1,0:T(8,128)(2,1)} custom-call(bf16[128,128]{1,0:T(8,128)(2,1)} %convert_element_type.1757.refs_0_), custom_call_target="tpu_custom_call" | custom-call | flops 5000000000 | bytes 50000000 | tf_op jit(solution)/shard_map/pallas_call | solution.py:258
  1211.6 10.9 shard_map.500
  1242.9 13.8 %collective-permute-done.28 = bf16[2,2,2,64,768]{4,3,2,1,0:T(8,128)(2,1)S(1)} collective-permute-done((bf16[2,2,2,64,768]{4,3,2,1,0:T(8,128)(2,1)S(1)}, bf16[2,2,2,64,768]{4,3,2,1,0:T(8,128)(2,1)S(1)}, u32[]{:S(2)}, u32[]{:S(2)}) %collective-permute-start.28) | collective-permute-done | bytes 786464 | tf_op jit(solution)/shard_map/ppermute | solution.py:120
  1281.3 16.2 %shard_map.502 = (f32[32,16,128]{2,1,0:T(8,128)}, f32[32,16,128]{2,1,0:T(8,128)}) custom-call(f32[32,16,128]{2,1,0:T(8,128)} %shard_map.499.refs_0_, f32[32,16,128]{2,1,0:T(8,128)} %pad.38.refs_1_), custom_call_target="tpu_custom_call" | custom-call | flops 5000000000 | bytes 50000000 | tf_op jit(solution)/shard_map/pallas_call | solution.py:258
  1337.5 11.2 shard_map.503
  (660 shorter events, 369.3 us)
Async XLA Ops:
  7.2 245.6 %all-gather.5.cloned.1.call-start = ((), (), s32[]{:S(2)}) async-start(), calls=%async_computation | async-start | bytes 17301504 | tf_op jit(solution)/shard_map/all_gather | solution.py:1107
  9.7 334.6 %all-gather.7.cloned.1.call-start = ((), (), s32[]{:S(2)}) async-start(), calls=%async_computation.1 | async-start | bytes 25952256 | tf_op jit(solution)/shard_map/all_gather | solution.py:1107
  131.9 519.4 %all-gather.11.cloned.1.call-start = ((), (), s32[]{:S(2)}) async-start(), calls=%async_computation.3 | async-start | bytes 2433024 | tf_op jit(solution)/shard_map/all_gather | solution.py:1180
  564.3 50.7 %collective-permute-start.6 = (bf16[2,512,512]{2,1,0:T(8,128)(2,1)}, bf16[2,512,512]{2,1,0:T(8,128)(2,1)S(1)}, u32[]{:S(2)}, u32[]{:S(2)}) collective-permute-start(bf16[2,512,512]{2,1,0:T(8,128)(2,1)} %get-tuple-element.165), channel_id=1, source_target_pairs={{0,2},{2,0},{4,6},{6,4},{8,10},{10,8},{12,14},{14,12},{16,18},{18,... | collective-permute-start | bytes 3145736 | tf_op jit(solution)/shard_map/ppermute | solution.py:120
  589.3 63.8 %collective-permute-start.5 = (bf16[2,512,2048]{2,1,0:T(8,128)(2,1)}, bf16[2,512,2048]{2,1,0:T(8,128)(2,1)}, u32[]{:S(2)}, u32[]{:S(2)}) collective-permute-start(bf16[2,512,2048]{2,1,0:T(8,128)(2,1)} %get-tuple-element.159), channel_id=1, source_target_pairs={{0,2},{2,0},{4,6},{6,4},{8,10},{10,8},{12,14},{14,12},{16,18},{18,... | collective-permute-start | bytes 12582920 | tf_op jit(solution)/shard_map/ppermute | solution.py:120
  589.6 617.6 %all-gather.9.cloned.1.call-start = ((), (), s32[]{:S(2)}) async-start(), calls=%async_computation.2 | async-start | bytes 3899392 | tf_op jit(solution)/shard_map/all_gather | solution.py:1240
  614.7 46.6 %collective-permute-start.4 = (bf16[2,512,2048]{2,1,0:T(8,128)(2,1)}, bf16[2,512,2048]{2,1,0:T(8,128)(2,1)}, u32[]{:S(2)}, u32[]{:S(2)}) collective-permute-start(bf16[2,512,2048]{2,1,0:T(8,128)(2,1)} %get-tuple-element.156), channel_id=1, source_target_pairs={{0,2},{2,0},{4,6},{6,4},{8,10},{10,8},{12,14},{14,12},{16,18},{18,... | collective-permute-start | bytes 12582920 | tf_op jit(solution)/shard_map/ppermute | solution.py:120
  657.7 83.2 %collective-permute-start.9 = (bf16[2,2,2,64,2048]{4,3,2,1,0:T(8,128)(2,1)}, bf16[2,2,2,64,2048]{4,3,2,1,0:T(8,128)(2,1)}, u32[]{:S(2)}, u32[]{:S(2)}) collective-permute-start(bf16[2,2,2,64,2048]{4,3,2,1,0:T(8,128)(2,1)} %fusion.1.refs_8_), channel_id=1, source_target_pairs={{0,4},{2,6},{4,0},{6,2},{8,12},{10,14},{12,8},{14,10},{16,20},{18,... | collective-permute-start | bytes 6291464 | tf_op jit(solution)/shard_map/ppermute | solution.py:120
  667.4 77.9 %collective-permute-start.7 = (bf16[2,2,2,64,2048]{4,3,1,0,2:T(8,128)(2,1)}, bf16[2,2,2,64,2048]{4,3,1,0,2:T(8,128)(2,1)}, u32[]{:S(2)}, u32[]{:S(2)}) collective-permute-start(bf16[2,2,2,64,2048]{4,3,1,0,2:T(8,128)(2,1)} %copy.226), channel_id=1, source_target_pairs={{0,1},{1,0},{2,3},{3,2},{4,5},{5,4},{6,7},{7,6},{8,9},{9,8},{10,11... | collective-permute-start | bytes 6291464 | tf_op jit(solution)/shard_map/ppermute | solution.py:120
  744.5 32.7 %collective-permute-start.10 = (bf16[2,2,64,2048]{3,2,1,0:T(8,128)(2,1)}, bf16[2,2,64,2048]{3,2,1,0:T(8,128)(2,1)S(1)}, u32[]{:S(2)}, u32[]{:S(2)}) collective-permute-start(bf16[2,2,64,2048]{3,2,1,0:T(8,128)(2,1)} %get-tuple-element.280.rest_1_), channel_id=1, source_target_pairs={{0,1},{1,0},{2,3},{3,2},{4,5},{5,4},{6,7},{7,6},{8,9},{9,8},{10,11... | collective-permute-start | bytes 3145736 | tf_op jit(solution)/shard_map/ppermute | solution.py:120
  770.3 73.6 %collective-permute-start.14 = (bf16[2,512,768]{2,1,0:T(8,128)(2,1)}, bf16[2,512,768]{2,1,0:T(8,128)(2,1)}, u32[]{:S(2)}, u32[]{:S(2)}) collective-permute-start(bf16[2,512,768]{2,1,0:T(8,128)(2,1)} %get-tuple-element.180), channel_id=1, source_target_pairs={{0,2},{2,0},{4,6},{6,4},{8,10},{10,8},{12,14},{14,12},{16,18},{18,... | collective-permute-start | bytes 4718600 | tf_op jit(solution)/shard_map/ppermute | solution.py:120
  770.3 75.6 %collective-permute-start.13 = (bf16[2,512,768]{2,1,0:T(8,128)(2,1)}, bf16[2,512,768]{2,1,0:T(8,128)(2,1)}, u32[]{:S(2)}, u32[]{:S(2)}) collective-permute-start(bf16[2,512,768]{2,1,0:T(8,128)(2,1)} %get-tuple-element.178), channel_id=1, source_target_pairs={{0,2},{2,0},{4,6},{6,4},{8,10},{10,8},{12,14},{14,12},{16,18},{18,... | collective-permute-start | bytes 4718600 | tf_op jit(solution)/shard_map/ppermute | solution.py:120
  774.6 47.1 %collective-permute-start.61 = (bf16[64,2048]{1,0:T(8,128)(2,1)}, bf16[64,2048]{1,0:T(8,128)(2,1)S(1)}, u32[]{:S(2)}, u32[]{:S(2)}) collective-permute-start(bf16[64,2048]{1,0:T(8,128)(2,1)} %get-tuple-element.302.refs_10_), channel_id=1, source_target_pairs={{0,8},{2,10},{4,12},{6,14},{8,0},{10,2},{12,4},{14,6},{16,24},{18,... | collective-permute-start | bytes 786440 | tf_op jit(solution)/shard_map/ppermute | solution.py:120
  776.2 46.3 %collective-permute-start.62 = (bf16[64,2048]{1,0:T(8,128)(2,1)}, bf16[64,2048]{1,0:T(8,128)(2,1)S(1)}, u32[]{:S(2)}, u32[]{:S(2)}) collective-permute-start(bf16[64,2048]{1,0:T(8,128)(2,1)} %get-tuple-element.301.refs_11_), channel_id=1, source_target_pairs={{0,16},{2,18},{4,20},{6,22},{8,24},{10,26},{12,28},{14,30},{16,0},... | collective-permute-start | bytes 786440 | tf_op jit(solution)/shard_map/ppermute | solution.py:120
  777.2 47.2 %collective-permute-start.63 = (bf16[64,2048]{1,0:T(8,128)(2,1)S(1)}, bf16[64,2048]{1,0:T(8,128)(2,1)}, u32[]{:S(2)}, u32[]{:S(2)}) collective-permute-start(bf16[64,2048]{1,0:T(8,128)(2,1)S(1)} %get-tuple-element.300.refs_12_), channel_id=1, source_target_pairs={{0,24},{2,26},{4,28},{6,30},{8,16},{10,18},{12,20},{14,22},{16,8},... | collective-permute-start | bytes 786440 | tf_op jit(solution)/shard_map/ppermute | solution.py:120
  847.5 64.1 %collective-permute-start.16 = (bf16[2,2,2,64,768]{4,3,2,1,0:T(8,128)(2,1)S(1)}, bf16[2,2,2,64,768]{4,3,2,1,0:T(8,128)(2,1)}, u32[]{:S(2)}, u32[]{:S(2)}) collective-permute-start(bf16[2,2,2,64,768]{4,3,2,1,0:T(8,128)(2,1)S(1)} %fusion.27.refs_15_), channel_id=1, source_target_pairs={{0,4},{2,6},{4,0},{6,2},{8,12},{10,14},{12,8},{14,10},{16,20},{18,... | collective-permute-start | bytes 2359304 | tf_op jit(solution)/shard_map/ppermute | solution.py:120
  895.0 83.0 %collective-permute-start.64 = (bf16[8,7168]{1,0:T(8,128)(2,1)}, bf16[8,7168]{1,0:T(8,128)(2,1)}, u32[]{:S(2)}, u32[]{:S(2)}) collective-permute-start(bf16[8,7168]{1,0:T(8,128)(2,1)} %get-tuple-element.347), channel_id=1, source_target_pairs={{0,1},{1,0},{2,3},{3,2},{4,5},{5,4},{6,7},{7,6},{8,9},{9,8},{10,11... | collective-permute-start | bytes 344072 | tf_op jit(solution)/shard_map/ppermute | solution.py:120
  910.9 29.6 %collective-permute-start.22 = (bf16[2,2,64,768]{3,2,1,0:T(8,128)(2,1)S(1)}, bf16[2,2,64,768]{3,2,1,0:T(8,128)(2,1)S(1)}, u32[]{:S(2)}, u32[]{:S(2)}) collective-permute-start(bf16[2,2,64,768]{3,2,1,0:T(8,128)(2,1)S(1)} %get-tuple-element.308.rest_1_), channel_id=1, source_target_pairs={{0,4},{2,6},{4,0},{6,2},{8,12},{10,14},{12,8},{14,10},{16,20},{18,... | collective-permute-start | bytes 1179656 | tf_op jit(solution)/shard_map/ppermute | solution.py:120
  939.6 91.0 %collective-permute-start.15 = (bf16[2,512,2048]{2,1,0:T(8,128)(2,1)}, bf16[2,512,2048]{2,1,0:T(8,128)(2,1)}, u32[]{:S(2)}, u32[]{:S(2)}) collective-permute-start(bf16[2,512,2048]{2,1,0:T(8,128)(2,1)} %get-tuple-element.188), channel_id=1, source_target_pairs={{0,2},{2,0},{4,6},{6,4},{8,10},{10,8},{12,14},{14,12},{16,18},{18,... | collective-permute-start | bytes 12582920 | tf_op jit(solution)/shard_map/ppermute | solution.py:120
  952.6 32.0 %collective-permute-start.23 = (bf16[2,512,512]{2,1,0:T(8,128)(2,1)}, bf16[2,512,512]{2,1,0:T(8,128)(2,1)S(1)}, u32[]{:S(2)}, u32[]{:S(2)}) collective-permute-start(bf16[2,512,512]{2,1,0:T(8,128)(2,1)} %get-tuple-element.197), channel_id=1, source_target_pairs={{0,2},{2,0},{4,6},{6,4},{8,10},{10,8},{12,14},{14,12},{16,18},{18,... | collective-permute-start | bytes 3145736 | tf_op jit(solution)/shard_map/ppermute | solution.py:120
  978.0 59.2 %collective-permute-start.18 = (bf16[2,512,2048]{2,1,0:T(8,128)(2,1)}, bf16[2,512,2048]{2,1,0:T(8,128)(2,1)}, u32[]{:S(2)}, u32[]{:S(2)}) collective-permute-start(bf16[2,512,2048]{2,1,0:T(8,128)(2,1)} %get-tuple-element.191), channel_id=1, source_target_pairs={{0,2},{2,0},{4,6},{6,4},{8,10},{10,8},{12,14},{14,12},{16,18},{18,... | collective-permute-start | bytes 12582920 | tf_op jit(solution)/shard_map/ppermute | solution.py:120
  1037.1 45.0 %collective-permute-start.19 = (bf16[2,2,2,64,2048]{4,3,1,0,2:T(8,128)(2,1)}, bf16[2,2,2,64,2048]{4,3,1,0,2:T(8,128)(2,1)}, u32[]{:S(2)}, u32[]{:S(2)}) collective-permute-start(bf16[2,2,2,64,2048]{4,3,1,0,2:T(8,128)(2,1)} %copy.242), channel_id=1, source_target_pairs={{0,1},{1,0},{2,3},{3,2},{4,5},{5,4},{6,7},{7,6},{8,9},{9,8},{10,11... | collective-permute-start | bytes 6291464 | tf_op jit(solution)/shard_map/ppermute | solution.py:120
  1042.5 48.9 %collective-permute-start.20 = (bf16[2,2,2,64,2048]{4,3,2,1,0:T(8,128)(2,1)}, bf16[2,2,2,64,2048]{4,3,2,1,0:T(8,128)(2,1)}, u32[]{:S(2)}, u32[]{:S(2)}) collective-permute-start(bf16[2,2,2,64,2048]{4,3,2,1,0:T(8,128)(2,1)} %fusion.2.refs_8_), channel_id=1, source_target_pairs={{0,4},{2,6},{4,0},{6,2},{8,12},{10,14},{12,8},{14,10},{16,20},{18,... | collective-permute-start | bytes 6291464 | tf_op jit(solution)/shard_map/ppermute | solution.py:120
  1094.7 64.2 %collective-permute-start.25 = (bf16[2,2,64,2048]{3,2,1,0:T(8,128)(2,1)}, bf16[2,2,64,2048]{3,2,1,0:T(8,128)(2,1)S(1)}, u32[]{:S(2)}, u32[]{:S(2)}) collective-permute-start(bf16[2,2,64,2048]{3,2,1,0:T(8,128)(2,1)} %get-tuple-element.276.refs_11_), channel_id=1, source_target_pairs={{0,1},{1,0},{2,3},{3,2},{4,5},{5,4},{6,7},{7,6},{8,9},{9,8},{10,11... | collective-permute-start | bytes 3145736 | tf_op jit(solution)/shard_map/ppermute | solution.py:120
  1110.9 45.0 %collective-permute-start.58 = (bf16[64,2048]{1,0:T(8,128)(2,1)S(1)}, bf16[64,2048]{1,0:T(8,128)(2,1)S(1)}, u32[]{:S(2)}, u32[]{:S(2)}) collective-permute-start(bf16[64,2048]{1,0:T(8,128)(2,1)S(1)} %get-tuple-element.294.rest_0_), channel_id=1, source_target_pairs={{0,8},{2,10},{4,12},{6,14},{8,0},{10,2},{12,4},{14,6},{16,24},{18,... | collective-permute-start | bytes 786440 | tf_op jit(solution)/shard_map/ppermute | solution.py:120
  1116.0 39.9 %collective-permute-start.59 = (bf16[64,2048]{1,0:T(8,128)(2,1)S(1)}, bf16[64,2048]{1,0:T(8,128)(2,1)}, u32[]{:S(2)}, u32[]{:S(2)}) collective-permute-start(bf16[64,2048]{1,0:T(8,128)(2,1)S(1)} %get-tuple-element.293.rest_1_), channel_id=1, source_target_pairs={{0,16},{2,18},{4,20},{6,22},{8,24},{10,26},{12,28},{14,30},{16,0},... | collective-permute-start | bytes 786440 | tf_op jit(solution)/shard_map/ppermute | solution.py:120
  1118.3 38.3 %collective-permute-start.60 = (bf16[64,2048]{1,0:T(8,128)(2,1)S(1)}, bf16[64,2048]{1,0:T(8,128)(2,1)}, u32[]{:S(2)}, u32[]{:S(2)}) collective-permute-start(bf16[64,2048]{1,0:T(8,128)(2,1)S(1)} %get-tuple-element.292.rest_2_), channel_id=1, source_target_pairs={{0,24},{2,26},{4,28},{6,30},{8,16},{10,18},{12,20},{14,22},{16,8},... | collective-permute-start | bytes 786440 | tf_op jit(solution)/shard_map/ppermute | solution.py:120
  1160.1 97.2 %collective-permute-start.52 = (bf16[64,2048]{1,0:T(8,128)(2,1)}, bf16[64,2048]{1,0:T(8,128)(2,1)}, u32[]{:S(2)}, u32[]{:S(2)}) collective-permute-start(bf16[64,2048]{1,0:T(8,128)(2,1)} %get-tuple-element.291.rest_3_), channel_id=1, source_target_pairs={{0,8},{2,10},{4,12},{6,14},{8,0},{10,2},{12,4},{14,6},{16,24},{18,... | collective-permute-start | bytes 786440 | tf_op jit(solution)/shard_map/ppermute | solution.py:120
  1160.7 96.6 %collective-permute-start.53 = (bf16[64,2048]{1,0:T(8,128)(2,1)}, bf16[64,2048]{1,0:T(8,128)(2,1)}, u32[]{:S(2)}, u32[]{:S(2)}) collective-permute-start(bf16[64,2048]{1,0:T(8,128)(2,1)} %get-tuple-element.290.rest_4_), channel_id=1, source_target_pairs={{0,16},{2,18},{4,20},{6,22},{8,24},{10,26},{12,28},{14,30},{16,0},... | collective-permute-start | bytes 786440 | tf_op jit(solution)/shard_map/ppermute | solution.py:120
  1163.1 94.2 %collective-permute-start.54 = (bf16[64,2048]{1,0:T(8,128)(2,1)}, bf16[64,2048]{1,0:T(8,128)(2,1)}, u32[]{:S(2)}, u32[]{:S(2)}) collective-permute-start(bf16[64,2048]{1,0:T(8,128)(2,1)} %get-tuple-element.289.rest_5_), channel_id=1, source_target_pairs={{0,24},{2,26},{4,28},{6,30},{8,16},{10,18},{12,20},{14,22},{16,8},... | collective-permute-start | bytes 786440 | tf_op jit(solution)/shard_map/ppermute | solution.py:120
  1185.6 49.5 %collective-permute-start.27 = (bf16[2,512,768]{2,1,0:T(8,128)(2,1)}, bf16[2,512,768]{2,1,0:T(8,128)(2,1)}, u32[]{:S(2)}, u32[]{:S(2)}) collective-permute-start(bf16[2,512,768]{2,1,0:T(8,128)(2,1)} %get-tuple-element.200.refs_1_), channel_id=1, source_target_pairs={{0,2},{2,0},{4,6},{6,4},{8,10},{10,8},{12,14},{14,12},{16,18},{18,... | collective-permute-start | bytes 4718600 | tf_op jit(solution)/shard_map/ppermute | solution.py:120
  1262.6 46.6 %collective-permute-start.35 = (bf16[2,2,64,768]{3,2,1,0:T(8,128)(2,1)}, bf16[2,2,64,768]{3,2,1,0:T(8,128)(2,1)}, u32[]{:S(2)}, u32[]{:S(2)}) collective-permute-start(bf16[2,2,64,768]{3,2,1,0:T(8,128)(2,1)} %get-tuple-element.304), channel_id=1, source_target_pairs={{0,4},{2,6},{4,0},{6,2},{8,12},{10,14},{12,8},{14,10},{16,20},{18,... | collective-permute-start | bytes 1179656 | tf_op jit(solution)/shard_map/ppermute | solution.py:120
  (168 other events, 2109.0 us)
Sparse Core Ops, SparseCore 0:
  11.5 174.3 all-gather.4
  189.3 154.9 all-gather.6
  589.7 58.8 all-gather.10
  987.1 55.7 all-gather.8

commit v2 on v1

--- a/solution.py
+++ b/solution.py
@@ -430,7 +430,7 @@
         self.keep = keep.reshape((2,) * len(self.dims) + (self.rows, self.columns))
         self.sent = send
         self.next = CORE
-        self.far = None
+        self.far, self.total = (None, None)
 
     def step(self):
         got = swap(self.sent, self.next).reshape(self.keep.shape)
@@ -451,9 +451,14 @@
         return self.far
 
     def finish(self):
+        if self.total is not None:
+            return self.total
+        while self.far is None:
+            self.step()
         result = self.keep
         for flip, sent in zip(far_flips()[1:], self.far):
             result = result + swap(sent, flip).astype(F32)
+        self.total = result
         return result
 
 
@@ -566,17 +571,17 @@
             column_copy(info[1], parts_r, w_reduce, sems.at[1]),
         )
 
-    total = None
     for p in range(tp):
         for start in range(0, columns, chunk):
             cols = slice(p * columns + start, p * columns + start + chunk)
             value = nn_dot(seq_m[...], w_expand[p, :, start : start + chunk]) + expand_bias[:, cols]
             pre[:, cols] = value
             bent, _ = gelu_parts(value)
-            hidden = (0.5 * value * (1.0 + bent)).astype(jnp.bfloat16)
-            acted[:, cols] = hidden
-            term = nt_dot(hidden, w_reduce[p, :, start : start + chunk])
-            total = term if total is None else total + term
+            acted[:, cols] = (0.5 * value * (1.0 + bent)).astype(jnp.bfloat16)
+    total = None
+    for p in range(tp):
+        term = nt_dot(acted[:, p * columns : (p + 1) * columns], w_reduce[p])
+        total = term if total is None else total + term
     branch[...] = total.astype(jnp.bfloat16)
     stream[...] = mid[...] + mods[0, 5:6, :] * (total + reduce_bias[...])
 
@@ -601,21 +606,28 @@
     d_reduce[...] += row_sum(carried)
     mod_grads[0, 5:6, :] = row_sum(grad * (branch_m[...].astype(jnp.float32) + reduce_bias[...]))
     seq_grad_m[...] = carried.astype(jnp.bfloat16)
+    spans = [(p, start) for p in range(tp) for start in range(0, columns, chunk)]
+
+    def product(p, start):
+        return nn_dot(seq_grad_m[...], w_reduce[p, :, start : start + chunk])
+
     total = None
-    for p in range(tp):
-        for start in range(0, columns, chunk):
-            cols = slice(p * columns + start, p * columns + start + chunk)
-            back = nn_dot(seq_grad_m[...], w_reduce[p, :, start : start + chunk])
-            value = pre[:, cols]
-            bent, square = gelu_parts(value)
-            slope = 0.5 * (1.0 + bent) + (0.5 * GELU_A) * value * (1.0 - bent * bent) * (
-                1.0 + (3.0 * GELU_B) * square
-            )
-            low = (back * slope).astype(jnp.bfloat16)
-            grad_pre[:, cols] = low
-            d_expand[:, cols] += row_sum(low.astype(jnp.float32))
-            term = nt_dot(low, w_expand[p, :, start : start + chunk])
-            total = term if total is None else total + term
+    ahead = product(*spans[0])
+    for i, (p, start) in enumerate(spans):
+        back = ahead
+        if i + 1 < len(spans):
+            ahead = product(*spans[i + 1])
+        cols = slice(p * columns + start, p * columns + start + chunk)
+        value = pre[:, cols]
+        bent, square = gelu_parts(value)
+        slope = 0.5 * (1.0 + bent) + (0.5 * GELU_A) * value * (1.0 - bent * bent) * (
+            1.0 + (3.0 * GELU_B) * square
+        )
+        low = (back * slope).astype(jnp.bfloat16)
+        grad_pre[:, cols] = low
+        d_expand[:, cols] += row_sum(low.astype(jnp.float32))
+        term = nt_dot(low, w_expand[p, :, start : start + chunk])
+        total = term if total is None else total + term
     normed, inverse = norm_parts(mid[...])
     mod_grads[0, 3:4, :] = row_sum(total)
     mod_grads[0, 4:5, :] = row_sum(total * normed)
@@ -804,10 +816,10 @@
 
 def call_parts(kernel, latents, ins, anys, outs, scratch, estimate, afters):
     parts = 2 if afters and latents % 2 == 0 else 1
-    afters = afters or [list, list]
+    afters = afters or [lambda done: []] * 2
     result, sums = (None, None)
     for part in range(parts):
-        after = afters[part]() if parts > 1 else afters[0]() + afters[1]()
+        after = afters[part](result) if parts > 1 else afters[0](None) + afters[1](None)
         result = call_part(
             kernel, part, parts, latents, ins, anys, outs, scratch, estimate, after, result
         )
@@ -856,7 +868,7 @@
 def run_mlp_forward(seq_m, mid, mods, expand_bias, reduce_bias, pieces_e, pieces_r, afters):
     total, depth = mid.shape
     hidden = expand_bias.shape[1]
-    chunk = min(hidden // lax.axis_size(TP), 512)
+    chunk = hidden // lax.axis_size(TP)
     return call_parts(
         functools.partial(mlp_forward_kernel, (pieces_e[1], pieces_r[1]), chunk),
         total // TOK_LAT,
@@ -879,7 +891,7 @@
 ):
     total, depth = mid.shape
     hidden = pre.shape[1]
-    chunk = min(hidden // lax.axis_size(TP), 512)
+    chunk = min(hidden // lax.axis_size(TP), 256)
     return call_parts(
         functools.partial(mlp_backward_kernel, (pieces_e[1], pieces_r[1]), chunk),
         total // TOK_LAT,
@@ -1110,16 +1122,13 @@
     hidden = expand_weight.shape[2]
     width = hidden + cols_qkv + out_weight.shape[1]
     first_half = gather([shard("expand", 0), shard("reduce", 0)])
-    rest = jnp.concatenate([shard(name, 1) for name in ("attn", "expand", "reduce")], axis=1)
-    second_half = gather([hold(rest, matrix)])
+    second_attn = gather([hold(shard("attn", 1), matrix)])
     attn_width = width - hidden
     pieces = {
         ("attn", 0): (matrix, 0, attn_width),
         ("expand", 0): (first_half, 0, hidden),
         ("reduce", 0): (first_half, hidden, hidden),
-        ("attn", 1): (second_half, 0, attn_width),
-        ("expand", 1): (second_half, attn_width, hidden),
-        ("reduce", 1): (second_half, width, hidden),
+        ("attn", 1): (second_attn, 0, attn_width),
     }
 
     features = step_features(steps_all).astype(BF16)
@@ -1174,6 +1183,11 @@
             pieces["reduce", layer],
             None,
         )
+        if layer == 0:
+            second_half = jnp.concatenate([shard("expand", 1), shard("reduce", 1)], axis=1)
+            second_half = gather([hold(second_half, att)])
+            pieces["expand", 1] = (second_half, 0, hidden)
+            pieces["reduce", 1] = (second_half, hidden, hidden)
         kept[layer] = (stream, seq_a, qkv, lse, att, branch_a, mid, seq_m, pre, acted, branch_m)
         stream = after
     cond_matrix = jnp.concatenate([step_out_own, table_own], axis=0).T
@@ -1187,7 +1201,15 @@
     sums, reduced = ({}, {})
 
     def step(*wanted):
-        return lambda: [sent for key in wanted for sent in sums[key].step()]
+        return lambda done=None: [sent for key in wanted for sent in sums[key].step()]
+
+    def finish(keys, array):
+        if array is not None:
+            wait_for(keys, array)
+        return [sums[key].finish() for key in keys]
+
+    def in_turn(steps, finished):
+        return lambda done=None: steps() + finish(finished, None if done is None else done[0])
 
     def mlp_backward(layer, grad, afters):
         stream, seq_a, qkv, lse, att, branch_a, mid, seq_m, pre, acted, branch_m = kept[layer]
@@ -1212,13 +1234,20 @@
     halves = 2 if cols_qkv // 2 % LANES == 0 else 1
     qkv_keys = [[("qkv", layer, i) for i in range(halves)] for layer in range(LAYERS)]
     rest_keys = [[("reduce", layer, 0), ("expand", layer, 0), ("out", layer, 0)] for layer in range(LAYERS)]
-    mlp_afters = [(step(*rest_keys[1]), step(*qkv_keys[1])), (step(), step())]
+    mlp_afters = [
+        (step(*rest_keys[1]), in_turn(step(*qkv_keys[1], *rest_keys[1][1:]), rest_keys[1][:1])),
+        None,
+    ]
     grad_afters = [[step(), step(*qkv_keys[1]), step(*qkv_keys[1])], [step()] * 3]
 
     attn_afters = [
-        (step(*rest_keys[0][:2]), step(*rest_keys[0])),
-        (step(*rest_keys[1][:2]), step(*rest_keys[1][2:])),
+        (step(*rest_keys[0][:2]), in_turn(step(rest_keys[0][2]), qkv_keys[1])),
+        (step(rest_keys[1][0]), step(rest_keys[1][1])),
     ]
+
+    def wait_for(keys, array):
+        for key in keys:
+            sums[key].keep = hold(sums[key].keep, array)
 
     def start(name, layer, left, right, width, firsts, after):
         started = start_sums(left, right, width, firsts, list(after))
@@ -1239,8 +1268,12 @@
             known_columns = exchange_tp(known_columns).reshape(group, -1)
             known_columns = lax.all_gather(known_columns, FSDP, axis=0, tiled=True)
         start("reduce", layer, seq_grad_m, acted, hidden, [FSDP], after[0]())
-        start("expand", layer, seq_m, grad_pre, hidden, [TP], after[1]())
-        start("out", layer, seq_grad_a, att, cols_out, [FSDP], after[2]())
+        first = [sums["reduce", layer, 0].sent]
+        start("expand", layer, seq_m, grad_pre, hidden, [TP], after[1]() + first)
+        first = [sums["expand", layer, 0].sent]
+        if layer == 0:
+            first += finish(rest_keys[1][1:], first[0])
+        start("out", layer, seq_grad_a, att, cols_out, [FSDP], after[2]() + first)
         grad_qkv, grad_stream, mod_early = run_attn_backward(
             seq_grad_a,
             qkv,
@@ -1252,25 +1285,18 @@
             cols_qkv,
             attn_afters[layer],
         )
-        after = step(*rest_keys[layer])()
+        after = step(*(rest_keys[layer] if layer == 0 else rest_keys[layer][::2]))()
         start("qkv", layer, seq_a, grad_qkv, cols_qkv, [TP, FSDP][:halves], after)
         mod_grads[layer] = jnp.concatenate([mod_early, mod_late[:, 2:]], axis=1)
         layer_bias_grads[layer] = (d_out[0], d_expand[0], d_reduce[0])
-    last_sent = sums["qkv", 0, 0].sent
+    last_sent = [sums[key].sent for key in qkv_keys[0]]
     mod_columns = modulate_weight.shape[1]
-    mod_early = hold(mod_early, last_sent)
+    mod_early, grad_stream = (hold(mod_early, *last_sent), hold(grad_stream, *last_sent))
     mod_last = mod_early.reshape(own, -1).astype(BF16)
     last_columns = push([mod_last.reshape(-1, LANES)], [-(-mod_last.shape[1] // mod_columns) + 1], 3)[0]
+    wait_for(qkv_keys[0] + rest_keys[0], last_columns)
+    step(*qkv_keys[0], *rest_keys[0])()
     last_columns = last_columns.reshape(latents, -1)
-    for total_sum in sums.values():
-        while total_sum.far is None:
-            last_sent = total_sum.step()[0]
-    for (name, layer, i), total_sum in sums.items():
-        reduced.setdefault((name, layer), []).append(total_sum.finish())
-    reduced = {key: jnp.concatenate(parts, axis=1) for key, parts in reduced.items()}
-    for layer in range(LAYERS):
-        reduced["qkv", layer] = heads_together(reduced["qkv", layer])
-    grad_stream = hold(grad_stream, sums["qkv", 0, 0].far[0])
     grad_embedded = grad_stream.astype(BF16)
     grad_patch_in = contract(noisy.reshape(-1, CH), grad_embedded, "tc,td->cd")
     grad_patch_bias = jnp.sum(grad_embedded.astype(F32), axis=0)
@@ -1282,7 +1308,8 @@
     grad_ada = contract(act_own, grad_columns, "gd,ge->de")
     act_part = contract(grad_columns, low_modulate, "ge,de->gd").reshape(-1, own, low_modulate.shape[0])
     act_part = jnp.pad(act_part, ((0, 0), (0, -own % 8), (0, -act_part.shape[2] % LANES)))
-    act_part = push([act_part], [1], 4)[0][:, :own, : low_modulate.shape[0]]
+    act_part = push([act_part], [1], 4)[0]
+    act_part = act_part[:, :own, : low_modulate.shape[0]]
     act_part = jnp.sum(act_part.reshape(fsdp_count, tp_count, own, -1), axis=1).swapaxes(0, 1).reshape(own, -1)
 
     def of_own(value):
@@ -1321,7 +1348,12 @@
     )
     width = small.shape[1]
     small = jnp.pad(small, ((0, 0), (0, -width % (8 * LANES)))).reshape(small.shape[0], -1, LANES)
-    small, both_grads = push([hold(small, sums["qkv", 0, 0].far[0]), both_grads], [1, 1], 1)
+    small, both_grads = push([small, both_grads], [1, 1], 1)
+    for (name, layer, i), total_sum in sums.items():
+        reduced.setdefault((name, layer), []).append(total_sum.finish())
+    reduced = {key: jnp.concatenate(parts, axis=1) for key, parts in reduced.items()}
+    for layer in range(LAYERS):
+        reduced["qkv", layer] = heads_together(reduced["qkv", layer])
     small = jnp.sum(small, axis=0).reshape(-1)[:width]
     grad_cond = both_grads[:, :own, :columns].reshape(latents, columns)
     grad_step_pre = both_grads[:, own : 2 * own, :columns].reshape(latents, columns)

time: 1380 us -> 1320 us (0.957)
  waiting for transfers between devices: 186 us -> 131 us
  Pallas kernels: 883 us -> 861 us
    ppermute x65, waiting for transfers between devices: 150 us -> 114 us  [swap(): lax.ppermute(value, name, [(i, i ^ bits) for i in range(lax.axis_size(nam...]
    pallas_call x13 -> x12, Pallas kernels: 551 us -> 531 us  [call_part(): pl.pallas_call(body, grid=(count,), in_specs=[spec(kind, dims_of(kind, ar...]
    all_gather x2 -> x3, waiting for transfers between devices: 35.7 us -> 16.9 us  [gather(): whole = lax.all_gather(packed, (TP, FSDP), axis=0, tiled=True)]
  transfers between devices with their start and end apart: 69 -> 70, of which waited for: 26 -> 24; matrix products, arithmetic and copies ran while one was open for 12% -> 13% of each run, Pallas kernels for 47% -> 65%
where the time goes in v2:
time: 1320 us; the launch traced here: 1310 us
  Pallas kernels  861 us (65%)
  waiting for transfers between devices  131 us (10%)
  other arithmetic  118 us (9%)
  starting transfers between devices  88.5 us (7%)
  local copies, waits for them, and re-layouts  58.6 us (4%)
  matrix products  29.9 us (2%)
  between operations  23.4 us (2%)
    pallas_call x12, Pallas kernels, call_part(): pl.pallas_call(body, grid=(count,), in_specs=[spec(kind, dims_of(kind, ar...  531 us
    pallas_call x8, Pallas kernels, start_sums(): pl.pallas_call(body, grid_spec=pltpu.PrefetchScalarGridSpec(num_scalar_pr...  162 us
    ppermute x65, waiting for transfers between devices, swap(): lax.ppermute(value, name, [(i, i ^ bits) for i in range(lax.axis_size(nam...  114 us
    pallas_call x1, Pallas kernels, run_head(): pl.pallas_call(head_kernel, in_specs=[vmem] * 3 + [ANY] * 2, out_specs=[v...  113 us
    ppermute x65, starting transfers between devices, swap(): lax.ppermute(value, name, [(i, i ^ bits) for i in range(lax.axis_size(nam...  88.1 us
    pallas_call x4, Pallas kernels, push(): pl.pallas_call(functools.partial(push_kernel, plans, len(arrays)), in_spe...  55.3 us
    convert_element_type x20, other arithmetic, step(): part(axis, 0).astype(BF16)  42.4 us
  transfers between devices with their start and end apart: 70, of which 24 were waited for; matrix products, arithmetic and copies ran while one was open for 13% of the time, Pallas kernels for 65%

profile of v2, /device:TPU:0, one launch (start us, length us, event | category | flops | bytes accessed | tf_op | source)
XLA Modules:
  0.0 1310.2 jit_solution(2399483530662186459)
XLA Ops:
  19.2 112.6 %shard_map.473 = (f32[32,16,128]{2,1,0:T(8,128)}, bf16[32,64,128]{2,1,0:T(8,128)(2,1)}, bf16[8,272,128]{2,1,0:T(8,128)(2,1)}, bf16[4,64,7168]{2,1,0:T(8,128)(2,1)}, bf16[2,1024,2048]{2,1,0:T(8,128)(2,1)}) custom-call(f32[16,128]{1,0:T(8,128)} %pad_bitcast_fusion.packed, bf16[64,128]{1,0:T(8,128)(2,1)} %reshape.841.step_in, bf16[272,128]{1,0:T(8,128)(2,1)} %pad.33.cond, ...), custom_call_target="tpu_custom_call" | custom-call | flops 40000000000 | bytes 100000000 | tf_op jit(solution)/shard_map/pallas_call | solution.py:405
  165.8 10.7 collective-permute-done
  195.0 56.8 %shard_map.474 = (bf16[2048,1024]{1,0:T(8,128)(2,1)}, bf16[2048,3072]{1,0:T(8,128)(2,1)}, f32[8,16,256]{2,1,0:T(8,128)}, bf16[2048,1024]{1,0:T(8,128)(2,1)}, bf1...) custom-call(f32[2048,1024]{1,0:T(8,128)} %bitcast.490, ...), custom_call_target="tpu_custom_call" | custom-call | flops 42949672960 | bytes 50331648 | tf_op jit(solution)/shard_map/pallas_call | solution.py:804
  256.8 53.2 %shard_map.475 = (f32[2048,4096]{1,0:T(8,128)}, bf16[2048,4096]{1,0:T(8,128)(2,1)}, bf16[2048,1024]{1,0:T(8,128)(2,1)}, f32[2048,1024]{1,0:T(8,128)}) custom-call(bf16[2048,1024]{1,0:T(8,128)(2,1)} %get-tuple-element.126.refs_0_.left, f32[2048,1024]{1,0:T(8,128)} %get-tuple-element.127.refs_1_.refs_3_, ...), custom_call_target="tpu_custom_call" | custom-call | flops 51539607552 | bytes 50331648 | tf_op jit(solution)/shard_map/pallas_call | solution.py:804
  310.0 56.4 %shard_map.477 = (bf16[2048,1024]{1,0:T(8,128)(2,1)}, bf16[2048,3072]{1,0:T(8,128)(2,1)}, f32[8,16,256]{2,1,0:T(8,128)}, bf16[2048,1024]{1,0:T(8,128)(2,1)}, bf1...) custom-call(f32[2048,1024]{1,0:T(8,128)} %get-tuple-element.128.refs_0_.refs_3_, ...), custom_call_target="tpu_custom_call" | custom-call | flops 42949672960 | bytes 50331648 | tf_op jit(solution)/shard_map/pallas_call | solution.py:804
  366.5 16.8 %all-gather.10.cloned.1.call-done = bf16[2048,4096]{1,0:T(8,128)(2,1)} async-done(((bf16[64,4096]{1,0:T(8,128)(2,1)}), bf16[2048,4096]{1,0:T(8,128)(2,1)}) %all-gather.10.cloned.1.call-update) | async-done | bytes 16777232 | tf_op jit(solution)/shard_map/all_gather | solution.py:1119
  383.4 64.5 %shard_map.479 = (f32[2048,4096]{1,0:T(8,128)}, bf16[2048,4096]{1,0:T(8,128)(2,1)}, bf16[2048,1024]{1,0:T(8,128)(2,1)}, f32[2048,1024]{1,0:T(8,128)}) custom-call(bf16[2048,1024]{1,0:T(8,128)(2,1)} %get-tuple-element.129.refs_0_.left.refs_1_, f32[2048,1024]{1,0:T(8,128)} %get-tuple-element.130.refs_1_.refs_3_, ...), custom_call_target="tpu_custom_call" | custom-call | flops 51539607552 | bytes 50331648 | tf_op jit(solution)/shard_map/pallas_call | solution.py:804
  447.8 13.9 %shard_map.480 = (f32[2048,1024]{1,0:T(8,128)}, f32[8,2,1024]{2,1,0:T(2,128)}, f32[16,1024]{1,0:T(8,128)}, f32[1,16]{1,0:T(1,128)}) custom-call(f32[2048,1024]{1,0:T(8,128)} %get-tuple-element.132.refs_0_, f32[8,2,1024]{2,1,0:T(2,128)} %slice.1017.refs_1_, f32[8,256,16]{2,1,0:T(8,128)} %copy.252.refs_2_, bf16[16,1024]{1,0:T(8,128)(2,1)} %convert_element_type.1416.refs_3_), custom_call_target="tpu_custom_call" | custom-call | flops 1610612736 | bytes 16777216 | tf_op jit(solution)/shard_map/pallas_call | solution.py:804
  461.8 64.3 %shard_map.481 = (bf16[2048,1024]{1,0:T(8,128)(2,1)}, bf16[2048,4096]{1,0:T(8,128)(2,1)}, f32[2048,1024]{1,0:T(8,128)}, bf16[2048,1024]{1,0:T(8,128)(2,1)}, f32[...) custom-call(f32[2048,1024]{1,0:T(8,128)} %get-tuple-element.133.refs_0_, ...), custom_call_target="tpu_custom_call" | custom-call | flops 51539607552 | bytes 50331648 | tf_op jit(solution)/shard_map/pallas_call | solution.py:804
  526.1 24.8 %shard_map.482 = (bf16[2,512,2048]{2,1,0:T(8,128)(2,1)}, bf16[2,512,2048]{2,1,0:T(8,128)(2,1)}) custom-call(s32[2]{0:T(128)} %pad_add_fusion.place, bf16[2048,1024]{1,0:T(8,128)(2,1)} %get-tuple-element.141.left, bf16[2048,4096]{1,0:T(8,128)(2,1)} %get-tuple-element.142.right), custom_call_target="tpu_custom_call" | custom-call | flops 21474836480 | bytes 20971520 | tf_op jit(solution)/shard_map/pallas_call | solution.py:994
  550.9 24.8 %shard_map.484 = (bf16[2,512,2048]{2,1,0:T(8,128)(2,1)}, bf16[2,512,2048]{2,1,0:T(8,128)(2,1)}) custom-call(s32[2]{0:T(128)} %pad_add_fusion.place, bf16[2048,1024]{1,0:T(8,128)(2,1)} %get-tuple-element.129.refs_0_.left.refs_1_, bf16[2048,4096]{1,0:T(8,128)(2,1)} %get-tuple-element.148.right, bf16[2,512,2048]{2,1,0:T(8,128)(2,1)} %get-tuple-element.144.rest_0_), custom_call_target="tpu_custom_call" | custom-call | flops 21474836480 | bytes 20971520 | tf_op jit(solution)/shard_map/pallas_call | solution.py:994
  576.2 10.4 shard_map.486
  593.6 12.6 collective-permute-done.10
  632.1 36.3 %shard_map.483 = (bf16[2048,3072]{1,0:T(8,128)(2,1)}, f32[2048,1024]{1,0:T(8,128)}, f32[8,2,1024]{2,1,0:T(2,128)}) custom-call(bf16[2048,1024]{1,0:T(8,128)(2,1)} %get-tuple-element.137.refs_0_.left, bf16[2048,3072]{1,0:T(8,128)(2,1)} %get-tuple-element.138.refs_1_, f32[8,16,256]{2,1,0:T(8,128)} %get-tuple-element.139.refs_2_, ...), custom_call_target="tpu_custom_call" | custom-call | flops 25769803776 | bytes 25165824 | tf_op jit(solution)/shard_map/pallas_call | solution.py:804
  668.4 36.1 %shard_map.485 = (bf16[2048,3072]{1,0:T(8,128)(2,1)}, f32[2048,1024]{1,0:T(8,128)}, f32[8,2,1024]{2,1,0:T(2,128)}) custom-call(bf16[2048,1024]{1,0:T(8,128)(2,1)} %get-tuple-element.137.refs_0_.left, bf16[2048,3072]{1,0:T(8,128)(2,1)} %get-tuple-element.138.refs_1_, ...), custom_call_target="tpu_custom_call", output_to_operand_aliasing={{0}: (7, {}), {1}: (8, {}), {2}: (9, {})} | custom-call | flops 25769803776 | bytes 25165824 | tf_op jit(solution)/shard_map/pallas_call | solution.py:804
  714.4 21.0 %shard_map.488 = (bf16[2,512,768]{2,1,0:T(8,128)(2,1)}, bf16[2,512,768]{2,1,0:T(8,128)(2,1)}, bf16[2,512,768]{2,1,0:T(8,128)(2,1)}, bf16[2,512,768]{2,1,0:T(8,128)(2,1)}) custom-call(s32[2]{0:T(128)} %pad_add_fusion.place, bf16[2048,1024]{1,0:T(8,128)(2,1)} %get-tuple-element.163.left, bf16[2048,3072]{1,0:T(8,128)(2,1)} %get-tuple-element.164.right, ...), custom_call_target="tpu_custom_call" | custom-call | flops 16106127360 | bytes 16777216 | tf_op jit(solution)/shard_map/pallas_call | solution.py:994
  740.3 38.3 %shard_map.487 = (bf16[2048,1024]{1,0:T(8,128)(2,1)}, bf16[2048,4096]{1,0:T(8,128)(2,1)}, f32[2048,1024]{1,0:T(8,128)}, bf16[2048,1024]{1,0:T(8,128)(2,1)}, f32[...) custom-call(f32[2048,1024]{1,0:T(8,128)} %get-tuple-element.151.refs_0_, ...), custom_call_target="tpu_custom_call" | custom-call | flops 25769803776 | bytes 25165824 | tf_op jit(solution)/shard_map/pallas_call | solution.py:804
  802.0 38.4 %shard_map.490 = (bf16[2048,1024]{1,0:T(8,128)(2,1)}, bf16[2048,4096]{1,0:T(8,128)(2,1)}, f32[2048,1024]{1,0:T(8,128)}, bf16[2048,1024]{1,0:T(8,128)(2,1)}, f32[...) custom-call(f32[2048,1024]{1,0:T(8,128)} %get-tuple-element.151.refs, ...), custom_call_target="tpu_custom_call", output_to_operand_aliasing={{0}: (10, {}), {1}: (11, {}), {2}: (12, {}), {3}: (13, {}),... | custom-call | flops 25769803776 | bytes 25165824 | tf_op jit(solution)/shard_map/pallas_call | solution.py:804
  843.7 24.9 %shard_map.491 = (bf16[2,512,2048]{2,1,0:T(8,128)(2,1)}, bf16[2,512,2048]{2,1,0:T(8,128)(2,1)}) custom-call(s32[2]{0:T(128)} %pad_add_fusion.place, bf16[2048,1024]{1,0:T(8,128)(2,1)} %get-tuple-element.173.left, bf16[2048,4096]{1,0:T(8,128)(2,1)} %get-tuple-element.174.right), custom_call_target="tpu_custom_call" | custom-call | flops 21474836480 | bytes 20971520 | tf_op jit(solution)/shard_map/pallas_call | solution.py:994
  876.4 25.0 %shard_map.492 = (bf16[2,512,2048]{2,1,0:T(8,128)(2,1)}, bf16[2,512,2048]{2,1,0:T(8,128)(2,1)}) custom-call(s32[2]{0:T(128)} %pad_add_fusion.place, bf16[2048,1024]{1,0:T(8,128)(2,1)} %get-tuple-element.126.refs_0_.left, bf16[2048,4096]{1,0:T(8,128)(2,1)} %get-tuple-element.177.right, bf16[2,2,64,768]{3,2,1,0:T(8,128)(2,1)} %get-tuple-element.298.rest_0_, ...), custom_call_target="tpu_custom_call" | custom-call | flops 21474836480 | bytes 20971520 | tf_op jit(solution)/shard_map/pallas_call | solution.py:994
  920.1 10.4 shard_map.496
  942.0 8.8 collective-permute-done.39
  967.3 36.2 %shard_map.493 = (bf16[2048,3072]{1,0:T(8,128)(2,1)}, f32[2048,1024]{1,0:T(8,128)}, f32[8,2,1024]{2,1,0:T(2,128)}) custom-call(bf16[2048,1024]{1,0:T(8,128)(2,1)} %get-tuple-element.169.refs_0_.left, bf16[2048,3072]{1,0:T(8,128)(2,1)} %get-tuple-element.170.refs_1_, f32[8,16,256]{2,1,0:T(8,128)} %get-tuple-element.171.refs_2_, f32[2048,1024]{1,0:T(8,128)} %bitcast.491, ...), custom_call_target="tpu_custom_call" | custom-call | flops 25769803776 | bytes 25165824 | tf_op jit(solution)/shard_map/pallas_call | solution.py:804
  1016.5 36.3 %shard_map.499 = (bf16[2048,3072]{1,0:T(8,128)(2,1)}, f32[2048,1024]{1,0:T(8,128)}, f32[8,2,1024]{2,1,0:T(2,128)}) custom-call(bf16[2048,1024]{1,0:T(8,128)(2,1)} %get-tuple-element.169.refs_0_.left, bf16[2048,3072]{1,0:T(8,128)(2,1)} %get-tuple-element.170.refs_1_, ...), custom_call_target="tpu_custom_call", output_to_operand_aliasing={{0}: (7, {}), {1}: (8, {}), {2}: (9, {})} | custom-call | flops 25769803776 | bytes 25165824 | tf_op jit(solution)/shard_map/pallas_call | solution.py:804
  1063.3 20.8 %shard_map.500 = (bf16[2,512,768]{2,1,0:T(8,128)(2,1)}, bf16[2,512,768]{2,1,0:T(8,128)(2,1)}, bf16[2,512,768]{2,1,0:T(8,128)(2,1)}, bf16[2,512,768]{2,1,0:T(8,128)(2,1)}) custom-call(s32[2]{0:T(128)} %pad_add_fusion.place, bf16[2048,1024]{1,0:T(8,128)(2,1)} %get-tuple-element.125.left, bf16[2048,3072]{1,0:T(8,128)(2,1)} %get-tuple-element.185.right, ...), custom_call_target="tpu_custom_call" | custom-call | flops 16106127360 | bytes 16777216 | tf_op jit(solution)/shard_map/pallas_call | solution.py:994
  1086.1 17.5 %shard_map.502.refs_1_ = bf16[32,128,128]{2,1,0:T(8,128)(2,1)} custom-call(bf16[128,128]{1,0:T(8,128)(2,1)} %convert_element_type.1621.refs_0_), custom_call_target="tpu_custom_call" | custom-call | flops 5000000000 | bytes 50000000 | tf_op jit(solution)/shard_map/pallas_call | solution.py:258
  1109.7 11.6 shard_map.509
  1139.6 15.7 %shard_map.511 = (f32[32,16,128]{2,1,0:T(8,128)}, f32[32,16,128]{2,1,0:T(8,128)}) custom-call(f32[32,16,128]{2,1,0:T(8,128)} %bitcast.567, f32[32,16,128]{2,1,0:T(8,128)} %pad.38.refs_1_), custom_call_target="tpu_custom_call" | custom-call | flops 5000000000 | bytes 50000000 | tf_op jit(solution)/shard_map/pallas_call | solution.py:258
  1188.2 7.2 collective-permute-done.62
  1204.7 8.6 collective-permute-done.56
  1220.9 9.3 collective-permute-done.47
  1270.4 10.5 shard_map.512
  (643 shorter events, 352.2 us)
Async XLA Ops:
  7.2 249.6 %all-gather.6.cloned.1.call-start = ((), (), s32[]{:S(2)}) async-start(), calls=%async_computation | async-start | bytes 17301504 | tf_op jit(solution)/shard_map/all_gather | solution.py:1119
  11.1 298.9 %all-gather.8.cloned.1.call-start = ((), (), s32[]{:S(2)}) async-start(), calls=%async_computation.1 | async-start | bytes 8650752 | tf_op jit(solution)/shard_map/all_gather | solution.py:1119
  131.9 251.5 %all-gather.10.cloned.1.call-start = ((), (), s32[]{:S(2)}) async-start(), calls=%async_computation.2 | async-start | bytes 17301504 | tf_op jit(solution)/shard_map/all_gather | solution.py:1119
  251.8 363.0 %all-gather.14.cloned.1.call-start = ((), (), s32[]{:S(2)}) async-start(), calls=%async_computation.4 | async-start | bytes 2433024 | tf_op jit(solution)/shard_map/all_gather | solution.py:1194
  366.5 738.8 %all-gather.12.cloned.1.call-start = ((), (), s32[]{:S(2)}) async-start(), calls=%async_computation.3 | async-start | bytes 3899392 | tf_op jit(solution)/shard_map/all_gather | solution.py:1269
  575.7 41.0 %collective-permute-start.5 = (bf16[2,512,2048]{2,1,0:T(8,128)(2,1)}, bf16[2,512,2048]{2,1,0:T(8,128)(2,1)}, u32[]{:S(2)}, u32[]{:S(2)}) collective-permute-start(bf16[2,512,2048]{2,1,0:T(8,128)(2,1)} %get-tuple-element.150.rest_0_), channel_id=1, source_target_pairs={{0,2},{2,0},{4,6},{6,4},{8,10},{10,8},{12,14},{14,12},{16,18},{18,... | collective-permute-start | bytes 12582920 | tf_op jit(solution)/shard_map/ppermute | solution.py:120
  575.9 49.0 %collective-permute-start.4 = (bf16[2,512,2048]{2,1,0:T(8,128)(2,1)}, bf16[2,512,2048]{2,1,0:T(8,128)(2,1)}, u32[]{:S(2)}, u32[]{:S(2)}) collective-permute-start(bf16[2,512,2048]{2,1,0:T(8,128)(2,1)} %get-tuple-element.144.rest_0_), channel_id=1, source_target_pairs={{0,2},{2,0},{4,6},{6,4},{8,10},{10,8},{12,14},{14,12},{16,18},{18,... | collective-permute-start | bytes 12582920 | tf_op jit(solution)/shard_map/ppermute | solution.py:120
  621.2 88.7 %collective-permute-start.8 = (bf16[2,2,2,64,2048]{4,3,2,1,0:T(8,128)(2,1)}, bf16[2,2,2,64,2048]{4,3,2,1,0:T(8,128)(2,1)}, u32[]{:S(2)}, u32[]{:S(2)}) collective-permute-start(bf16[2,2,2,64,2048]{4,3,2,1,0:T(8,128)(2,1)} %fusion.1.refs_10_), channel_id=1, source_target_pairs={{0,4},{2,6},{4,0},{6,2},{8,12},{10,14},{12,8},{14,10},{16,20},{18,... | collective-permute-start | bytes 6291464 | tf_op jit(solution)/shard_map/ppermute | solution.py:120
  631.0 73.5 %collective-permute-start.6 = (bf16[2,2,2,64,2048]{4,3,1,0,2:T(8,128)(2,1)}, bf16[2,2,2,64,2048]{4,3,1,0,2:T(8,128)(2,1)}, u32[]{:S(2)}, u32[]{:S(2)}) collective-permute-start(bf16[2,2,2,64,2048]{4,3,1,0,2:T(8,128)(2,1)} %copy.256), channel_id=1, source_target_pairs={{0,1},{1,0},{2,3},{3,2},{4,5},{5,4},{6,7},{7,6},{8,9},{9,8},{10,11... | collective-permute-start | bytes 6291464 | tf_op jit(solution)/shard_map/ppermute | solution.py:120
  713.4 65.2 %collective-permute-start.13 = (bf16[2,2,64,2048]{3,2,1,0:T(8,128)(2,1)}, bf16[2,2,64,2048]{3,2,1,0:T(8,128)(2,1)S(1)}, u32[]{:S(2)}, u32[]{:S(2)}) collective-permute-start(bf16[2,2,64,2048]{3,2,1,0:T(8,128)(2,1)} %get-tuple-element.264.refs_13_), channel_id=1, source_target_pairs={{0,1},{1,0},{2,3},{3,2},{4,5},{5,4},{6,7},{7,6},{8,9},{9,8},{10,11... | collective-permute-start | bytes 3145736 | tf_op jit(solution)/shard_map/ppermute | solution.py:120
  735.3 61.4 %collective-permute-start.12 = (bf16[2,512,768]{2,1,0:T(8,128)(2,1)}, bf16[2,512,768]{2,1,0:T(8,128)(2,1)}, u32[]{:S(2)}, u32[]{:S(2)}) collective-permute-start(bf16[2,512,768]{2,1,0:T(8,128)(2,1)} %get-tuple-element.168), channel_id=1, source_target_pairs={{0,2},{2,0},{4,6},{6,4},{8,10},{10,8},{12,14},{14,12},{16,18},{18,... | collective-permute-start | bytes 4718600 | tf_op jit(solution)/shard_map/ppermute | solution.py:120
  735.3 64.3 %collective-permute-start.11 = (bf16[2,512,768]{2,1,0:T(8,128)(2,1)}, bf16[2,512,768]{2,1,0:T(8,128)(2,1)}, u32[]{:S(2)}, u32[]{:S(2)}) collective-permute-start(bf16[2,512,768]{2,1,0:T(8,128)(2,1)} %get-tuple-element.166), channel_id=1, source_target_pairs={{0,2},{2,0},{4,6},{6,4},{8,10},{10,8},{12,14},{14,12},{16,18},{18,... | collective-permute-start | bytes 4718600 | tf_op jit(solution)/shard_map/ppermute | solution.py:120
  738.3 44.0 %collective-permute-start.15 = (bf16[64,2048]{1,0:T(8,128)(2,1)}, bf16[64,2048]{1,0:T(8,128)(2,1)S(1)}, u32[]{:S(2)}, u32[]{:S(2)}) collective-permute-start(bf16[64,2048]{1,0:T(8,128)(2,1)} %get-tuple-element.284.refs_10_), channel_id=1, source_target_pairs={{0,8},{2,10},{4,12},{6,14},{8,0},{10,2},{12,4},{14,6},{16,24},{18,... | collective-permute-start | bytes 786440 | tf_op jit(solution)/shard_map/ppermute | solution.py:120
  738.7 43.6 %collective-permute-start.16 = (bf16[64,2048]{1,0:T(8,128)(2,1)}, bf16[64,2048]{1,0:T(8,128)(2,1)S(1)}, u32[]{:S(2)}, u32[]{:S(2)}) collective-permute-start(bf16[64,2048]{1,0:T(8,128)(2,1)} %get-tuple-element.283.refs_11_), channel_id=1, source_target_pairs={{0,16},{2,18},{4,20},{6,22},{8,24},{10,26},{12,28},{14,30},{16,0},... | collective-permute-start | bytes 786440 | tf_op jit(solution)/shard_map/ppermute | solution.py:120
  782.3 124.8 %collective-permute-start.27 = (bf16[64,512]{1,0:T(8,128)(2,1)S(1)}, bf16[64,512]{1,0:T(8,128)(2,1)S(1)}, u32[]{:S(2)}, u32[]{:S(2)}) collective-permute-start(bf16[64,512]{1,0:T(8,128)(2,1)S(1)} %get-tuple-element.326.refs_20_), channel_id=1, source_target_pairs={{0,8},{2,10},{4,12},{6,14},{8,0},{10,2},{12,4},{14,6},{16,24},{18,... | collective-permute-start | bytes 196616 | tf_op jit(solution)/shard_map/ppermute | solution.py:120
  782.4 126.6 %collective-permute-start.28 = (bf16[64,512]{1,0:T(8,128)(2,1)S(1)}, bf16[64,512]{1,0:T(8,128)(2,1)S(1)}, u32[]{:S(2)}, u32[]{:S(2)}) collective-permute-start(bf16[64,512]{1,0:T(8,128)(2,1)S(1)} %get-tuple-element.325.refs_21_), channel_id=1, source_target_pairs={{0,16},{2,18},{4,20},{6,22},{8,24},{10,26},{12,28},{14,30},{16,0},... | collective-permute-start | bytes 196616 | tf_op jit(solution)/shard_map/ppermute | solution.py:120
  789.9 111.5 %collective-permute-start.24 = (bf16[64,2048]{1,0:T(8,128)(2,1)S(1)}, bf16[64,2048]{1,0:T(8,128)(2,1)}, u32[]{:S(2)}, u32[]{:S(2)}) collective-permute-start(bf16[64,2048]{1,0:T(8,128)(2,1)S(1)} %get-tuple-element.280.refs_17_), channel_id=1, source_target_pairs={{0,8},{2,10},{4,12},{6,14},{8,0},{10,2},{12,4},{14,6},{16,24},{18,... | collective-permute-start | bytes 786440 | tf_op jit(solution)/shard_map/ppermute | solution.py:120
  801.0 71.0 %collective-permute-start.19 = (bf16[2,2,2,64,768]{4,3,2,1,0:T(8,128)(2,1)S(1)}, bf16[2,2,2,64,768]{4,3,2,1,0:T(8,128)(2,1)}, u32[]{:S(2)}, u32[]{:S(2)}) collective-permute-start(bf16[2,2,2,64,768]{4,3,2,1,0:T(8,128)(2,1)S(1)} %fusion.31.refs_15_), channel_id=1, source_target_pairs={{0,4},{2,6},{4,0},{6,2},{8,12},{10,14},{12,8},{14,10},{16,20},{18,... | collective-permute-start | bytes 2359304 | tf_op jit(solution)/shard_map/ppermute | solution.py:120
  871.0 32.7 %collective-permute-start.25 = (bf16[64,2048]{1,0:T(8,128)(2,1)S(1)}, bf16[64,2048]{1,0:T(8,128)(2,1)}, u32[]{:S(2)}, u32[]{:S(2)}) collective-permute-start(bf16[64,2048]{1,0:T(8,128)(2,1)S(1)} %copy-done.35), channel_id=1, source_target_pairs={{0,16},{2,18},{4,20},{6,22},{8,24},{10,26},{12,28},{14,30},{16,0},... | collective-permute-start | bytes 786440 | tf_op jit(solution)/shard_map/ppermute | solution.py:120
  903.8 50.3 %collective-permute-start.18 = (bf16[2,512,2048]{2,1,0:T(8,128)(2,1)}, bf16[2,512,2048]{2,1,0:T(8,128)(2,1)}, u32[]{:S(2)}, u32[]{:S(2)}) collective-permute-start(bf16[2,512,2048]{2,1,0:T(8,128)(2,1)} %get-tuple-element.176.rest_2_), channel_id=1, source_target_pairs={{0,2},{2,0},{4,6},{6,4},{8,10},{10,8},{12,14},{14,12},{16,18},{18,... | collective-permute-start | bytes 12582920 | tf_op jit(solution)/shard_map/ppermute | solution.py:120
  909.0 52.6 %collective-permute-start.21 = (bf16[2,512,2048]{2,1,0:T(8,128)(2,1)}, bf16[2,512,2048]{2,1,0:T(8,128)(2,1)}, u32[]{:S(2)}, u32[]{:S(2)}) collective-permute-start(bf16[2,512,2048]{2,1,0:T(8,128)(2,1)} %get-tuple-element.179.refs_1_.rest_6_), channel_id=1, source_target_pairs={{0,2},{2,0},{4,6},{6,4},{8,10},{10,8},{12,14},{14,12},{16,18},{18,... | collective-permute-start | bytes 12582920 | tf_op jit(solution)/shard_map/ppermute | solution.py:120
  939.0 64.5 %collective-permute-start.34 = (bf16[64,768]{1,0:T(8,128)(2,1)}, bf16[64,768]{1,0:T(8,128)(2,1)S(1)}, u32[]{:S(2)}, u32[]{:S(2)}) collective-permute-start(bf16[64,768]{1,0:T(8,128)(2,1)} %get-tuple-element.315.rest_3_), channel_id=1, source_target_pairs={{0,8},{2,10},{4,12},{6,14},{8,0},{10,2},{12,4},{14,6},{16,24},{18,... | collective-permute-start | bytes 294920 | tf_op jit(solution)/shard_map/ppermute | solution.py:120
  939.1 68.0 %collective-permute-start.35 = (bf16[64,768]{1,0:T(8,128)(2,1)}, bf16[64,768]{1,0:T(8,128)(2,1)S(1)}, u32[]{:S(2)}, u32[]{:S(2)}) collective-permute-start(bf16[64,768]{1,0:T(8,128)(2,1)} %get-tuple-element.314.rest_4_), channel_id=1, source_target_pairs={{0,16},{2,18},{4,20},{6,22},{8,24},{10,26},{12,28},{14,30},{16,0},... | collective-permute-start | bytes 294920 | tf_op jit(solution)/shard_map/ppermute | solution.py:120
  950.8 57.3 %collective-permute-start.36 = (bf16[64,768]{1,0:T(8,128)(2,1)}, bf16[64,768]{1,0:T(8,128)(2,1)S(1)}, u32[]{:S(2)}, u32[]{:S(2)}) collective-permute-start(bf16[64,768]{1,0:T(8,128)(2,1)} %get-tuple-element.313.rest_5_), channel_id=1, source_target_pairs={{0,24},{2,26},{4,28},{6,30},{8,16},{10,18},{12,20},{14,22},{16,8},... | collective-permute-start | bytes 294920 | tf_op jit(solution)/shard_map/ppermute | solution.py:120
  954.1 55.8 %collective-permute-start.31 = (bf16[64,768]{1,0:T(8,128)(2,1)S(1)}, bf16[64,768]{1,0:T(8,128)(2,1)S(1)}, u32[]{:S(2)}, u32[]{:S(2)}) collective-permute-start(bf16[64,768]{1,0:T(8,128)(2,1)S(1)} %copy-done.81), channel_id=1, source_target_pairs={{0,8},{2,10},{4,12},{6,14},{8,0},{10,2},{12,4},{14,6},{16,24},{18,... | collective-permute-start | bytes 294920 | tf_op jit(solution)/shard_map/ppermute | solution.py:120
  961.6 49.6 %collective-permute-start.32 = (bf16[64,768]{1,0:T(8,128)(2,1)S(1)}, bf16[64,768]{1,0:T(8,128)(2,1)S(1)}, u32[]{:S(2)}, u32[]{:S(2)}) collective-permute-start(bf16[64,768]{1,0:T(8,128)(2,1)S(1)} %copy-done.80), channel_id=1, source_target_pairs={{0,16},{2,18},{4,20},{6,22},{8,24},{10,26},{12,28},{14,30},{16,0},... | collective-permute-start | bytes 294920 | tf_op jit(solution)/shard_map/ppermute | solution.py:120
  1007.1 150.6 %collective-permute-start.52 = (bf16[2,2,64,512]{3,2,1,0:T(8,128)(2,1)}, bf16[2,2,64,512]{3,2,1,0:T(8,128)(2,1)}, u32[]{:S(2)}, u32[]{:S(2)}) collective-permute-start(bf16[2,2,64,512]{3,2,1,0:T(8,128)(2,1)} %get-tuple-element.300.rest_2_), channel_id=1, source_target_pairs={{0,4},{2,6},{4,0},{6,2},{8,12},{10,14},{12,8},{14,10},{16,20},{18,... | collective-permute-start | bytes 786440 | tf_op jit(solution)/shard_map/ppermute | solution.py:120
  1008.1 45.2 %collective-permute-start.37 = (bf16[2,2,2,64,2048]{4,3,1,0,2:T(8,128)(2,1)}, bf16[2,2,2,64,2048]{4,3,1,0,2:T(8,128)(2,1)}, u32[]{:S(2)}, u32[]{:S(2)}) collective-permute-start(bf16[2,2,2,64,2048]{4,3,1,0,2:T(8,128)(2,1)} %copy.270), channel_id=1, source_target_pairs={{0,1},{1,0},{2,3},{3,2},{4,5},{5,4},{6,7},{7,6},{8,9},{9,8},{10,11... | collective-permute-start | bytes 6291464 | tf_op jit(solution)/shard_map/ppermute | solution.py:120
  1009.9 49.6 %collective-permute-start.38 = (bf16[2,2,2,64,2048]{4,3,2,1,0:T(8,128)(2,1)}, bf16[2,2,2,64,2048]{4,3,2,1,0:T(8,128)(2,1)}, u32[]{:S(2)}, u32[]{:S(2)}) collective-permute-start(bf16[2,2,2,64,2048]{4,3,2,1,0:T(8,128)(2,1)} %fusion.2.refs_8_), channel_id=1, source_target_pairs={{0,4},{2,6},{4,0},{6,2},{8,12},{10,14},{12,8},{14,10},{16,20},{18,... | collective-permute-start | bytes 6291464 | tf_op jit(solution)/shard_map/ppermute | solution.py:120
  1057.7 111.9 %collective-permute-start.60 = (bf16[2,2,64,2048]{3,2,1,0:T(8,128)(2,1)}, bf16[2,2,64,2048]{3,2,1,0:T(8,128)(2,1)S(1)}, u32[]{:S(2)}, u32[]{:S(2)}) collective-permute-start(bf16[2,2,64,2048]{3,2,1,0:T(8,128)(2,1)} %get-tuple-element.260.rest_0_), channel_id=1, source_target_pairs={{0,4},{2,6},{4,0},{6,2},{8,12},{10,14},{12,8},{14,10},{16,20},{18,... | collective-permute-start | bytes 3145736 | tf_op jit(solution)/shard_map/ppermute | solution.py:120
  1084.1 113.6 %collective-permute-start.40 = (bf16[2,512,768]{2,1,0:T(8,128)(2,1)}, bf16[2,512,768]{2,1,0:T(8,128)(2,1)}, u32[]{:S(2)}, u32[]{:S(2)}) collective-permute-start(bf16[2,512,768]{2,1,0:T(8,128)(2,1)} %get-tuple-element.188.refs_1_), channel_id=1, source_target_pairs={{0,2},{2,0},{4,6},{6,4},{8,10},{10,8},{12,14},{14,12},{16,18},{18,... | collective-permute-start | bytes 4718600 | tf_op jit(solution)/shard_map/ppermute | solution.py:120
  1084.1 118.0 %collective-permute-start.46 = (bf16[2,512,768]{2,1,0:T(8,128)(2,1)}, bf16[2,512,768]{2,1,0:T(8,128)(2,1)}, u32[]{:S(2)}, u32[]{:S(2)}) collective-permute-start(bf16[2,512,768]{2,1,0:T(8,128)(2,1)} %get-tuple-element.189.refs_2_), channel_id=1, source_target_pairs={{0,2},{2,0},{4,6},{6,4},{8,10},{10,8},{12,14},{14,12},{16,18},{18,... | collective-permute-start | bytes 4718600 | tf_op jit(solution)/shard_map/ppermute | solution.py:120
  (157 other events, 1797.2 us)
Sparse Core Ops, SparseCore 0:
  11.5 174.4 all-gather.5
  189.3 77.0 all-gather.7
  269.8 113.5 all-gather.9
  386.7 55.5 all-gather.13
  939.2 48.9 all-gather.11

commit v3 on v2

--- a/solution.py
+++ b/solution.py
@@ -1191,7 +1191,6 @@
         kept[layer] = (stream, seq_a, qkv, lse, att, branch_a, mid, seq_m, pre, acted, branch_m)
         stream = after
     cond_matrix = jnp.concatenate([step_out_own, table_own], axis=0).T
-    cond_matrix = lax.all_gather(hold(cond_matrix, seq_m), everywhere, axis=0, tiled=True)
     total = float(latents * length * CH)
     grad_stream, grad_final_mod, grad_patch_out, loss_rows = run_final(
         stream, mods[:, 6 * LAYERS :], noise_patches, patch_out_low, 2.0 / total
@@ -1260,6 +1259,8 @@
             layer, grad_stream, mlp_afters[layer]
         )
         after = grad_afters[layer]
+        if layer == LAYERS - 1:
+            cond_matrix = lax.all_gather(hold(cond_matrix, seq_grad_m), everywhere, axis=0, tiled=True)
         if layer == 0:
             mod_known = [jnp.zeros_like(mod_late[:, :2]), mod_late[:, 2:]] + mod_grads[1:]
             mod_known = jnp.concatenate(mod_known + [grad_final_mod], axis=1).reshape(own, -1)

time: 1320 us -> 1310 us (level)
  transfers between devices with their start and end apart: 70 -> 70, of which waited for: 24 -> 24; matrix products, arithmetic and copies ran while one was open for 13% -> 13% of each run, Pallas kernels for 65% -> 54%
where the time goes in v3:
time: 1310 us; the launch traced here: 1300 us
  Pallas kernels  849 us (65%)
  waiting for transfers between devices  132 us (10%)
  other arithmetic  118 us (9%)
  starting transfers between devices  88.5 us (7%)
  local copies, waits for them, and re-layouts  58.6 us (4%)
  matrix products  29.9 us (2%)
  between operations  23.4 us (2%)
    pallas_call x12, Pallas kernels, call_part(): pl.pallas_call(body, grid=(count,), in_specs=[spec(kind, dims_of(kind, ar...  519 us
    pallas_call x8, Pallas kernels, start_sums(): pl.pallas_call(body, grid_spec=pltpu.PrefetchScalarGridSpec(num_scalar_pr...  162 us
    ppermute x65, waiting for transfers between devices, swap(): lax.ppermute(value, name, [(i, i ^ bits) for i in range(lax.axis_size(nam...  115 us
    pallas_call x1, Pallas kernels, run_head(): pl.pallas_call(head_kernel, in_specs=[vmem] * 3 + [ANY] * 2, out_specs=[v...  113 us
    ppermute x65, starting transfers between devices, swap(): lax.ppermute(value, name, [(i, i ^ bits) for i in range(lax.axis_size(nam...  88.1 us
    pallas_call x4, Pallas kernels, push(): pl.pallas_call(functools.partial(push_kernel, plans, len(arrays)), in_spe...  55.3 us
    convert_element_type x20, other arithmetic, step(): part(axis, 0).astype(BF16)  42.4 us
    dot_general x10, matrix products, contract(): return jnp.einsum(form, left, right, preferred_element_type=jnp.float32)  26.4 us
  transfers between devices with their start and end apart: 70, of which 24 were waited for; matrix products, arithmetic and copies ran while one was open for 13% of the time, Pallas kernels for 54%

profile of v3, /device:TPU:0, one launch (start us, length us, event | category | flops | bytes accessed | tf_op | source)
XLA Modules:
  0.0 1299.6 jit_solution(11357717058069767908)
XLA Ops:
  19.2 112.6 %shard_map.473 = (f32[32,16,128]{2,1,0:T(8,128)}, bf16[32,64,128]{2,1,0:T(8,128)(2,1)}, bf16[8,272,128]{2,1,0:T(8,128)(2,1)}, bf16[4,64,7168]{2,1,0:T(8,128)(2,1)}, bf16[2,1024,2048]{2,1,0:T(8,128)(2,1)}) custom-call(f32[16,128]{1,0:T(8,128)} %pad_bitcast_fusion.packed, bf16[64,128]{1,0:T(8,128)(2,1)} %reshape.841.step_in, bf16[272,128]{1,0:T(8,128)(2,1)} %pad.33.cond, ...), custom_call_target="tpu_custom_call" | custom-call | flops 40000000000 | bytes 100000000 | tf_op jit(solution)/shard_map/pallas_call | solution.py:405
  165.8 10.7 collective-permute-done
  195.0 56.8 %shard_map.474 = (bf16[2048,1024]{1,0:T(8,128)(2,1)}, bf16[2048,3072]{1,0:T(8,128)(2,1)}, f32[8,16,256]{2,1,0:T(8,128)}, bf16[2048,1024]{1,0:T(8,128)(2,1)}, bf1...) custom-call(f32[2048,1024]{1,0:T(8,128)} %bitcast.490, ...), custom_call_target="tpu_custom_call" | custom-call | flops 42949672960 | bytes 50331648 | tf_op jit(solution)/shard_map/pallas_call | solution.py:804
  256.8 53.3 %shard_map.475 = (f32[2048,4096]{1,0:T(8,128)}, bf16[2048,4096]{1,0:T(8,128)(2,1)}, bf16[2048,1024]{1,0:T(8,128)(2,1)}, f32[2048,1024]{1,0:T(8,128)}) custom-call(bf16[2048,1024]{1,0:T(8,128)(2,1)} %get-tuple-element.126.refs_0_.left, f32[2048,1024]{1,0:T(8,128)} %get-tuple-element.127.refs_1_.refs_3_, ...), custom_call_target="tpu_custom_call" | custom-call | flops 51539607552 | bytes 50331648 | tf_op jit(solution)/shard_map/pallas_call | solution.py:804
  310.2 56.4 %shard_map.477 = (bf16[2048,1024]{1,0:T(8,128)(2,1)}, bf16[2048,3072]{1,0:T(8,128)(2,1)}, f32[8,16,256]{2,1,0:T(8,128)}, bf16[2048,1024]{1,0:T(8,128)(2,1)}, bf1...) custom-call(f32[2048,1024]{1,0:T(8,128)} %get-tuple-element.128.refs_0_.refs_3_, ...), custom_call_target="tpu_custom_call" | custom-call | flops 42949672960 | bytes 50331648 | tf_op jit(solution)/shard_map/pallas_call | solution.py:804
  366.6 16.7 %all-gather.10.cloned.1.call-done = bf16[2048,4096]{1,0:T(8,128)(2,1)} async-done(((bf16[64,4096]{1,0:T(8,128)(2,1)}), bf16[2048,4096]{1,0:T(8,128)(2,1)}) %all-gather.10.cloned.1.call-update) | async-done | bytes 16777232 | tf_op jit(solution)/shard_map/all_gather | solution.py:1119
  383.3 52.7 %shard_map.479 = (f32[2048,4096]{1,0:T(8,128)}, bf16[2048,4096]{1,0:T(8,128)(2,1)}, bf16[2048,1024]{1,0:T(8,128)(2,1)}, f32[2048,1024]{1,0:T(8,128)}) custom-call(bf16[2048,1024]{1,0:T(8,128)(2,1)} %get-tuple-element.129.refs_0_.left, f32[2048,1024]{1,0:T(8,128)} %get-tuple-element.130.refs_1_.refs_3_, ...), custom_call_target="tpu_custom_call" | custom-call | flops 51539607552 | bytes 50331648 | tf_op jit(solution)/shard_map/pallas_call | solution.py:804
  436.0 13.9 %shard_map.480 = (f32[2048,1024]{1,0:T(8,128)}, f32[8,2,1024]{2,1,0:T(2,128)}, f32[16,1024]{1,0:T(8,128)}, f32[1,16]{1,0:T(1,128)}) custom-call(f32[2048,1024]{1,0:T(8,128)} %get-tuple-element.132.refs_0_, f32[8,2,1024]{2,1,0:T(2,128)} %slice.1017.refs_1_, f32[8,256,16]{2,1,0:T(8,128)} %copy.252.refs_2_, bf16[16,1024]{1,0:T(8,128)(2,1)} %convert_element_type.1416.refs_3_), custom_call_target="tpu_custom_call" | custom-call | flops 1610612736 | bytes 16777216 | tf_op jit(solution)/shard_map/pallas_call | solution.py:804
  450.0 64.3 %shard_map.481 = (bf16[2048,1024]{1,0:T(8,128)(2,1)}, bf16[2048,4096]{1,0:T(8,128)(2,1)}, f32[2048,1024]{1,0:T(8,128)}, bf16[2048,1024]{1,0:T(8,128)(2,1)}, f32[...) custom-call(f32[2048,1024]{1,0:T(8,128)} %get-tuple-element.133.refs_0_, ...), custom_call_target="tpu_custom_call" | custom-call | flops 51539607552 | bytes 50331648 | tf_op jit(solution)/shard_map/pallas_call | solution.py:804
  514.3 25.0 %shard_map.482 = (bf16[2,512,2048]{2,1,0:T(8,128)(2,1)}, bf16[2,512,2048]{2,1,0:T(8,128)(2,1)}) custom-call(s32[2]{0:T(128)} %pad_add_fusion.place, bf16[2048,1024]{1,0:T(8,128)(2,1)} %get-tuple-element.141.left.refs_1_, bf16[2048,4096]{1,0:T(8,128)(2,1)} %get-tuple-element.142.right), custom_call_target="tpu_custom_call" | custom-call | flops 21474836480 | bytes 20971520 | tf_op jit(solution)/shard_map/pallas_call | solution.py:994
  539.4 24.8 %shard_map.484 = (bf16[2,512,2048]{2,1,0:T(8,128)(2,1)}, bf16[2,512,2048]{2,1,0:T(8,128)(2,1)}) custom-call(s32[2]{0:T(128)} %pad_add_fusion.place, bf16[2048,1024]{1,0:T(8,128)(2,1)} %get-tuple-element.129.refs_0_.left, bf16[2048,4096]{1,0:T(8,128)(2,1)} %get-tuple-element.148.right, bf16[2,512,2048]{2,1,0:T(8,128)(2,1)} %get-tuple-element.144.rest_0_), custom_call_target="tpu_custom_call" | custom-call | flops 21474836480 | bytes 20971520 | tf_op jit(solution)/shard_map/pallas_call | solution.py:994
  564.7 10.3 shard_map.486
  582.8 12.6 collective-permute-done.10
  621.4 36.3 %shard_map.483 = (bf16[2048,3072]{1,0:T(8,128)(2,1)}, f32[2048,1024]{1,0:T(8,128)}, f32[8,2,1024]{2,1,0:T(2,128)}) custom-call(bf16[2048,1024]{1,0:T(8,128)(2,1)} %get-tuple-element.137.refs_0_.left, bf16[2048,3072]{1,0:T(8,128)(2,1)} %get-tuple-element.138.refs_1_, f32[8,16,256]{2,1,0:T(8,128)} %get-tuple-element.139.refs_2_, ...), custom_call_target="tpu_custom_call" | custom-call | flops 25769803776 | bytes 25165824 | tf_op jit(solution)/shard_map/pallas_call | solution.py:804
  657.7 36.1 %shard_map.485 = (bf16[2048,3072]{1,0:T(8,128)(2,1)}, f32[2048,1024]{1,0:T(8,128)}, f32[8,2,1024]{2,1,0:T(2,128)}) custom-call(bf16[2048,1024]{1,0:T(8,128)(2,1)} %get-tuple-element.137.refs_0_.left, bf16[2048,3072]{1,0:T(8,128)(2,1)} %get-tuple-element.138.refs_1_, ...), custom_call_target="tpu_custom_call", output_to_operand_aliasing={{0}: (7, {}), {1}: (8, {}), {2}: (9, {})} | custom-call | flops 25769803776 | bytes 25165824 | tf_op jit(solution)/shard_map/pallas_call | solution.py:804
  703.7 20.9 %shard_map.488 = (bf16[2,512,768]{2,1,0:T(8,128)(2,1)}, bf16[2,512,768]{2,1,0:T(8,128)(2,1)}, bf16[2,512,768]{2,1,0:T(8,128)(2,1)}, bf16[2,512,768]{2,1,0:T(8,128)(2,1)}) custom-call(s32[2]{0:T(128)} %pad_add_fusion.place, bf16[2048,1024]{1,0:T(8,128)(2,1)} %get-tuple-element.163.left, bf16[2048,3072]{1,0:T(8,128)(2,1)} %get-tuple-element.164.right, ...), custom_call_target="tpu_custom_call" | custom-call | flops 16106127360 | bytes 16777216 | tf_op jit(solution)/shard_map/pallas_call | solution.py:994
  729.6 38.3 %shard_map.487 = (bf16[2048,1024]{1,0:T(8,128)(2,1)}, bf16[2048,4096]{1,0:T(8,128)(2,1)}, f32[2048,1024]{1,0:T(8,128)}, bf16[2048,1024]{1,0:T(8,128)(2,1)}, f32[...) custom-call(f32[2048,1024]{1,0:T(8,128)} %get-tuple-element.151.refs_0_, ...), custom_call_target="tpu_custom_call" | custom-call | flops 25769803776 | bytes 25165824 | tf_op jit(solution)/shard_map/pallas_call | solution.py:804
  791.3 38.4 %shard_map.490 = (bf16[2048,1024]{1,0:T(8,128)(2,1)}, bf16[2048,4096]{1,0:T(8,128)(2,1)}, f32[2048,1024]{1,0:T(8,128)}, bf16[2048,1024]{1,0:T(8,128)(2,1)}, f32[...) custom-call(f32[2048,1024]{1,0:T(8,128)} %get-tuple-element.151.refs, ...), custom_call_target="tpu_custom_call", output_to_operand_aliasing={{0}: (10, {}), {1}: (11, {}), {2}: (12, {}), {3}: (13, {}),... | custom-call | flops 25769803776 | bytes 25165824 | tf_op jit(solution)/shard_map/pallas_call | solution.py:804
  833.1 24.9 %shard_map.491 = (bf16[2,512,2048]{2,1,0:T(8,128)(2,1)}, bf16[2,512,2048]{2,1,0:T(8,128)(2,1)}) custom-call(s32[2]{0:T(128)} %pad_add_fusion.place, bf16[2048,1024]{1,0:T(8,128)(2,1)} %get-tuple-element.173.left, bf16[2048,4096]{1,0:T(8,128)(2,1)} %get-tuple-element.174.right), custom_call_target="tpu_custom_call" | custom-call | flops 21474836480 | bytes 20971520 | tf_op jit(solution)/shard_map/pallas_call | solution.py:994
  865.7 25.0 %shard_map.492 = (bf16[2,512,2048]{2,1,0:T(8,128)(2,1)}, bf16[2,512,2048]{2,1,0:T(8,128)(2,1)}) custom-call(s32[2]{0:T(128)} %pad_add_fusion.place, bf16[2048,1024]{1,0:T(8,128)(2,1)} %get-tuple-element.126.refs_0_.left, bf16[2048,4096]{1,0:T(8,128)(2,1)} %get-tuple-element.177.right, bf16[2,2,64,768]{3,2,1,0:T(8,128)(2,1)} %get-tuple-element.298.rest_0_, ...), custom_call_target="tpu_custom_call" | custom-call | flops 21474836480 | bytes 20971520 | tf_op jit(solution)/shard_map/pallas_call | solution.py:994
  909.4 10.4 shard_map.496
  931.3 8.8 collective-permute-done.39
  956.6 36.2 %shard_map.493 = (bf16[2048,3072]{1,0:T(8,128)(2,1)}, f32[2048,1024]{1,0:T(8,128)}, f32[8,2,1024]{2,1,0:T(2,128)}) custom-call(bf16[2048,1024]{1,0:T(8,128)(2,1)} %get-tuple-element.169.refs_0_.left, bf16[2048,3072]{1,0:T(8,128)(2,1)} %get-tuple-element.170.refs_1_, f32[8,16,256]{2,1,0:T(8,128)} %get-tuple-element.171.refs_2_, f32[2048,1024]{1,0:T(8,128)} %bitcast.491, ...), custom_call_target="tpu_custom_call" | custom-call | flops 25769803776 | bytes 25165824 | tf_op jit(solution)/shard_map/pallas_call | solution.py:804
  1005.8 36.3 %shard_map.499 = (bf16[2048,3072]{1,0:T(8,128)(2,1)}, f32[2048,1024]{1,0:T(8,128)}, f32[8,2,1024]{2,1,0:T(2,128)}) custom-call(bf16[2048,1024]{1,0:T(8,128)(2,1)} %get-tuple-element.169.refs_0_.left, bf16[2048,3072]{1,0:T(8,128)(2,1)} %get-tuple-element.170.refs_1_, ...), custom_call_target="tpu_custom_call", output_to_operand_aliasing={{0}: (7, {}), {1}: (8, {}), {2}: (9, {})} | custom-call | flops 25769803776 | bytes 25165824 | tf_op jit(solution)/shard_map/pallas_call | solution.py:804
  1052.6 20.8 %shard_map.500 = (bf16[2,512,768]{2,1,0:T(8,128)(2,1)}, bf16[2,512,768]{2,1,0:T(8,128)(2,1)}, bf16[2,512,768]{2,1,0:T(8,128)(2,1)}, bf16[2,512,768]{2,1,0:T(8,128)(2,1)}) custom-call(s32[2]{0:T(128)} %pad_add_fusion.place, bf16[2048,1024]{1,0:T(8,128)(2,1)} %get-tuple-element.125.left, bf16[2048,3072]{1,0:T(8,128)(2,1)} %get-tuple-element.185.right, ...), custom_call_target="tpu_custom_call" | custom-call | flops 16106127360 | bytes 16777216 | tf_op jit(solution)/shard_map/pallas_call | solution.py:994
  1075.5 17.5 %shard_map.502.refs_1_ = bf16[32,128,128]{2,1,0:T(8,128)(2,1)} custom-call(bf16[128,128]{1,0:T(8,128)(2,1)} %convert_element_type.1621.refs_0_), custom_call_target="tpu_custom_call" | custom-call | flops 5000000000 | bytes 50000000 | tf_op jit(solution)/shard_map/pallas_call | solution.py:258
  1099.0 11.6 shard_map.509
  1129.0 15.7 %shard_map.511 = (f32[32,16,128]{2,1,0:T(8,128)}, f32[32,16,128]{2,1,0:T(8,128)}) custom-call(f32[32,16,128]{2,1,0:T(8,128)} %bitcast.567, f32[32,16,128]{2,1,0:T(8,128)} %pad.38.refs_1_), custom_call_target="tpu_custom_call" | custom-call | flops 5000000000 | bytes 50000000 | tf_op jit(solution)/shard_map/pallas_call | solution.py:258
  1177.6 7.2 collective-permute-done.62
  1194.0 8.6 collective-permute-done.56
  1210.2 9.3 collective-permute-done.47
  1259.7 10.5 shard_map.512
  (643 shorter events, 353.1 us)
Async XLA Ops:
  7.2 249.6 %all-gather.6.cloned.1.call-start = ((), (), s32[]{:S(2)}) async-start(), calls=%async_computation | async-start | bytes 17301504 | tf_op jit(solution)/shard_map/all_gather | solution.py:1119
  11.1 299.1 %all-gather.8.cloned.1.call-start = ((), (), s32[]{:S(2)}) async-start(), calls=%async_computation.1 | async-start | bytes 8650752 | tf_op jit(solution)/shard_map/all_gather | solution.py:1119
  131.9 251.5 %all-gather.10.cloned.1.call-start = ((), (), s32[]{:S(2)}) async-start(), calls=%async_computation.2 | async-start | bytes 17301504 | tf_op jit(solution)/shard_map/all_gather | solution.py:1119
  251.8 352.3 %all-gather.14.cloned.1.call-start = ((), (), s32[]{:S(2)}) async-start(), calls=%async_computation.4 | async-start | bytes 2433024 | tf_op jit(solution)/shard_map/all_gather | solution.py:1263
  514.3 580.3 %all-gather.12.cloned.1.call-start = ((), (), s32[]{:S(2)}) async-start(), calls=%async_computation.3 | async-start | bytes 3899392 | tf_op jit(solution)/shard_map/all_gather | solution.py:1270
  564.2 41.8 %collective-permute-start.5 = (bf16[2,512,2048]{2,1,0:T(8,128)(2,1)}, bf16[2,512,2048]{2,1,0:T(8,128)(2,1)}, u32[]{:S(2)}, u32[]{:S(2)}) collective-permute-start(bf16[2,512,2048]{2,1,0:T(8,128)(2,1)} %get-tuple-element.150.rest_0_), channel_id=1, source_target_pairs={{0,2},{2,0},{4,6},{6,4},{8,10},{10,8},{12,14},{14,12},{16,18},{18,... | collective-permute-start | bytes 12582920 | tf_op jit(solution)/shard_map/ppermute | solution.py:120
  564.5 49.8 %collective-permute-start.4 = (bf16[2,512,2048]{2,1,0:T(8,128)(2,1)}, bf16[2,512,2048]{2,1,0:T(8,128)(2,1)}, u32[]{:S(2)}, u32[]{:S(2)}) collective-permute-start(bf16[2,512,2048]{2,1,0:T(8,128)(2,1)} %get-tuple-element.144.rest_0_), channel_id=1, source_target_pairs={{0,2},{2,0},{4,6},{6,4},{8,10},{10,8},{12,14},{14,12},{16,18},{18,... | collective-permute-start | bytes 12582920 | tf_op jit(solution)/shard_map/ppermute | solution.py:120
  610.5 88.8 %collective-permute-start.8 = (bf16[2,2,2,64,2048]{4,3,2,1,0:T(8,128)(2,1)}, bf16[2,2,2,64,2048]{4,3,2,1,0:T(8,128)(2,1)}, u32[]{:S(2)}, u32[]{:S(2)}) collective-permute-start(bf16[2,2,2,64,2048]{4,3,2,1,0:T(8,128)(2,1)} %fusion.1.refs_10_), channel_id=1, source_target_pairs={{0,4},{2,6},{4,0},{6,2},{8,12},{10,14},{12,8},{14,10},{16,20},{18,... | collective-permute-start | bytes 6291464 | tf_op jit(solution)/shard_map/ppermute | solution.py:120
  620.3 73.5 %collective-permute-start.6 = (bf16[2,2,2,64,2048]{4,3,1,0,2:T(8,128)(2,1)}, bf16[2,2,2,64,2048]{4,3,1,0,2:T(8,128)(2,1)}, u32[]{:S(2)}, u32[]{:S(2)}) collective-permute-start(bf16[2,2,2,64,2048]{4,3,1,0,2:T(8,128)(2,1)} %copy.256), channel_id=1, source_target_pairs={{0,1},{1,0},{2,3},{3,2},{4,5},{5,4},{6,7},{7,6},{8,9},{9,8},{10,11... | collective-permute-start | bytes 6291464 | tf_op jit(solution)/shard_map/ppermute | solution.py:120
  702.8 65.2 %collective-permute-start.13 = (bf16[2,2,64,2048]{3,2,1,0:T(8,128)(2,1)}, bf16[2,2,64,2048]{3,2,1,0:T(8,128)(2,1)S(1)}, u32[]{:S(2)}, u32[]{:S(2)}) collective-permute-start(bf16[2,2,64,2048]{3,2,1,0:T(8,128)(2,1)} %get-tuple-element.264.refs_13_), channel_id=1, source_target_pairs={{0,1},{1,0},{2,3},{3,2},{4,5},{5,4},{6,7},{7,6},{8,9},{9,8},{10,11... | collective-permute-start | bytes 3145736 | tf_op jit(solution)/shard_map/ppermute | solution.py:120
  724.7 61.4 %collective-permute-start.12 = (bf16[2,512,768]{2,1,0:T(8,128)(2,1)}, bf16[2,512,768]{2,1,0:T(8,128)(2,1)}, u32[]{:S(2)}, u32[]{:S(2)}) collective-permute-start(bf16[2,512,768]{2,1,0:T(8,128)(2,1)} %get-tuple-element.168), channel_id=1, source_target_pairs={{0,2},{2,0},{4,6},{6,4},{8,10},{10,8},{12,14},{14,12},{16,18},{18,... | collective-permute-start | bytes 4718600 | tf_op jit(solution)/shard_map/ppermute | solution.py:120
  724.7 64.3 %collective-permute-start.11 = (bf16[2,512,768]{2,1,0:T(8,128)(2,1)}, bf16[2,512,768]{2,1,0:T(8,128)(2,1)}, u32[]{:S(2)}, u32[]{:S(2)}) collective-permute-start(bf16[2,512,768]{2,1,0:T(8,128)(2,1)} %get-tuple-element.166), channel_id=1, source_target_pairs={{0,2},{2,0},{4,6},{6,4},{8,10},{10,8},{12,14},{14,12},{16,18},{18,... | collective-permute-start | bytes 4718600 | tf_op jit(solution)/shard_map/ppermute | solution.py:120
  727.7 44.0 %collective-permute-start.15 = (bf16[64,2048]{1,0:T(8,128)(2,1)}, bf16[64,2048]{1,0:T(8,128)(2,1)S(1)}, u32[]{:S(2)}, u32[]{:S(2)}) collective-permute-start(bf16[64,2048]{1,0:T(8,128)(2,1)} %get-tuple-element.284.refs_10_), channel_id=1, source_target_pairs={{0,8},{2,10},{4,12},{6,14},{8,0},{10,2},{12,4},{14,6},{16,24},{18,... | collective-permute-start | bytes 786440 | tf_op jit(solution)/shard_map/ppermute | solution.py:120
  728.1 43.6 %collective-permute-start.16 = (bf16[64,2048]{1,0:T(8,128)(2,1)}, bf16[64,2048]{1,0:T(8,128)(2,1)S(1)}, u32[]{:S(2)}, u32[]{:S(2)}) collective-permute-start(bf16[64,2048]{1,0:T(8,128)(2,1)} %get-tuple-element.283.refs_11_), channel_id=1, source_target_pairs={{0,16},{2,18},{4,20},{6,22},{8,24},{10,26},{12,28},{14,30},{16,0},... | collective-permute-start | bytes 786440 | tf_op jit(solution)/shard_map/ppermute | solution.py:120
  771.6 124.7 %collective-permute-start.27 = (bf16[64,512]{1,0:T(8,128)(2,1)S(1)}, bf16[64,512]{1,0:T(8,128)(2,1)S(1)}, u32[]{:S(2)}, u32[]{:S(2)}) collective-permute-start(bf16[64,512]{1,0:T(8,128)(2,1)S(1)} %get-tuple-element.326.refs_20_), channel_id=1, source_target_pairs={{0,8},{2,10},{4,12},{6,14},{8,0},{10,2},{12,4},{14,6},{16,24},{18,... | collective-permute-start | bytes 196616 | tf_op jit(solution)/shard_map/ppermute | solution.py:120
  771.7 126.6 %collective-permute-start.28 = (bf16[64,512]{1,0:T(8,128)(2,1)S(1)}, bf16[64,512]{1,0:T(8,128)(2,1)S(1)}, u32[]{:S(2)}, u32[]{:S(2)}) collective-permute-start(bf16[64,512]{1,0:T(8,128)(2,1)S(1)} %get-tuple-element.325.refs_21_), channel_id=1, source_target_pairs={{0,16},{2,18},{4,20},{6,22},{8,24},{10,26},{12,28},{14,30},{16,0},... | collective-permute-start | bytes 196616 | tf_op jit(solution)/shard_map/ppermute | solution.py:120
  779.2 111.6 %collective-permute-start.24 = (bf16[64,2048]{1,0:T(8,128)(2,1)S(1)}, bf16[64,2048]{1,0:T(8,128)(2,1)}, u32[]{:S(2)}, u32[]{:S(2)}) collective-permute-start(bf16[64,2048]{1,0:T(8,128)(2,1)S(1)} %get-tuple-element.280.refs_17_), channel_id=1, source_target_pairs={{0,8},{2,10},{4,12},{6,14},{8,0},{10,2},{12,4},{14,6},{16,24},{18,... | collective-permute-start | bytes 786440 | tf_op jit(solution)/shard_map/ppermute | solution.py:120
  790.3 71.0 %collective-permute-start.19 = (bf16[2,2,2,64,768]{4,3,2,1,0:T(8,128)(2,1)S(1)}, bf16[2,2,2,64,768]{4,3,2,1,0:T(8,128)(2,1)}, u32[]{:S(2)}, u32[]{:S(2)}) collective-permute-start(bf16[2,2,2,64,768]{4,3,2,1,0:T(8,128)(2,1)S(1)} %fusion.31.refs_15_), channel_id=1, source_target_pairs={{0,4},{2,6},{4,0},{6,2},{8,12},{10,14},{12,8},{14,10},{16,20},{18,... | collective-permute-start | bytes 2359304 | tf_op jit(solution)/shard_map/ppermute | solution.py:120
  860.3 32.7 %collective-permute-start.25 = (bf16[64,2048]{1,0:T(8,128)(2,1)S(1)}, bf16[64,2048]{1,0:T(8,128)(2,1)}, u32[]{:S(2)}, u32[]{:S(2)}) collective-permute-start(bf16[64,2048]{1,0:T(8,128)(2,1)S(1)} %copy-done.35), channel_id=1, source_target_pairs={{0,16},{2,18},{4,20},{6,22},{8,24},{10,26},{12,28},{14,30},{16,0},... | collective-permute-start | bytes 786440 | tf_op jit(solution)/shard_map/ppermute | solution.py:120
  893.1 50.3 %collective-permute-start.18 = (bf16[2,512,2048]{2,1,0:T(8,128)(2,1)}, bf16[2,512,2048]{2,1,0:T(8,128)(2,1)}, u32[]{:S(2)}, u32[]{:S(2)}) collective-permute-start(bf16[2,512,2048]{2,1,0:T(8,128)(2,1)} %get-tuple-element.176.rest_2_), channel_id=1, source_target_pairs={{0,2},{2,0},{4,6},{6,4},{8,10},{10,8},{12,14},{14,12},{16,18},{18,... | collective-permute-start | bytes 12582920 | tf_op jit(solution)/shard_map/ppermute | solution.py:120
  898.3 52.6 %collective-permute-start.21 = (bf16[2,512,2048]{2,1,0:T(8,128)(2,1)}, bf16[2,512,2048]{2,1,0:T(8,128)(2,1)}, u32[]{:S(2)}, u32[]{:S(2)}) collective-permute-start(bf16[2,512,2048]{2,1,0:T(8,128)(2,1)} %get-tuple-element.179.refs_1_.rest_6_), channel_id=1, source_target_pairs={{0,2},{2,0},{4,6},{6,4},{8,10},{10,8},{12,14},{14,12},{16,18},{18,... | collective-permute-start | bytes 12582920 | tf_op jit(solution)/shard_map/ppermute | solution.py:120
  928.4 64.5 %collective-permute-start.34 = (bf16[64,768]{1,0:T(8,128)(2,1)}, bf16[64,768]{1,0:T(8,128)(2,1)S(1)}, u32[]{:S(2)}, u32[]{:S(2)}) collective-permute-start(bf16[64,768]{1,0:T(8,128)(2,1)} %get-tuple-element.315.rest_3_), channel_id=1, source_target_pairs={{0,8},{2,10},{4,12},{6,14},{8,0},{10,2},{12,4},{14,6},{16,24},{18,... | collective-permute-start | bytes 294920 | tf_op jit(solution)/shard_map/ppermute | solution.py:120
  928.5 68.0 %collective-permute-start.35 = (bf16[64,768]{1,0:T(8,128)(2,1)}, bf16[64,768]{1,0:T(8,128)(2,1)S(1)}, u32[]{:S(2)}, u32[]{:S(2)}) collective-permute-start(bf16[64,768]{1,0:T(8,128)(2,1)} %get-tuple-element.314.rest_4_), channel_id=1, source_target_pairs={{0,16},{2,18},{4,20},{6,22},{8,24},{10,26},{12,28},{14,30},{16,0},... | collective-permute-start | bytes 294920 | tf_op jit(solution)/shard_map/ppermute | solution.py:120
  940.1 57.3 %collective-permute-start.36 = (bf16[64,768]{1,0:T(8,128)(2,1)}, bf16[64,768]{1,0:T(8,128)(2,1)S(1)}, u32[]{:S(2)}, u32[]{:S(2)}) collective-permute-start(bf16[64,768]{1,0:T(8,128)(2,1)} %get-tuple-element.313.rest_5_), channel_id=1, source_target_pairs={{0,24},{2,26},{4,28},{6,30},{8,16},{10,18},{12,20},{14,22},{16,8},... | collective-permute-start | bytes 294920 | tf_op jit(solution)/shard_map/ppermute | solution.py:120
  943.4 55.8 %collective-permute-start.31 = (bf16[64,768]{1,0:T(8,128)(2,1)S(1)}, bf16[64,768]{1,0:T(8,128)(2,1)S(1)}, u32[]{:S(2)}, u32[]{:S(2)}) collective-permute-start(bf16[64,768]{1,0:T(8,128)(2,1)S(1)} %copy-done.81), channel_id=1, source_target_pairs={{0,8},{2,10},{4,12},{6,14},{8,0},{10,2},{12,4},{14,6},{16,24},{18,... | collective-permute-start | bytes 294920 | tf_op jit(solution)/shard_map/ppermute | solution.py:120
  950.9 49.6 %collective-permute-start.32 = (bf16[64,768]{1,0:T(8,128)(2,1)S(1)}, bf16[64,768]{1,0:T(8,128)(2,1)S(1)}, u32[]{:S(2)}, u32[]{:S(2)}) collective-permute-start(bf16[64,768]{1,0:T(8,128)(2,1)S(1)} %copy-done.80), channel_id=1, source_target_pairs={{0,16},{2,18},{4,20},{6,22},{8,24},{10,26},{12,28},{14,30},{16,0},... | collective-permute-start | bytes 294920 | tf_op jit(solution)/shard_map/ppermute | solution.py:120
  996.5 150.6 %collective-permute-start.52 = (bf16[2,2,64,512]{3,2,1,0:T(8,128)(2,1)}, bf16[2,2,64,512]{3,2,1,0:T(8,128)(2,1)}, u32[]{:S(2)}, u32[]{:S(2)}) collective-permute-start(bf16[2,2,64,512]{3,2,1,0:T(8,128)(2,1)} %get-tuple-element.300.rest_2_), channel_id=1, source_target_pairs={{0,4},{2,6},{4,0},{6,2},{8,12},{10,14},{12,8},{14,10},{16,20},{18,... | collective-permute-start | bytes 786440 | tf_op jit(solution)/shard_map/ppermute | solution.py:120
  997.4 45.2 %collective-permute-start.37 = (bf16[2,2,2,64,2048]{4,3,1,0,2:T(8,128)(2,1)}, bf16[2,2,2,64,2048]{4,3,1,0,2:T(8,128)(2,1)}, u32[]{:S(2)}, u32[]{:S(2)}) collective-permute-start(bf16[2,2,2,64,2048]{4,3,1,0,2:T(8,128)(2,1)} %copy.270), channel_id=1, source_target_pairs={{0,1},{1,0},{2,3},{3,2},{4,5},{5,4},{6,7},{7,6},{8,9},{9,8},{10,11... | collective-permute-start | bytes 6291464 | tf_op jit(solution)/shard_map/ppermute | solution.py:120
  999.3 49.6 %collective-permute-start.38 = (bf16[2,2,2,64,2048]{4,3,2,1,0:T(8,128)(2,1)}, bf16[2,2,2,64,2048]{4,3,2,1,0:T(8,128)(2,1)}, u32[]{:S(2)}, u32[]{:S(2)}) collective-permute-start(bf16[2,2,2,64,2048]{4,3,2,1,0:T(8,128)(2,1)} %fusion.2.refs_8_), channel_id=1, source_target_pairs={{0,4},{2,6},{4,0},{6,2},{8,12},{10,14},{12,8},{14,10},{16,20},{18,... | collective-permute-start | bytes 6291464 | tf_op jit(solution)/shard_map/ppermute | solution.py:120
  1047.1 111.9 %collective-permute-start.60 = (bf16[2,2,64,2048]{3,2,1,0:T(8,128)(2,1)}, bf16[2,2,64,2048]{3,2,1,0:T(8,128)(2,1)S(1)}, u32[]{:S(2)}, u32[]{:S(2)}) collective-permute-start(bf16[2,2,64,2048]{3,2,1,0:T(8,128)(2,1)} %get-tuple-element.260.rest_0_), channel_id=1, source_target_pairs={{0,4},{2,6},{4,0},{6,2},{8,12},{10,14},{12,8},{14,10},{16,20},{18,... | collective-permute-start | bytes 3145736 | tf_op jit(solution)/shard_map/ppermute | solution.py:120
  1073.4 113.6 %collective-permute-start.40 = (bf16[2,512,768]{2,1,0:T(8,128)(2,1)}, bf16[2,512,768]{2,1,0:T(8,128)(2,1)}, u32[]{:S(2)}, u32[]{:S(2)}) collective-permute-start(bf16[2,512,768]{2,1,0:T(8,128)(2,1)} %get-tuple-element.188.refs_1_), channel_id=1, source_target_pairs={{0,2},{2,0},{4,6},{6,4},{8,10},{10,8},{12,14},{14,12},{16,18},{18,... | collective-permute-start | bytes 4718600 | tf_op jit(solution)/shard_map/ppermute | solution.py:120
  1073.4 118.0 %collective-permute-start.46 = (bf16[2,512,768]{2,1,0:T(8,128)(2,1)}, bf16[2,512,768]{2,1,0:T(8,128)(2,1)}, u32[]{:S(2)}, u32[]{:S(2)}) collective-permute-start(bf16[2,512,768]{2,1,0:T(8,128)(2,1)} %get-tuple-element.189.refs_2_), channel_id=1, source_target_pairs={{0,2},{2,0},{4,6},{6,4},{8,10},{10,8},{12,14},{14,12},{16,18},{18,... | collective-permute-start | bytes 4718600 | tf_op jit(solution)/shard_map/ppermute | solution.py:120
  (157 other events, 1798.5 us)
Sparse Core Ops, SparseCore 0:
  11.5 174.4 all-gather.5
  189.3 77.0 all-gather.7
  269.8 113.4 all-gather.9
  514.4 58.5 all-gather.13
  928.5 48.9 all-gather.11
